TPU v7x, 512 devices: a whole 4x8x8 slice. The times are simulated.
512 devices in a mesh: segment: 4 (over x), expert: 128 (over z, y, core).
Axes of the slice: x: 4, y: 8, z: 8, core: 2. Of those that a mesh axis runs over, the one named last changes fastest.
Arguments:
- activations: bfloat16 [4, 2, 1024, 2048], P('segment', None, 'expert'), may hold values from -6 to 6
- norm_gain: float32 [4, 2048], P('segment'), may hold values from 0.5 to 1.5
- gate_weight: bfloat16 [4, 128, 2048, 384], P('segment', 'expert'), may hold values from -0.125 to 0.125
- up_weight: bfloat16 [4, 128, 2048, 384], P('segment', 'expert'), may hold values from -0.125 to 0.125
- down_weight: bfloat16 [4, 128, 384, 2048], P('segment', 'expert'), may hold values from -0.21875 to 0.21875
- expert_ids: int32 [4, 2, 1024, 8], P('segment', None, 'expert'), may hold values from 0 to 63, as said below
- route_weights: float32 [4, 2, 1024, 8], P('segment', None, 'expert'), may hold values from 0.1 to 0.4
Outputs:
- passed: bfloat16 [4, 2, 1024, 2048], P('segment', None, 'expert')
Inputs may be any that keep to these rules, and one draw needn't show every extreme that they name: `expert_ids`: each token names 8 different experts. In the aligned blocks of 8 tokens of one layer and micro-batch (the tokens of one index of expert), no expert is named by more than 2 tokens; in each layer and micro-batch one expert is named by exactly 2 tokens in every block.
All inputs are finite; a program needn't handle non-finite values.
Results may differ from a plain program's by a relative error of at most 0.0054.
Values may be sent and summed in bfloat16 or wider, within the bound.
No kernel may reach another device: no remote copies, remote signals or barrier semaphores. Data moves between devices by JAX's collectives and lax.ppermute only.
A program may use at most 64 MiB of HBM per device.

v0:
```python
import jax
import jax.numpy as jnp
from jax import lax
from jax.sharding import PartitionSpec as P

norm_eps = 1e-06


def shifted(block, axis, distance):
    devices = range(lax.axis_size(axis))
    route = [((i - distance) % len(devices), i) for i in devices]
    return lax.ppermute(block, axis, route)


def rms_scaled(tokens, gain_row):
    float_rows = tokens.astype(jnp.float32)
    inv_scale = lax.rsqrt(jnp.mean(float_rows * float_rows, axis=-1, keepdims=True) + norm_eps)
    return (float_rows * inv_scale * gain_row).astype(jnp.bfloat16)


def routing_tables(flat_choice, weight_rows, experts, capacity):
    token_count, choice_count = flat_choice.shape
    flat_ids = flat_choice.reshape(-1)
    expert_hits = (flat_ids[:, None] == jnp.arange(experts, dtype=jnp.int32)[None, :]).astype(
        jnp.int32
    )
    earlier = jnp.cumsum(expert_hits, axis=0) - expert_hits
    slot_index = jnp.sum(earlier * expert_hits, axis=1)
    position = flat_ids * capacity + slot_index
    slot_hits = (
        position[:, None] == jnp.arange(experts * capacity, dtype=jnp.int32)[None, :]
    ).astype(jnp.float32)
    routed_rows = jnp.arange(token_count * choice_count, dtype=jnp.int32)
    owner_map = (
        routed_rows[:, None] // choice_count == jnp.arange(token_count, dtype=jnp.int32)[None, :]
    ).astype(jnp.float32)
    pick_rows = jnp.dot(slot_hits.T, owner_map, precision=lax.Precision.HIGHEST)
    blend_rows = jnp.dot(
        owner_map.T, slot_hits * weight_rows.reshape(-1)[:, None], precision=lax.Precision.HIGHEST
    )
    return (pick_rows.astype(jnp.bfloat16), blend_rows)


def on_device(
    activations, norm_gain, gate_weight, up_weight, down_weight, expert_ids, route_weights
):
    devices = lax.axis_size("expert")
    local_halves = gate_weight.shape[1]
    experts = local_halves * devices // 2
    micro_count = activations.shape[1]
    token_count = activations.shape[2]
    model_width = activations.shape[3]
    choice_count = expert_ids.shape[3]
    capacity = 2 * token_count * choice_count // experts
    gain_row = norm_gain[0]
    gate_local = gate_weight[0]
    up_local = up_weight[0]
    down_local = down_weight[0]
    outputs_list = []
    for batch_index in range(micro_count):
        tokens = activations[0, batch_index]
        normed = rms_scaled(tokens, gain_row)
        pick_rows, blend_rows = routing_tables(
            expert_ids[0, batch_index], route_weights[0, batch_index], experts, capacity
        )
        buffer = jnp.dot(pick_rows, normed, preferred_element_type=jnp.float32).astype(jnp.bfloat16)
        outgoing = jnp.concatenate([buffer, buffer], axis=0).reshape(
            devices, local_halves, capacity, model_width
        )
        arrived = lax.all_to_all(outgoing, "expert", split_axis=0, concat_axis=0, tiled=True)
        gate_value = jnp.einsum(
            "nqcd,qdf->nqcf", arrived, gate_local, preferred_element_type=jnp.float32
        )
        up_value = jnp.einsum(
            "nqcd,qdf->nqcf", arrived, up_local, preferred_element_type=jnp.float32
        )
        hidden = (jax.nn.silu(gate_value) * up_value).astype(jnp.bfloat16)
        returned = lax.all_to_all(
            jnp.einsum(
                "nqcf,qfd->nqcd", hidden, down_local, preferred_element_type=jnp.float32
            ).astype(jnp.bfloat16),
            "expert",
            split_axis=0,
            concat_axis=0,
            tiled=True,
        )
        pieces = returned.reshape(2, experts * capacity, model_width)
        expert_out = (pieces[0].astype(jnp.float32) + pieces[1].astype(jnp.float32)).astype(
            jnp.bfloat16
        )
        mixed_sum = jnp.dot(
            blend_rows, expert_out.astype(jnp.float32), precision=lax.Precision.HIGHEST
        )
        outputs_list.append((tokens.astype(jnp.float32) + mixed_sum).astype(jnp.bfloat16))
    stacked = jnp.stack(outputs_list)[None]
    return shifted(stacked, "segment", 1)


def solution(mesh):
    return jax.shard_map(
        on_device,
        mesh=mesh,
        in_specs=(
            P("segment", None, "expert", None),
            P("segment", None),
            P("segment", "expert", None, None),
            P("segment", "expert", None, None),
            P("segment", "expert", None, None),
            P("segment", None, "expert", None),
            P("segment", None, "expert", None),
        ),
        out_specs=P("segment", None, "expert", None),
        check_vma=False,
    )
```

profile of v0, /device:TPU:8, one launch (start us, length us, event | category | flops | bytes accessed | tf_op | source)
XLA Modules:
  0.0 178.2 jit_solution(18423162196481122960)
XLA Ops:
  0.0 0.0 copy-start
  0.0 0.8 fusion.112
  0.8 0.1 reshape_squeeze.7
  0.9 0.1 fusion.87
  1.0 0.1 reduce_window_sum.18
  1.1 0.2 select_reduce_fusion
  1.3 0.9 fusion.74
  2.2 0.3 convolution_convert_fusion.4
  2.5 1.1 convolution_convert_fusion.2
  3.6 0.1 pad_maximum_fusion.1
  3.7 1.5 reshape.147
  5.2 0.0 copy-start.2
  5.2 0.0 copy-start.3
  5.2 18.0 %all-to-all-start.2 = ((bf16[128,1,2,2048]{3,2,1,0:T(2,128)(2,1)}), bf16[128,1,2,2048]{3,2,1,0:T(2,128)(2,1)}, u32[]{:S(2)}, u32[]{:S(2)}) async-start(bf16[128,1,2,2048]{3,2,1,0:T(2,128)(2,1)} %bitcast.26), calls=%async_computation.2 | async-start | bytes 2097152 | tf_op jit(solution)/shard_map/all_to_all | solution.py:70
  23.2 0.1 reshape_squeeze.6
  23.3 0.1 fusion.93
  23.4 0.1 reduce_window_sum.17
  23.5 0.2 select_reduce_fusion.1
  23.7 0.3 convolution_convert_fusion.5
  23.9 0.0 copy-done.2
  23.9 0.0 copy-done.3
  23.9 0.3 convolution_convert_fusion.3
  24.3 0.1 pad_maximum_fusion
  24.4 1.5 reshape.141
  25.9 28.4 %all-to-all-done.2 = bf16[128,1,2,2048]{3,2,1,0:T(2,128)(2,1)} async-done(((bf16[128,1,2,2048]{3,2,1,0:T(2,128)(2,1)}), bf16[128,1,2,2048]{3,2,1,0:T(2,128)(2,1)}, u32[]{:S(2)}, u32[]{:S(2)}) %all-to-all-start.2) | async-done | bytes 1048608 | tf_op jit(solution)/shard_map/all_to_all | solution.py:70
  54.3 5.9 %all-to-all-start = ((bf16[128,1,2,2048]{3,2,1,0:T(2,128)(2,1)}), bf16[128,1,2,2048]{3,2,1,0:T(2,128)(2,1)S(1)}, u32[]{:S(2)}, u32[]{:S(2)}) async-start(bf16[128,1,2,2048]{3,2,1,0:T(2,128)(2,1)} %bitcast.3), calls=%async_computation | async-start | bytes 2097152 | tf_op jit(solution)/shard_map/all_to_all | solution.py:70
  60.2 2.5 %fusion.19 = f32[128,1,2,384]{3,0,2,1:T(8,128)S(1)} fusion(bf16[1,1,2048,384]{3,2,1,0:T(8,128)(2,1)} %param.9, bf16[128,1,2,2048]{3,2,1,0:T(2,128)(2,1)} %all-to-all-done.2), kind=kOutput, calls=%fused_computation.23 | convolution fusion | flops 402653184 | bytes 3014656 | tf_op jit(solution)/shard_map/nqcd,qdf->nqcf/dot_general | solution.py:71
  62.7 0.0 copy-done
  62.7 4.1 %fusion.1 = bf16[128,1,2,2048]{3,0,2,1:T(8,128)(2,1)} fusion(bf16[1,1,384,2048]{3,2,1,0:T(8,128)(2,1)S(1)} %copy-done, bf16[1,1,2048,384]{3,2,1,0:T(8,128)(2,1)} %param.10, bf16[128,1,2,2048]{3,2,1,0:T(2,128)(2,1)} %all-to-all-done.2, f32[128,1,2,384]{3,0,2,1:T(8,128)S(1)} %fusion.19), kind=kOutput, calls=%fused_computation.3 | convolution fusion | flops 806420480 | bytes 5636096 | tf_op jit(solution)/shard_map/nqcf,qfd->nqcd/dot_general | solution.py:79
  66.8 3.3 %copy.19 = bf16[128,1,2,2048]{3,2,1,0:T(2,128)(2,1)} copy(bf16[128,1,2,2048]{3,0,2,1:T(8,128)(2,1)} %fusion.1) | data formatting | bytes 2097152 | tf_op jit(solution)/shard_map/convert_element_type | solution.py:81
  70.1 21.6 %all-to-all-done = bf16[128,1,2,2048]{3,2,1,0:T(2,128)(2,1)S(1)} async-done(((bf16[128,1,2,2048]{3,2,1,0:T(2,128)(2,1)}), bf16[128,1,2,2048]{3,2,1,0:T(2,128)(2,1)S(1)}, u32[]{:S(2)}, u32[]{:S(2)}) %all-to-all-start) | async-done | bytes 1048608 | tf_op jit(solution)/shard_map/all_to_all | solution.py:70
  91.7 0.0 copy-start.1
  91.7 1.0 copy-done.1
  92.7 5.9 %all-to-all-start.3 = ((bf16[128,1,2,2048]{3,2,1,0:T(2,128)(2,1)}), bf16[128,1,2,2048]{3,2,1,0:T(2,128)(2,1)S(1)}, u32[]{:S(2)}, u32[]{:S(2)}) async-start(bf16[128,1,2,2048]{3,2,1,0:T(2,128)(2,1)} %copy.19), calls=%async_computation.3 | async-start | bytes 2097152 | tf_op jit(solution)/shard_map/all_to_all | solution.py:78
  98.7 2.5 %fusion.16 = f32[128,1,2,384]{3,0,2,1:T(8,128)S(1)} fusion(bf16[1,1,2048,384]{3,2,1,0:T(8,128)(2,1)} %param.9, bf16[128,1,2,2048]{3,2,1,0:T(2,128)(2,1)} %copy-done.1), kind=kOutput, calls=%fused_computation.22 | convolution fusion | flops 402653184 | bytes 3014656 | tf_op jit(solution)/shard_map/nqcd,qdf->nqcf/dot_general | solution.py:71
  101.1 4.1 %fusion = bf16[128,1,2,2048]{3,0,2,1:T(8,128)(2,1)} fusion(bf16[1,1,384,2048]{3,2,1,0:T(8,128)(2,1)S(1)} %copy-done, bf16[1,1,2048,384]{3,2,1,0:T(8,128)(2,1)} %param.10, bf16[128,1,2,2048]{3,2,1,0:T(2,128)(2,1)} %copy-done.1, f32[128,1,2,384]{3,0,2,1:T(8,128)S(1)} %fusion.16), kind=kOutput, calls=%fused_computation.2 | convolution fusion | flops 806420480 | bytes 5636096 | tf_op jit(solution)/shard_map/nqcf,qfd->nqcd/dot_general | solution.py:79
  105.2 3.3 %copy.16 = bf16[128,1,2,2048]{3,2,1,0:T(2,128)(2,1)} copy(bf16[128,1,2,2048]{3,0,2,1:T(8,128)(2,1)} %fusion) | data formatting | bytes 2097152 | tf_op jit(solution)/shard_map/convert_element_type | solution.py:81
  108.5 0.0 copy-start.4
  108.5 21.6 %all-to-all-done.3 = bf16[128,1,2,2048]{3,2,1,0:T(2,128)(2,1)S(1)} async-done(((bf16[128,1,2,2048]{3,2,1,0:T(2,128)(2,1)}), bf16[128,1,2,2048]{3,2,1,0:T(2,128)(2,1)S(1)}, u32[]{:S(2)}, u32[]{:S(2)}) %all-to-all-start.3) | async-done | bytes 1048608 | tf_op jit(solution)/shard_map/all_to_all | solution.py:78
  130.1 6.4 %all-to-all-start.1 = ((bf16[128,1,2,2048]{3,2,1,0:T(2,128)(2,1)}), bf16[128,1,2,2048]{3,2,1,0:T(2,128)(2,1)}, u32[]{:S(2)}, u32[]{:S(2)}) async-start(bf16[128,1,2,2048]{3,2,1,0:T(2,128)(2,1)} %copy.16), calls=%async_computation.1 | async-start | bytes 2097152 | tf_op jit(solution)/shard_map/all_to_all | solution.py:78
  136.6 0.0 copy-done.4
  136.6 0.1 mul.106
  136.7 0.1 mul.93
  136.8 0.3 fusion.85
  137.0 0.3 fusion.91
  137.3 0.6 add_convert_fusion
  137.9 0.2 convert_element_type.138
  138.1 29.6 %all-to-all-done.1 = bf16[128,1,2,2048]{3,2,1,0:T(2,128)(2,1)} async-done(((bf16[128,1,2,2048]{3,2,1,0:T(2,128)(2,1)}), bf16[128,1,2,2048]{3,2,1,0:T(2,128)(2,1)}, u32[]{:S(2)}, u32[]{:S(2)}) %all-to-all-start.1) | async-done | bytes 1048608 | tf_op jit(solution)/shard_map/all_to_all | solution.py:78
  167.6 1.7 add_convert_fusion.1
  169.4 0.2 convert_element_type.122
  169.6 0.3 fusion.4
  169.9 0.3 fusion.5
  170.2 3.4 %collective-permute-start = (bf16[1,2,8,2048]{3,2,1,0:T(8,128)(2,1)S(1)}, bf16[1,2,8,2048]{3,2,1,0:T(8,128)(2,1)S(1)}, u32[]{:S(2)}, u32[]{:S(2)}) collective-permute-start(bf16[1,2,8,2048]{3,2,1,0:T(8,128)(2,1)S(1)} %maximum_bitcast_fusion), channel_id=1, source_target_pairs={{384,0},{0,128},{128,256},{256,384},{385,1},{1,129},{129,257},{257... | collective-permute-start | bytes 196616 | tf_op jit(solution)/shard_map/ppermute | solution.py:12
  173.6 4.0 %collective-permute-done = bf16[1,2,8,2048]{3,2,1,0:T(8,128)(2,1)S(1)} collective-permute-done((bf16[1,2,8,2048]{3,2,1,0:T(8,128)(2,1)S(1)}, bf16[1,2,8,2048]{3,2,1,0:T(8,128)(2,1)S(1)}, u32[]{:S(2)}, u32[]{:S(2)}) %collective-permute-start) | collective-permute-done | bytes 65568 | tf_op jit(solution)/shard_map/ppermute | solution.py:12
  177.6 0.6 copy.41
  (5 shorter events, 0.0 us)
Async XLA Ops:
  0.0 62.7 %copy-start = (bf16[1,1,384,2048]{3,2,1,0:T(8,128)(2,1)S(1)}, bf16[1,1,384,2048]{3,2,1,0:T(8,128)(2,1)}, u32[]{:S(2)}) copy-start(bf16[1,1,384,2048]{3,2,1,0:T(8,128)(2,1)} %param.11) | copy-start | bytes 4718596
  5.2 18.7 %copy-start.2 = (bf16[1,2,8,2048]{3,2,1,0:T(8,128)(2,1)S(1)}, bf16[1,2,8,2048]{3,2,1,0:T(8,128)(2,1)}, u32[]{:S(2)}) copy-start(bf16[1,2,8,2048]{3,2,1,0:T(8,128)(2,1)} %param.7) | copy-start | bytes 196612
  5.2 18.7 %copy-start.3 = (f32[1,2048]{1,0:T(1,128)S(1)}, f32[1,2048]{1,0:T(1,128)}, u32[]{:S(2)}) copy-start(f32[1,2048]{1,0:T(1,128)} %param.8) | copy-start | bytes 24580
  5.2 49.1 %all-to-all-start.2 = ((bf16[128,1,2,2048]{3,2,1,0:T(2,128)(2,1)}), bf16[128,1,2,2048]{3,2,1,0:T(2,128)(2,1)}, u32[]{:S(2)}, u32[]{:S(2)}) async-start(bf16[128,1,2,2048]{3,2,1,0:T(2,128)(2,1)} %bitcast.26), calls=%async_computation.2 | async-start | bytes 2097152 | tf_op jit(solution)/shard_map/all_to_all | solution.py:70
  54.3 37.4 %all-to-all-start = ((bf16[128,1,2,2048]{3,2,1,0:T(2,128)(2,1)}), bf16[128,1,2,2048]{3,2,1,0:T(2,128)(2,1)S(1)}, u32[]{:S(2)}, u32[]{:S(2)}) async-start(bf16[128,1,2,2048]{3,2,1,0:T(2,128)(2,1)} %bitcast.3), calls=%async_computation | async-start | bytes 2097152 | tf_op jit(solution)/shard_map/all_to_all | solution.py:70
  91.7 1.0 copy-start.1
  92.7 37.4 %all-to-all-start.3 = ((bf16[128,1,2,2048]{3,2,1,0:T(2,128)(2,1)}), bf16[128,1,2,2048]{3,2,1,0:T(2,128)(2,1)S(1)}, u32[]{:S(2)}, u32[]{:S(2)}) async-start(bf16[128,1,2,2048]{3,2,1,0:T(2,128)(2,1)} %copy.19), calls=%async_computation.3 | async-start | bytes 2097152 | tf_op jit(solution)/shard_map/all_to_all | solution.py:78
  108.5 28.0 %copy-start.4 = (f32[1,2,8,8]{3,2,1,0:T(8,128)S(1)}, f32[1,2,8,8]{3,2,1,0:T(8,128)}, u32[]{:S(2)}) copy-start(f32[1,2,8,8]{3,2,1,0:T(8,128)} %param.13) | copy-start | bytes 1540
  130.1 37.5 %all-to-all-start.1 = ((bf16[128,1,2,2048]{3,2,1,0:T(2,128)(2,1)}), bf16[128,1,2,2048]{3,2,1,0:T(2,128)(2,1)}, u32[]{:S(2)}, u32[]{:S(2)}) async-start(bf16[128,1,2,2048]{3,2,1,0:T(2,128)(2,1)} %copy.16), calls=%async_computation.1 | async-start | bytes 2097152 | tf_op jit(solution)/shard_map/all_to_all | solution.py:78
  170.2 7.4 %collective-permute-start = (bf16[1,2,8,2048]{3,2,1,0:T(8,128)(2,1)S(1)}, bf16[1,2,8,2048]{3,2,1,0:T(8,128)(2,1)S(1)}, u32[]{:S(2)}, u32[]{:S(2)}) collective-permute-start(bf16[1,2,8,2048]{3,2,1,0:T(8,128)(2,1)S(1)} %maximum_bitcast_fusion), channel_id=1, source_target_pairs={{384,0},{0,128},{128,256},{256,384},{385,1},{1,129},{129,257},{257... | collective-permute-start | bytes 196616 | tf_op jit(solution)/shard_map/ppermute | solution.py:12
where the time goes:
time: 179 us; the launch traced here: 178 us
  waiting for transfers between devices  105 us (59%)
  starting transfers between devices  39.6 us (22%)
  matrix products  16.2 us (9%)
  local copies, waits for them, and re-layouts  12.8 us (7%)
  other arithmetic  4.18 us (2%)
    all_to_all x2, waiting for transfers between devices, on_device(): lax.all_to_all(jnp.einsum('nqcf,qfd->nqcd', hidden, down_local, preferred...  51.1 us
    all_to_all x2, waiting for transfers between devices, on_device(): lax.all_to_all(outgoing, 'expert', split_axis=0, concat_axis=0, tiled=True)  50 us
    all_to_all x2, starting transfers between devices, on_device(): lax.all_to_all(outgoing, 'expert', split_axis=0, concat_axis=0, tiled=True)  23.9 us
    all_to_all x2, starting transfers between devices, on_device(): lax.all_to_all(jnp.einsum('nqcf,qfd->nqcd', hidden, down_local, preferred...  12.4 us
    dot_general x2, matrix products, on_device(): jnp.einsum('nqcf,qfd->nqcd', hidden, down_local, preferred_element_type=j...  8.16 us
    convert_element_type x2, local copies, waits for them, and re-layouts, on_device(): returned = lax.all_to_all(jnp.einsum('nqcf,qfd->nqcd', hidden, down_local...  6.61 us
    dot_general x2, matrix products, on_device(): jnp.einsum('nqcd,qdf->nqcf', arrived, gate_local, preferred_element_type=...  4.92 us
    ppermute x1, waiting for transfers between devices, shifted(): return lax.ppermute(block, axis, route)  3.96 us
  transfers between devices with their start and end apart: 5, of which 5 were waited for; matrix products, arithmetic and copies ran while one was open for 13% of the time, Pallas kernels for 0%

commit v1 on v0

v1 whole, which is shorter than its diff:
```python
import jax
import jax.numpy as jnp
from jax import lax
from jax.experimental import pallas as pl
from jax.experimental.pallas import tpu as pltpu
from jax.sharding import PartitionSpec as P

norm_eps = 1e-06
RING = 8
CAP = 2
MIB = 1 << 20


def ring_groups(first_axis):
    along_y = [[z * 16 + y * 2 for y in range(RING)] for z in range(RING)]
    along_z = [[z * 16 + y * 2 for z in range(RING)] for y in range(RING)]
    even, odd = (along_y, along_z) if first_axis == "y" else (along_z, along_y)
    return even + [[i + 1 for i in ring] for ring in odd]


def exchange(chunks, groups):
    return lax.all_to_all(
        chunks, "expert", split_axis=0, concat_axis=0, tiled=True, axis_index_groups=groups
    )


def dot(a, b, contract=((1,), (0,))):
    return lax.dot_general(a, b, (contract, ((), ())), preferred_element_type=jnp.float32)


def payload_kernel(tokens, gain, ids, route, out):
    width = tokens.shape[1]
    rows = tokens[...].astype(jnp.float32)
    inv_scale = lax.rsqrt(jnp.mean(rows * rows, axis=-1, keepdims=True) + norm_eps)
    normed = (rows * inv_scale * gain[...]).astype(jnp.bfloat16)
    id_rows, weight_rows = ids[...], route[...]
    lane = lax.broadcasted_iota(jnp.int32, (rows.shape[0], 128), 1)
    dense = jnp.zeros((rows.shape[0], 128), jnp.float32)
    for k in range(id_rows.shape[1]):
        dense += jnp.where(lane % 64 == id_rows[:, k : k + 1], weight_rows[:, k : k + 1], 0.0)
    high = dense.astype(jnp.bfloat16)
    low = (dense - high.astype(jnp.float32)).astype(jnp.bfloat16)
    parts = jnp.where(lane < 64, high.astype(jnp.float32), low.astype(jnp.float32))
    parts = parts.astype(jnp.bfloat16)
    for i in range(RING):
        out[i, :, :width] = normed
        out[i, :, width:] = parts


def pack_kernel(place, gathered, out, blend):
    tokens = gathered.shape[0] * gathered.shape[1]
    width = out.shape[2]
    slots = out.shape[0] * out.shape[1]
    mine = place[0]
    z, y, core = mine // 16, (mine // 2) % RING, mine % 2
    shape = (slots, 128)
    row = lax.broadcasted_iota(jnp.int32, shape, 0)
    lane = lax.broadcasted_iota(jnp.int32, shape, 1)
    member, other, block, rank = row >> 6, (row >> 5) & 1, (row >> 1) & 15, row & 1
    chip = jnp.where(core == 0, (member & 3) * RING + y, (z % 4) * RING + member)
    expert = chip * 2 + (other ^ core)
    parts = gathered[:, :, width:].reshape(tokens, 128)
    pick_high = (lane == expert).astype(jnp.bfloat16)
    pick_low = (lane == expert + 64).astype(jnp.bfloat16)
    high = dot(pick_high, parts, ((1,), (1,)))
    low = dot(pick_low, parts, ((1,), (1,)))
    named = jnp.where((high != 0.0) & ((lane >> 3) == block), 1.0, 0.0)
    before = (
        lax.broadcasted_iota(jnp.int32, (128, 128), 0)
        < lax.broadcasted_iota(jnp.int32, (128, 128), 1)
    ).astype(jnp.bfloat16)
    earlier = dot(named.astype(jnp.bfloat16), before)
    pick = jnp.where(earlier == rank.astype(jnp.float32), named, 0.0)
    blend[0] = (pick * high).astype(jnp.bfloat16)
    blend[1] = (pick * low).astype(jnp.bfloat16)
    rows = gathered[:, :, :width].reshape(tokens, width)
    out[...] = dot(pick.astype(jnp.bfloat16), rows).astype(jnp.bfloat16).reshape(out.shape)


def expert_kernel(rows, *refs):
    weights, out = refs[:6], refs[6]
    up_gate, down, sems = refs[7:]
    hidden_units = down.shape[1]
    half = rows.shape[1] // 2
    copies = []
    for e in range(2):
        gate_ref, up_ref, down_ref = weights[3 * e : 3 * e + 3]
        copies.append(
            [
                pltpu.make_async_copy(gate_ref, up_gate.at[e, 0], sems.at[e, 0]),
                pltpu.make_async_copy(up_ref, up_gate.at[e, 1], sems.at[e, 1]),
                pltpu.make_async_copy(down_ref, down.at[e], sems.at[e, 2]),
            ]
        )
    for group in copies:
        for copy in group:
            copy.start()
    for e in range(2):
        x = rows[:, e * half : (e + 1) * half, :].reshape(-1, rows.shape[2])
        copies[e][0].wait()
        gate = dot(x, up_gate[e, 0])
        copies[e][1].wait()
        up = dot(x, up_gate[e, 1])
        hidden = (gate / (1.0 + jnp.exp(-gate)) * up).astype(jnp.bfloat16)
        copies[e][2].wait()
        answer = dot(hidden, down[e]).astype(jnp.bfloat16)
        out[:, e * half : (e + 1) * half, :] = answer.reshape(out.shape[0], half, out.shape[2])


def mix_kernel(returned, blend, out):
    rows = returned[...].reshape(-1, returned.shape[2])
    total = dot(blend[0], rows, ((0,), (0,))) + dot(blend[1], rows, ((0,), (0,)))
    out[...] = total.astype(jnp.bfloat16).reshape(out.shape)


def finish_kernel(tokens, pieces, out):
    total = tokens[...].astype(jnp.float32)
    for i in range(RING):
        total += pieces[i].astype(jnp.float32)
    out[...] = total.astype(jnp.bfloat16)


def kernel_call(body, out_shape, operands, specs=None, scratch=(), limit=24, flops=0, moved=0):
    whole = pl.BlockSpec(memory_space=pltpu.VMEM)
    return pl.pallas_call(
        body,
        out_shape=out_shape,
        in_specs=specs or [whole] * len(operands),
        out_specs=jax.tree.map(lambda _: whole, out_shape),
        scratch_shapes=scratch,
        compiler_params=pltpu.CompilerParams(vmem_limit_bytes=limit * MIB),
        cost_estimate=pl.CostEstimate(flops=flops, bytes_accessed=moved, transcendentals=0),
    )(*operands)


def on_device(
    activations, norm_gain, gate_weight, up_weight, down_weight, expert_ids, route_weights
):
    _, micro, block_tokens, width = activations.shape
    hidden_units = gate_weight.shape[3]
    held = micro * block_tokens
    slots = RING * micro * 2 * CAP
    spread, deliver = ring_groups("y"), ring_groups("z")
    whole = pl.BlockSpec(memory_space=pltpu.VMEM)
    bf16 = jnp.bfloat16

    own = [gate_weight[0, 0], up_weight[0, 0], down_weight[0, 0]]
    swap = [(i, i ^ 1) for i in range(lax.axis_size("expert"))]
    tokens = activations.reshape(held, width)
    payload = kernel_call(
        payload_kernel,
        jax.ShapeDtypeStruct((RING, held, width + 128), bf16),
        (tokens, norm_gain, expert_ids.reshape(held, -1), route_weights.reshape(held, -1)),
    )
    gathered = exchange(payload, spread)
    sibling = [lax.ppermute(w, "expert", swap) for w in own]
    place = lax.axis_index("expert").astype(jnp.int32).reshape(1)
    outgoing, blend = kernel_call(
        pack_kernel,
        (
            jax.ShapeDtypeStruct((RING, slots, width), bf16),
            jax.ShapeDtypeStruct((2, RING * slots, RING * held), bf16),
        ),
        (place, gathered),
        specs=[pl.BlockSpec(memory_space=pltpu.SMEM), whole],
    )
    arrived = exchange(outgoing, deliver)
    answers = kernel_call(
        expert_kernel,
        jax.ShapeDtypeStruct((RING, slots, width), bf16),
        (arrived, *own, *sibling),
        specs=[whole] + [pl.BlockSpec(memory_space=pl.ANY)] * 6,
        scratch=(
            pltpu.VMEM((2, 2, width, hidden_units), bf16),
            pltpu.VMEM((2, hidden_units, width), bf16),
            pltpu.SemaphoreType.DMA((2, 3)),
        ),
        limit=36,
        flops=6 * RING * slots * width * hidden_units,
    )
    returned = exchange(answers, deliver)
    partial = kernel_call(
        mix_kernel, jax.ShapeDtypeStruct((RING, held, width), bf16), (returned, blend)
    )
    pieces = exchange(partial, spread)
    layer_out = kernel_call(
        finish_kernel, jax.ShapeDtypeStruct((held, width), bf16), (tokens, pieces)
    )
    sections = lax.axis_size("segment")
    route = [(i, (i + 1) % sections) for i in range(sections)]
    return lax.ppermute(layer_out, "segment", route).reshape(activations.shape)


def solution(mesh):
    return jax.shard_map(
        on_device,
        mesh=mesh,
        in_specs=(
            P("segment", None, "expert", None),
            P("segment", None),
            P("segment", "expert", None, None),
            P("segment", "expert", None, None),
            P("segment", "expert", None, None),
            P("segment", None, "expert", None),
            P("segment", None, "expert", None),
        ),
        out_specs=P("segment", None, "expert", None),
        check_vma=False,
    )
```

time: 179 us -> 138 us (0.77)
  waiting for transfers between devices: 105 us -> 36.7 us
  blocking collectives: 0 us -> 48.3 us
  matrix products: 16.2 us -> 0 us
  starting transfers between devices: 39.6 us -> 27.5 us
  Pallas kernels: 0 us -> 7.83 us
  other arithmetic: 4.18 us -> 0 us
  local copies, waits for them, and re-layouts: 12.8 us -> 16.8 us
    all_to_all x4 -> x2, waiting for transfers between devices: 101 us -> 31.3 us  [exchange(): lax.all_to_all(chunks, 'expert', split_axis=0, concat_axis=0, tiled=True,...]
    all_to_all x0 -> x2, blocking collectives: none -> 48.3 us  [exchange(): lax.all_to_all(chunks, 'expert', split_axis=0, concat_axis=0, tiled=True,...]
    all_to_all x4 -> x2, starting transfers between devices: 36.2 us -> 17.8 us  [exchange(): lax.all_to_all(chunks, 'expert', split_axis=0, concat_axis=0, tiled=True,...]
    dot_general x12 -> x0, matrix products: 16.2 us -> none  [the longest x2 8.16 us: on_device(): jnp.einsum('nqcf,qfd->nqcd', hidden, down_local, preferred_element_type=j...]
    unnamed x11 -> x31, local copies, waits for them, and re-layouts: 1.67 us -> 16.8 us
    pallas_call x0 -> x5, Pallas kernels: none -> 7.83 us  [kernel_call(): pl.pallas_call(body, out_shape=out_shape, in_specs=specs or [whole] * len...]
    convert_element_type x4 -> x0, local copies, waits for them, and re-layouts: 7 us -> none  [the longest x2 6.61 us: on_device(): returned = lax.all_to_all(jnp.einsum('nqcf,qfd->nqcd', hidden, down_local...]
    ppermute x1 -> x4, starting transfers between devices: 3.4 us -> 9.64 us  [the longest x3 6.24 us: on_device(): sibling = [lax.ppermute(w, 'expert', swap) for w in own]]
  transfers between devices with their start and end apart: 5 -> 6, of which waited for: 5 -> 5; matrix products, arithmetic and copies ran while one was open for 13% -> 0% of each run, Pallas kernels for 0% -> 0%
where the time goes in v1:
time: 138 us; the launch traced here: 137 us
  blocking collectives  48.3 us (35%)
  waiting for transfers between devices  36.7 us (27%)
  starting transfers between devices  27.5 us (20%)
  local copies, waits for them, and re-layouts  16.8 us (12%)
  Pallas kernels  7.83 us (6%)
    all_to_all x2, blocking collectives, exchange(): lax.all_to_all(chunks, 'expert', split_axis=0, concat_axis=0, tiled=True,...  48.3 us
    all_to_all x2, waiting for transfers between devices, exchange(): lax.all_to_all(chunks, 'expert', split_axis=0, concat_axis=0, tiled=True,...  31.3 us
    all_to_all x2, starting transfers between devices, exchange(): lax.all_to_all(chunks, 'expert', split_axis=0, concat_axis=0, tiled=True,...  17.8 us
    unnamed x31, local copies, waits for them, and re-layouts  16.8 us
    pallas_call x5, Pallas kernels, kernel_call(): pl.pallas_call(body, out_shape=out_shape, in_specs=specs or [whole] * len...  7.83 us
    ppermute x3, starting transfers between devices, on_device(): sibling = [lax.ppermute(w, 'expert', swap) for w in own]  6.24 us
    ppermute x1, waiting for transfers between devices, on_device(): return lax.ppermute(layer_out, 'segment', route).reshape(activations.shape)  3.96 us
    ppermute x1, starting transfers between devices, on_device(): return lax.ppermute(layer_out, 'segment', route).reshape(activations.shape)  3.4 us
  transfers between devices with their start and end apart: 6, of which 5 were waited for; matrix products, arithmetic and copies ran while one was open for 0% of the time, Pallas kernels for 0%

profile of v1, /device:TPU:8, one launch (start us, length us, event | category | flops | bytes accessed | tf_op | source)
XLA Modules:
  0.0 137.2 jit_solution(1370581474555423007)
XLA Ops:
  0.0 0.0 copy-start.10
  0.0 0.8 copy-done.10
  0.8 0.0 copy-start.12
  0.8 0.7 copy-done.12
  1.5 0.0 copy-start.13
  1.5 0.7 copy-done.13
  2.2 0.0 copy-start.14
  2.2 0.7 copy-done.14
  2.9 1.0 shard_map.73
  3.9 9.3 %all-to-all-start = ((bf16[8,16,2176]{2,1,0:T(8,128)(2,1)}), bf16[8,16,2176]{2,1,0:T(8,128)(2,1)S(1)}, u32[]{:S(2)}, u32[]{:S(2)}) async-start(bf16[8,16,2176]{2,1,0:T(8,128)(2,1)} %shard_map.73), calls=%async_computation | async-start | bytes 1114112 | tf_op jit(solution)/shard_map/all_to_all | solution.py:22
  13.2 12.2 %all-to-all-done.gathered = bf16[8,16,2176]{2,1,0:T(8,128)(2,1)S(1)} async-done(((bf16[8,16,2176]{2,1,0:T(8,128)(2,1)}), bf16[8,16,2176]{2,1,0:T(8,128)(2,1)S(1)}, u32[]{:S(2)}, u32[]{:S(2)}) %all-to-all-start) | async-done | bytes 557088 | tf_op jit(solution)/shard_map/all_to_all | solution.py:22
  25.4 1.0 shard_map.74
  26.3 0.0 copy-start
  26.3 1.3 copy-done
  27.7 8.6 %all-to-all-start.1 = ((bf16[8,64,2048]{2,1,0:T(8,128)(2,1)}), bf16[8,64,2048]{2,1,0:T(8,128)(2,1)S(1)}, u32[]{:S(2)}, u32[]{:S(2)}) async-start(bf16[8,64,2048]{2,1,0:T(8,128)(2,1)} %copy-done), calls=%async_computation.1 | async-start | bytes 4194304 | tf_op jit(solution)/shard_map/all_to_all | solution.py:22
  36.2 1.9 %collective-permute-start = (bf16[2048,384]{1,0:T(8,128)(2,1)}, bf16[2048,384]{1,0:T(8,128)(2,1)S(1)}, u32[]{:S(2)}, u32[]{:S(2)}) collective-permute-start(bf16[2048,384]{1,0:T(8,128)(2,1)} %bitcast.8), channel_id=1, source_target_pairs={{0,1},{1,0},{2,3},{3,2},{4,5},{5,4},{6,7},{7,6},{8,9},{9,8},{10,11... | collective-permute-start | bytes 4718600 | tf_op jit(solution)/shard_map/ppermute | solution.py:156
  38.2 2.4 %collective-permute-start.1 = (bf16[2048,384]{1,0:T(8,128)(2,1)}, bf16[2048,384]{1,0:T(8,128)(2,1)S(1)}, u32[]{:S(2)}, u32[]{:S(2)}) collective-permute-start(bf16[2048,384]{1,0:T(8,128)(2,1)} %bitcast.10), channel_id=1, source_target_pairs={{0,1},{1,0},{2,3},{3,2},{4,5},{5,4},{6,7},{7,6},{8,9},{9,8},{10,11... | collective-permute-start | bytes 4718600 | tf_op jit(solution)/shard_map/ppermute | solution.py:156
  40.6 1.9 %collective-permute-start.2 = (bf16[384,2048]{1,0:T(8,128)(2,1)}, bf16[384,2048]{1,0:T(8,128)(2,1)S(1)}, u32[]{:S(2)}, u32[]{:S(2)}) collective-permute-start(bf16[384,2048]{1,0:T(8,128)(2,1)} %bitcast.12), channel_id=1, source_target_pairs={{0,1},{1,0},{2,3},{3,2},{4,5},{5,4},{6,7},{7,6},{8,9},{9,8},{10,11... | collective-permute-start | bytes 4718600 | tf_op jit(solution)/shard_map/ppermute | solution.py:156
  42.5 0.0 collective-permute-done.refs_3_
  42.5 0.0 copy-start.4
  42.5 1.1 copy-done.4
  43.7 0.3 collective-permute-done.1.refs_4_
  44.0 0.0 copy-start.6
  44.0 1.2 copy-done.6
  45.1 1.1 collective-permute-done.2.refs_5_
  46.2 0.0 copy-start.8
  46.2 1.2 copy-done.8
  47.4 19.1 %all-to-all-done.1.rows = bf16[8,64,2048]{2,1,0:T(8,128)(2,1)S(1)} async-done(((bf16[8,64,2048]{2,1,0:T(8,128)(2,1)}), bf16[8,64,2048]{2,1,0:T(8,128)(2,1)S(1)}, u32[]{:S(2)}, u32[]{:S(2)}) %all-to-all-start.1) | async-done | bytes 2097184 | tf_op jit(solution)/shard_map/all_to_all | solution.py:22
  66.5 0.0 copy-start.1
  66.5 1.4 %copy-done.1 = bf16[1,1,2048,384]{3,2,1,0:T(8,128)(2,1)S(1)} copy-done((bf16[1,1,2048,384]{3,2,1,0:T(8,128)(2,1)S(1)}, bf16[1,1,2048,384]{3,2,1,0:T(8,128)(2,1)}, u32[]{:S(2)}) %copy-start.1) | copy-done | bytes 1572888
  67.9 0.0 copy-start.2
  67.9 1.4 %copy-done.2 = bf16[1,1,2048,384]{3,2,1,0:T(8,128)(2,1)S(1)} copy-done((bf16[1,1,2048,384]{3,2,1,0:T(8,128)(2,1)S(1)}, bf16[1,1,2048,384]{3,2,1,0:T(8,128)(2,1)}, u32[]{:S(2)}) %copy-start.2) | copy-done | bytes 1572888
  69.3 0.0 copy-start.3
  69.3 1.4 %copy-done.3 = bf16[1,1,384,2048]{3,2,1,0:T(8,128)(2,1)S(1)} copy-done((bf16[1,1,384,2048]{3,2,1,0:T(8,128)(2,1)S(1)}, bf16[1,1,384,2048]{3,2,1,0:T(8,128)(2,1)}, u32[]{:S(2)}) %copy-start.3) | copy-done | bytes 1572888
  70.7 0.0 copy-start.5
  70.7 1.4 %copy-done.5 = bf16[2048,384]{1,0:T(8,128)(2,1)S(1)} copy-done((bf16[2048,384]{1,0:T(8,128)(2,1)S(1)}, bf16[2048,384]{1,0:T(8,128)(2,1)}, u32[]{:S(2)}) %copy-start.5) | copy-done | bytes 1572888
  72.2 0.0 copy-start.7
  72.2 1.4 %copy-done.7 = bf16[2048,384]{1,0:T(8,128)(2,1)S(1)} copy-done((bf16[2048,384]{1,0:T(8,128)(2,1)S(1)}, bf16[2048,384]{1,0:T(8,128)(2,1)}, u32[]{:S(2)}) %copy-start.7) | copy-done | bytes 1572888
  73.6 0.0 copy-start.9
  73.6 1.4 %copy-done.9 = bf16[384,2048]{1,0:T(8,128)(2,1)S(1)} copy-done((bf16[384,2048]{1,0:T(8,128)(2,1)S(1)}, bf16[384,2048]{1,0:T(8,128)(2,1)}, u32[]{:S(2)}) %copy-start.9) | copy-done | bytes 1572888
  75.0 5.1 %shard_map.75 = bf16[8,64,2048]{2,1,0:T(8,128)(2,1)S(1)} custom-call(bf16[8,64,2048]{2,1,0:T(8,128)(2,1)S(1)} %all-to-all-done.1.rows, bf16[2048,384]{1,0:T(8,128)(2,1)S(1)} %bitcast.9, bf16[2048,384]{1,0:T(8,128)(2,1)S(1)} %bitcast.11, bf16[384,2048]{1,0:T(8,128)(2,1)S(1)} %bitcast.13, bf16[2048,384]{1,0:T(8,128)(2,1)S(1)} %copy-done.5, ...), custom_call_target="tpu_custom_call" | custom-call | flops 2415919104 | tf_op jit(solution)/shard_map/pallas_call | solution.py:125
  80.1 32.6 %all_to_all.20.returned = bf16[8,64,2048]{2,1,0:T(8,128)(2,1)S(1)} all-to-all(bf16[8,64,2048]{2,1,0:T(8,128)(2,1)S(1)} %shard_map.75), channel_id=1, replica_groups={{0,16,32,48,64,80,96,112},{2,18,34,50,66,82,98,114},{4,20,36,52,68,84,1..., dimensions={0} | all-to-all | bytes 4194304 | tf_op jit(solution)/shard_map/all_to_all | solution.py:22
  112.6 0.0 copy-start.11
  112.6 0.7 shard_map.76
  113.4 15.7 %all_to_all.21.pieces = bf16[8,16,2048]{2,1,0:T(8,128)(2,1)S(1)} all-to-all(bf16[8,16,2048]{2,1,0:T(8,128)(2,1)S(1)} %shard_map.76), channel_id=1, replica_groups={{0,2,4,6,8,10,12,14},{16,18,20,22,24,26,28,30},{32,34,36,38,40,42,44,46..., dimensions={0} | all-to-all | bytes 1048576 | tf_op jit(solution)/shard_map/all_to_all | solution.py:22
  129.1 0.0 copy-done.11
  129.1 0.1 shard_map.77
  129.2 3.4 %collective-permute-start.3 = (bf16[16,2048]{1,0:T(8,128)(2,1)S(1)}, bf16[16,2048]{1,0:T(8,128)(2,1)S(1)}, u32[]{:S(2)}, u32[]{:S(2)}) collective-permute-start(bf16[16,2048]{1,0:T(8,128)(2,1)S(1)} %shard_map.77), channel_id=1, source_target_pairs={{0,128},{128,256},{256,384},{384,0},{1,129},{129,257},{257,385},{3... | collective-permute-start | bytes 196616 | tf_op jit(solution)/shard_map/ppermute | solution.py:191
  132.6 4.0 %collective-permute-done.3 = bf16[16,2048]{1,0:T(8,128)(2,1)S(1)} collective-permute-done((bf16[16,2048]{1,0:T(8,128)(2,1)S(1)}, bf16[16,2048]{1,0:T(8,128)(2,1)S(1)}, u32[]{:S(2)}, u32[]{:S(2)}) %collective-permute-start.3) | collective-permute-done | bytes 65568 | tf_op jit(solution)/shard_map/ppermute | solution.py:191
  136.6 0.6 copy.15
Async XLA Ops:
  0.0 0.8 copy-start.10
  0.8 0.7 copy-start.12
  1.5 0.7 copy-start.13
  2.2 0.7 copy-start.14
  3.9 21.5 %all-to-all-start = ((bf16[8,16,2176]{2,1,0:T(8,128)(2,1)}), bf16[8,16,2176]{2,1,0:T(8,128)(2,1)S(1)}, u32[]{:S(2)}, u32[]{:S(2)}) async-start(bf16[8,16,2176]{2,1,0:T(8,128)(2,1)} %shard_map.73), calls=%async_computation | async-start | bytes 1114112 | tf_op jit(solution)/shard_map/all_to_all | solution.py:22
  26.3 1.3 copy-start
  27.7 38.9 %all-to-all-start.1 = ((bf16[8,64,2048]{2,1,0:T(8,128)(2,1)}), bf16[8,64,2048]{2,1,0:T(8,128)(2,1)S(1)}, u32[]{:S(2)}, u32[]{:S(2)}) async-start(bf16[8,64,2048]{2,1,0:T(8,128)(2,1)} %copy-done), calls=%async_computation.1 | async-start | bytes 4194304 | tf_op jit(solution)/shard_map/all_to_all | solution.py:22
  36.2 6.3 %collective-permute-start = (bf16[2048,384]{1,0:T(8,128)(2,1)}, bf16[2048,384]{1,0:T(8,128)(2,1)S(1)}, u32[]{:S(2)}, u32[]{:S(2)}) collective-permute-start(bf16[2048,384]{1,0:T(8,128)(2,1)} %bitcast.8), channel_id=1, source_target_pairs={{0,1},{1,0},{2,3},{3,2},{4,5},{5,4},{6,7},{7,6},{8,9},{9,8},{10,11... | collective-permute-start | bytes 4718600 | tf_op jit(solution)/shard_map/ppermute | solution.py:156
  38.2 5.8 %collective-permute-start.1 = (bf16[2048,384]{1,0:T(8,128)(2,1)}, bf16[2048,384]{1,0:T(8,128)(2,1)S(1)}, u32[]{:S(2)}, u32[]{:S(2)}) collective-permute-start(bf16[2048,384]{1,0:T(8,128)(2,1)} %bitcast.10), channel_id=1, source_target_pairs={{0,1},{1,0},{2,3},{3,2},{4,5},{5,4},{6,7},{7,6},{8,9},{9,8},{10,11... | collective-permute-start | bytes 4718600 | tf_op jit(solution)/shard_map/ppermute | solution.py:156
  40.6 5.7 %collective-permute-start.2 = (bf16[384,2048]{1,0:T(8,128)(2,1)}, bf16[384,2048]{1,0:T(8,128)(2,1)S(1)}, u32[]{:S(2)}, u32[]{:S(2)}) collective-permute-start(bf16[384,2048]{1,0:T(8,128)(2,1)} %bitcast.12), channel_id=1, source_target_pairs={{0,1},{1,0},{2,3},{3,2},{4,5},{5,4},{6,7},{7,6},{8,9},{9,8},{10,11... | collective-permute-start | bytes 4718600 | tf_op jit(solution)/shard_map/ppermute | solution.py:156
  42.5 1.1 copy-start.4
  44.0 1.2 copy-start.6
  46.2 1.2 copy-start.8
  66.5 1.4 %copy-start.1 = (bf16[1,1,2048,384]{3,2,1,0:T(8,128)(2,1)S(1)}, bf16[1,1,2048,384]{3,2,1,0:T(8,128)(2,1)}, u32[]{:S(2)}) copy-start(bf16[1,1,2048,384]{3,2,1,0:T(8,128)(2,1)} %param.9) | copy-start | bytes 4718596
  67.9 1.4 %copy-start.2 = (bf16[1,1,2048,384]{3,2,1,0:T(8,128)(2,1)S(1)}, bf16[1,1,2048,384]{3,2,1,0:T(8,128)(2,1)}, u32[]{:S(2)}) copy-start(bf16[1,1,2048,384]{3,2,1,0:T(8,128)(2,1)} %param.10) | copy-start | bytes 4718596
  69.3 1.4 %copy-start.3 = (bf16[1,1,384,2048]{3,2,1,0:T(8,128)(2,1)S(1)}, bf16[1,1,384,2048]{3,2,1,0:T(8,128)(2,1)}, u32[]{:S(2)}) copy-start(bf16[1,1,384,2048]{3,2,1,0:T(8,128)(2,1)} %param.11) | copy-start | bytes 4718596
  70.7 1.4 %copy-start.5 = (bf16[2048,384]{1,0:T(8,128)(2,1)S(1)}, bf16[2048,384]{1,0:T(8,128)(2,1)}, u32[]{:S(2)}) copy-start(bf16[2048,384]{1,0:T(8,128)(2,1)} %copy-done.4) | copy-start | bytes 4718596
  72.2 1.4 %copy-start.7 = (bf16[2048,384]{1,0:T(8,128)(2,1)S(1)}, bf16[2048,384]{1,0:T(8,128)(2,1)}, u32[]{:S(2)}) copy-start(bf16[2048,384]{1,0:T(8,128)(2,1)} %copy-done.6) | copy-start | bytes 4718596
  73.6 1.4 %copy-start.9 = (bf16[384,2048]{1,0:T(8,128)(2,1)S(1)}, bf16[384,2048]{1,0:T(8,128)(2,1)}, u32[]{:S(2)}) copy-start(bf16[384,2048]{1,0:T(8,128)(2,1)} %copy-done.8) | copy-start | bytes 4718596
  112.6 16.5 %copy-start.11 = (bf16[1,2,8,2048]{3,2,1,0:T(8,128)(2,1)S(1)}, bf16[1,2,8,2048]{3,2,1,0:T(8,128)(2,1)}, u32[]{:S(2)}) copy-start(bf16[1,2,8,2048]{3,2,1,0:T(8,128)(2,1)} %param.7) | copy-start | bytes 196612
  129.2 7.4 %collective-permute-start.3 = (bf16[16,2048]{1,0:T(8,128)(2,1)S(1)}, bf16[16,2048]{1,0:T(8,128)(2,1)S(1)}, u32[]{:S(2)}, u32[]{:S(2)}) collective-permute-start(bf16[16,2048]{1,0:T(8,128)(2,1)S(1)} %shard_map.77), channel_id=1, source_target_pairs={{0,128},{128,256},{256,384},{384,0},{1,129},{129,257},{257,385},{3... | collective-permute-start | bytes 196616 | tf_op jit(solution)/shard_map/ppermute | solution.py:191

commit v2 on v1

--- a/solution.py
+++ b/solution.py
@@ -28,7 +28,13 @@
     return lax.dot_general(a, b, (contract, ((), ())), preferred_element_type=jnp.float32)
 
 
-def payload_kernel(tokens, gain, ids, route, out):
+def payload_kernel(*refs):
+    out, (tokens, gain, ids, route, sems) = refs[4], refs[5:]
+    copies = [pltpu.make_async_copy(refs[i], refs[5 + i], sems.at[i]) for i in range(4)]
+    for copy in copies:
+        copy.start()
+    for copy in copies:
+        copy.wait()
     width = tokens.shape[1]
     rows = tokens[...].astype(jnp.float32)
     inv_scale = lax.rsqrt(jnp.mean(rows * rows, axis=-1, keepdims=True) + norm_eps)
@@ -56,9 +62,9 @@
     shape = (slots, 128)
     row = lax.broadcasted_iota(jnp.int32, shape, 0)
     lane = lax.broadcasted_iota(jnp.int32, shape, 1)
-    member, other, block, rank = row >> 6, (row >> 5) & 1, (row >> 1) & 15, row & 1
+    member, which, block, rank = row >> 6, (row >> 5) & 1, (row >> 1) & 15, row & 1
     chip = jnp.where(core == 0, (member & 3) * RING + y, (z % 4) * RING + member)
-    expert = chip * 2 + (other ^ core)
+    expert = chip * 2 + which
     parts = gathered[:, :, width:].reshape(tokens, 128)
     pick_high = (lane == expert).astype(jnp.bfloat16)
     pick_low = (lane == expert + 64).astype(jnp.bfloat16)
@@ -78,31 +84,26 @@
 
 
 def expert_kernel(rows, *refs):
-    weights, out = refs[:6], refs[6]
-    up_gate, down, sems = refs[7:]
+    gate_ref, up_ref, down_ref, out, gate_up, down, sems = refs
     hidden_units = down.shape[1]
     half = rows.shape[1] // 2
     copies = []
     for e in range(2):
-        gate_ref, up_ref, down_ref = weights[3 * e : 3 * e + 3]
-        copies.append(
-            [
-                pltpu.make_async_copy(gate_ref, up_gate.at[e, 0], sems.at[e, 0]),
-                pltpu.make_async_copy(up_ref, up_gate.at[e, 1], sems.at[e, 1]),
-                pltpu.make_async_copy(down_ref, down.at[e], sems.at[e, 2]),
-            ]
-        )
-    for group in copies:
-        for copy in group:
-            copy.start()
+        copies += [
+            pltpu.make_async_copy(gate_ref.at[e], gate_up.at[e, :, :hidden_units], sems.at[e, 0]),
+            pltpu.make_async_copy(up_ref.at[e], gate_up.at[e, :, hidden_units:], sems.at[e, 1]),
+            pltpu.make_async_copy(down_ref.at[e], down.at[e], sems.at[e, 2]),
+        ]
+    for copy in copies:
+        copy.start()
     for e in range(2):
         x = rows[:, e * half : (e + 1) * half, :].reshape(-1, rows.shape[2])
-        copies[e][0].wait()
-        gate = dot(x, up_gate[e, 0])
-        copies[e][1].wait()
-        up = dot(x, up_gate[e, 1])
+        copies[3 * e].wait()
+        copies[3 * e + 1].wait()
+        both = dot(x, gate_up[e])
+        gate, up = both[:, :hidden_units], both[:, hidden_units:]
         hidden = (gate / (1.0 + jnp.exp(-gate)) * up).astype(jnp.bfloat16)
-        copies[e][2].wait()
+        copies[3 * e + 2].wait()
         answer = dot(hidden, down[e]).astype(jnp.bfloat16)
         out[:, e * half : (e + 1) * half, :] = answer.reshape(out.shape[0], half, out.shape[2])
 
@@ -142,18 +143,25 @@
     slots = RING * micro * 2 * CAP
     spread, deliver = ring_groups("y"), ring_groups("z")
     whole = pl.BlockSpec(memory_space=pltpu.VMEM)
+    far = pl.BlockSpec(memory_space=pltpu.HBM)
     bf16 = jnp.bfloat16
 
-    own = [gate_weight[0, 0], up_weight[0, 0], down_weight[0, 0]]
-    swap = [(i, i ^ 1) for i in range(lax.axis_size("expert"))]
+    chips = [[i, i + 1] for i in range(0, lax.axis_size("expert"), 2)]
+    chip_weights = [
+        lax.all_gather(w[0], "expert", axis=0, tiled=True, axis_index_groups=chips)
+        for w in (gate_weight, up_weight, down_weight)
+    ]
     tokens = activations.reshape(held, width)
+    inputs = (tokens, norm_gain, expert_ids.reshape(held, -1), route_weights.reshape(held, -1))
     payload = kernel_call(
         payload_kernel,
         jax.ShapeDtypeStruct((RING, held, width + 128), bf16),
-        (tokens, norm_gain, expert_ids.reshape(held, -1), route_weights.reshape(held, -1)),
+        inputs,
+        specs=[far] * 4,
+        limit=60,
+        scratch=[pltpu.VMEM(a.shape, a.dtype) for a in inputs] + [pltpu.SemaphoreType.DMA((4,))],
     )
     gathered = exchange(payload, spread)
-    sibling = [lax.ppermute(w, "expert", swap) for w in own]
     place = lax.axis_index("expert").astype(jnp.int32).reshape(1)
     outgoing, blend = kernel_call(
         pack_kernel,
@@ -168,14 +176,14 @@
     answers = kernel_call(
         expert_kernel,
         jax.ShapeDtypeStruct((RING, slots, width), bf16),
-        (arrived, *own, *sibling),
-        specs=[whole] + [pl.BlockSpec(memory_space=pl.ANY)] * 6,
+        (arrived, *chip_weights),
+        specs=[whole] + [far] * 3,
         scratch=(
-            pltpu.VMEM((2, 2, width, hidden_units), bf16),
+            pltpu.VMEM((2, width, 2 * hidden_units), bf16),
             pltpu.VMEM((2, hidden_units, width), bf16),
             pltpu.SemaphoreType.DMA((2, 3)),
         ),
-        limit=36,
+        limit=58,
         flops=6 * RING * slots * width * hidden_units,
     )
     returned = exchange(answers, deliver)

time: 138 us -> 165 us (1.20)
  waiting for transfers between devices: 36.7 us -> 57 us
  local copies, waits for them, and re-layouts: 16.8 us -> 1.95 us
  between operations: 0.1 us -> 13.2 us
  blocking collectives: 48.3 us -> 56.4 us
  Pallas kernels: 7.83 us -> 14.4 us
  starting transfers between devices: 27.5 us -> 21.3 us
    all_gather x0 -> x3, waiting for transfers between devices: none -> 38.8 us  [on_device(): lax.all_gather(w[0], 'expert', axis=0, tiled=True, axis_index_groups=chips)]
    all_to_all x2, waiting for transfers between devices: 31.3 us -> 12.2 us  [exchange(): lax.all_to_all(chunks, 'expert', split_axis=0, concat_axis=0, tiled=True,...]
    unnamed x31 -> x5, local copies, waits for them, and re-layouts: 16.8 us -> 1.95 us
    all_to_all x2, blocking collectives: 48.3 us -> 56.4 us  [exchange(): lax.all_to_all(chunks, 'expert', split_axis=0, concat_axis=0, tiled=True,...]
    pallas_call x5, Pallas kernels: 7.83 us -> 14.4 us  [kernel_call(): pl.pallas_call(body, out_shape=out_shape, in_specs=specs or [whole] * len...]
    ppermute x3 -> x0, starting transfers between devices: 6.24 us -> none  [on_device(): sibling = [lax.ppermute(w, 'expert', swap) for w in own]]
    unnamed x0 -> x3, waiting for transfers between devices: none -> 2.09 us
  transfers between devices with their start and end apart: 6 -> 6, of which waited for: 5 -> 4; matrix products, arithmetic and copies ran while one was open for 0% -> 0% of each run, Pallas kernels for 0% -> 3%
where the time goes in v2:
time: 165 us; the launch traced here: 164 us
  waiting for transfers between devices  57 us (35%)
  blocking collectives  56.4 us (34%)
  starting transfers between devices  21.3 us (13%)
  Pallas kernels  14.4 us (9%)
  between operations  13.2 us (8%)
  local copies, waits for them, and re-layouts  1.95 us (1%)
    all_to_all x2, blocking collectives, exchange(): lax.all_to_all(chunks, 'expert', split_axis=0, concat_axis=0, tiled=True,...  56.4 us
    all_gather x3, waiting for transfers between devices, on_device(): lax.all_gather(w[0], 'expert', axis=0, tiled=True, axis_index_groups=chips)  38.8 us
    all_to_all x2, starting transfers between devices, exchange(): lax.all_to_all(chunks, 'expert', split_axis=0, concat_axis=0, tiled=True,...  17.8 us
    pallas_call x5, Pallas kernels, kernel_call(): pl.pallas_call(body, out_shape=out_shape, in_specs=specs or [whole] * len...  14.4 us
    all_to_all x2, waiting for transfers between devices, exchange(): lax.all_to_all(chunks, 'expert', split_axis=0, concat_axis=0, tiled=True,...  12.2 us
    ppermute x1, waiting for transfers between devices, on_device(): return lax.ppermute(layer_out, 'segment', route).reshape(activations.shape)  3.97 us
    ppermute x1, starting transfers between devices, on_device(): return lax.ppermute(layer_out, 'segment', route).reshape(activations.shape)  3.39 us
  transfers between devices with their start and end apart: 6, of which 4 were waited for; matrix products, arithmetic and copies ran while one was open for 0% of the time, Pallas kernels for 3%

profile of v2, /device:TPU:8, one launch (start us, length us, event | category | flops | bytes accessed | tf_op | source)
XLA Modules:
  0.0 164.3 jit_solution(10422930811162339259)
XLA Ops:
  6.5 0.0 all-gather.7.cloned.1.call-start
  6.5 0.7 all-gather.7.cloned.1.call-update
  7.3 0.0 all-gather.9.cloned.1.call-start
  7.3 0.7 all-gather.9.cloned.1.call-update
  8.0 1.8 %shard_map.73 = bf16[8,16,2176]{2,1,0:T(8,128)(2,1)} custom-call(bf16[16,2048]{1,0:T(8,128)(2,1)} %bitcast.8, f32[1,2048]{1,0:T(1,128)} %refs_1_.1, s32[16,8]{1,0:T(8,128)} %bitcast.14, f32[16,8]{1,0:T(8,128)} %bitcast.15), custom_call_target="tpu_custom_call" | custom-call | tf_op jit(solution)/shard_map/pallas_call | solution.py:126
  9.8 9.3 %all-to-all-start = ((bf16[8,16,2176]{2,1,0:T(8,128)(2,1)}), bf16[8,16,2176]{2,1,0:T(8,128)(2,1)S(1)}, u32[]{:S(2)}, u32[]{:S(2)}) async-start(bf16[8,16,2176]{2,1,0:T(8,128)(2,1)} %shard_map.73), calls=%async_computation | async-start | bytes 1114112 | tf_op jit(solution)/shard_map/all_to_all | solution.py:22
  19.1 12.2 %all-to-all-done.gathered = bf16[8,16,2176]{2,1,0:T(8,128)(2,1)S(1)} async-done(((bf16[8,16,2176]{2,1,0:T(8,128)(2,1)}), bf16[8,16,2176]{2,1,0:T(8,128)(2,1)S(1)}, u32[]{:S(2)}, u32[]{:S(2)}) %all-to-all-start) | async-done | bytes 557088 | tf_op jit(solution)/shard_map/all_to_all | solution.py:22
  31.3 2.3 %shard_map.74 = (bf16[8,64,2048]{2,1,0:T(8,128)(2,1)}, bf16[2,512,128]{2,1,0:T(8,128)(2,1)S(1)}) custom-call(s32[1]{0:T(128)} %bitcast.1.place, bf16[8,16,2176]{2,1,0:T(8,128)(2,1)S(1)} %all-to-all-done.gathered), custom_call_target="tpu_custom_call" | custom-call | tf_op jit(solution)/shard_map/pallas_call | solution.py:126
  33.6 8.6 %all-to-all-start.1 = ((bf16[8,64,2048]{2,1,0:T(8,128)(2,1)}), bf16[8,64,2048]{2,1,0:T(8,128)(2,1)S(1)}, u32[]{:S(2)}, u32[]{:S(2)}) async-start(bf16[8,64,2048]{2,1,0:T(8,128)(2,1)} %get-tuple-element.7), calls=%async_computation.1 | async-start | bytes 4194304 | tf_op jit(solution)/shard_map/all_to_all | solution.py:22
  42.2 0.0 all-gather.11.cloned.1.call-start
  42.2 0.7 all-gather.11.cloned.1.call-update
  42.9 0.0 all-gather.7.cloned.1.call-done
  42.9 15.0 %all-gather.9.cloned.1.call-done = bf16[2,1,2048,384]{3,2,1,0:T(8,128)(2,1)} async-done(((bf16[1,1,2048,384]{3,2,1,0:T(8,128)(2,1)}), bf16[2,1,2048,384]{3,2,1,0:T(8,128)(2,1)}) %all-gather.9.cloned.1.call-update) | async-done | bytes 3145744 | tf_op jit(solution)/shard_map/all_gather | solution.py:151
  58.0 23.7 %all-gather.11.cloned.1.call-done = bf16[2,1,384,2048]{3,2,1,0:T(8,128)(2,1)} async-done(((bf16[1,1,384,2048]{3,2,1,0:T(8,128)(2,1)}), bf16[2,1,384,2048]{3,2,1,0:T(8,128)(2,1)}) %all-gather.11.cloned.1.call-update) | async-done | bytes 3145744 | tf_op jit(solution)/shard_map/all_gather | solution.py:151
  81.7 0.0 all-to-all-done.1.rows
  81.7 0.0 copy-start.1
  81.7 1.3 copy-done.1
  83.0 9.5 %shard_map.75 = bf16[8,64,2048]{2,1,0:T(8,128)(2,1)} custom-call(bf16[8,64,2048]{2,1,0:T(8,128)(2,1)} %copy-done.1, bf16[2,2048,384]{2,1,0:T(8,128)(2,1)} %bitcast.10, bf16[2,2048,384]{2,1,0:T(8,128)(2,1)} %bitcast.11, bf16[2,384,2048]{2,1,0:T(8,128)(2,1)} %bitcast.12), custom_call_target="tpu_custom_call" | custom-call | flops 2415919104 | tf_op jit(solution)/shard_map/pallas_call | solution.py:126
  92.5 37.5 %all_to_all.20.returned = bf16[8,64,2048]{2,1,0:T(8,128)(2,1)S(1)} all-to-all(bf16[8,64,2048]{2,1,0:T(8,128)(2,1)} %shard_map.75), channel_id=1, replica_groups={{0,16,32,48,64,80,96,112},{2,18,34,50,66,82,98,114},{4,20,36,52,68,84,1..., dimensions={0} | all-to-all | bytes 4194304 | tf_op jit(solution)/shard_map/all_to_all | solution.py:22
  130.0 0.0 copy-start
  130.0 0.7 shard_map.76
  130.8 18.9 %all_to_all.21.pieces = bf16[8,16,2048]{2,1,0:T(8,128)(2,1)S(1)} all-to-all(bf16[8,16,2048]{2,1,0:T(8,128)(2,1)S(1)} %shard_map.76), channel_id=1, replica_groups={{0,2,4,6,8,10,12,14},{16,18,20,22,24,26,28,30},{32,34,36,38,40,42,44,46..., dimensions={0} | all-to-all | bytes 1048576 | tf_op jit(solution)/shard_map/all_to_all | solution.py:22
  149.7 0.0 copy-done
  149.7 0.1 shard_map.77
  149.8 3.4 %collective-permute-start = (bf16[16,2048]{1,0:T(8,128)(2,1)S(1)}, bf16[16,2048]{1,0:T(8,128)(2,1)S(1)}, u32[]{:S(2)}, u32[]{:S(2)}) collective-permute-start(bf16[16,2048]{1,0:T(8,128)(2,1)S(1)} %shard_map.77), channel_id=1, source_target_pairs={{0,128},{128,256},{256,384},{384,0},{1,129},{129,257},{257,385},{3... | collective-permute-start | bytes 196616 | tf_op jit(solution)/shard_map/ppermute | solution.py:199
  153.2 4.0 %collective-permute-done = bf16[16,2048]{1,0:T(8,128)(2,1)S(1)} collective-permute-done((bf16[16,2048]{1,0:T(8,128)(2,1)S(1)}, bf16[16,2048]{1,0:T(8,128)(2,1)S(1)}, u32[]{:S(2)}, u32[]{:S(2)}) %collective-permute-start) | collective-permute-done | bytes 65568 | tf_op jit(solution)/shard_map/ppermute | solution.py:199
  157.1 0.6 copy.22
Async XLA Ops:
  6.5 36.4 %all-gather.7.cloned.1.call-start = ((), (), s32[]{:S(2)}) async-start(), calls=%async_computation.4 | async-start | bytes 4718592 | tf_op jit(solution)/shard_map/all_gather | solution.py:151
  7.3 50.7 %all-gather.9.cloned.1.call-start = ((), (), s32[]{:S(2)}) async-start(), calls=%async_computation.5 | async-start | bytes 4718592 | tf_op jit(solution)/shard_map/all_gather | solution.py:151
  9.8 21.5 %all-to-all-start = ((bf16[8,16,2176]{2,1,0:T(8,128)(2,1)}), bf16[8,16,2176]{2,1,0:T(8,128)(2,1)S(1)}, u32[]{:S(2)}, u32[]{:S(2)}) async-start(bf16[8,16,2176]{2,1,0:T(8,128)(2,1)} %shard_map.73), calls=%async_computation | async-start | bytes 1114112 | tf_op jit(solution)/shard_map/all_to_all | solution.py:22
  33.6 48.1 %all-to-all-start.1 = ((bf16[8,64,2048]{2,1,0:T(8,128)(2,1)}), bf16[8,64,2048]{2,1,0:T(8,128)(2,1)S(1)}, u32[]{:S(2)}, u32[]{:S(2)}) async-start(bf16[8,64,2048]{2,1,0:T(8,128)(2,1)} %get-tuple-element.7), calls=%async_computation.1 | async-start | bytes 4194304 | tf_op jit(solution)/shard_map/all_to_all | solution.py:22
  42.2 39.5 %all-gather.11.cloned.1.call-start = ((), (), s32[]{:S(2)}) async-start(), calls=%async_computation.6 | async-start | bytes 4718592 | tf_op jit(solution)/shard_map/all_gather | solution.py:151
  81.7 1.3 copy-start.1
  130.0 19.6 %copy-start = (bf16[1,2,8,2048]{3,2,1,0:T(8,128)(2,1)S(1)}, bf16[1,2,8,2048]{3,2,1,0:T(8,128)(2,1)}, u32[]{:S(2)}) copy-start(bf16[1,2,8,2048]{3,2,1,0:T(8,128)(2,1)} %param.7) | copy-start | bytes 196612
  149.8 7.4 %collective-permute-start = (bf16[16,2048]{1,0:T(8,128)(2,1)S(1)}, bf16[16,2048]{1,0:T(8,128)(2,1)S(1)}, u32[]{:S(2)}, u32[]{:S(2)}) collective-permute-start(bf16[16,2048]{1,0:T(8,128)(2,1)S(1)} %shard_map.77), channel_id=1, source_target_pairs={{0,128},{128,256},{256,384},{384,0},{1,129},{129,257},{257,385},{3... | collective-permute-start | bytes 196616 | tf_op jit(solution)/shard_map/ppermute | solution.py:199
Sparse Core Ops, SparseCore 0:
  9.4 24.8 all-gather.6
  36.4 21.5 all-gather.8
  60.1 21.5 all-gather.10

commit v3 on v2

--- a/solution.py
+++ b/solution.py
@@ -53,7 +53,8 @@
         out[i, :, width:] = parts
 
 
-def pack_kernel(place, gathered, out, blend):
+def pack_kernel(place, gathered, *refs):
+    out, blend = refs[-2:]
     tokens = gathered.shape[0] * gathered.shape[1]
     width = out.shape[2]
     slots = out.shape[0] * out.shape[1]
@@ -62,9 +63,9 @@
     shape = (slots, 128)
     row = lax.broadcasted_iota(jnp.int32, shape, 0)
     lane = lax.broadcasted_iota(jnp.int32, shape, 1)
-    member, which, block, rank = row >> 6, (row >> 5) & 1, (row >> 1) & 15, row & 1
+    member, other, block, rank = row >> 6, (row >> 5) & 1, (row >> 1) & 15, row & 1
     chip = jnp.where(core == 0, (member & 3) * RING + y, (z % 4) * RING + member)
-    expert = chip * 2 + which
+    expert = chip * 2 + (other ^ core)
     parts = gathered[:, :, width:].reshape(tokens, 128)
     pick_high = (lane == expert).astype(jnp.bfloat16)
     pick_low = (lane == expert + 64).astype(jnp.bfloat16)
@@ -84,27 +85,14 @@
 
 
 def expert_kernel(rows, *refs):
-    gate_ref, up_ref, down_ref, out, gate_up, down, sems = refs
-    hidden_units = down.shape[1]
+    weights, out = refs[:6], refs[6]
     half = rows.shape[1] // 2
-    copies = []
     for e in range(2):
-        copies += [
-            pltpu.make_async_copy(gate_ref.at[e], gate_up.at[e, :, :hidden_units], sems.at[e, 0]),
-            pltpu.make_async_copy(up_ref.at[e], gate_up.at[e, :, hidden_units:], sems.at[e, 1]),
-            pltpu.make_async_copy(down_ref.at[e], down.at[e], sems.at[e, 2]),
-        ]
-    for copy in copies:
-        copy.start()
-    for e in range(2):
+        gate_ref, up_ref, down_ref = weights[3 * e : 3 * e + 3]
         x = rows[:, e * half : (e + 1) * half, :].reshape(-1, rows.shape[2])
-        copies[3 * e].wait()
-        copies[3 * e + 1].wait()
-        both = dot(x, gate_up[e])
-        gate, up = both[:, :hidden_units], both[:, hidden_units:]
+        gate, up = dot(x, gate_ref[...]), dot(x, up_ref[...])
         hidden = (gate / (1.0 + jnp.exp(-gate)) * up).astype(jnp.bfloat16)
-        copies[3 * e + 2].wait()
-        answer = dot(hidden, down[e]).astype(jnp.bfloat16)
+        answer = dot(hidden, down_ref[...]).astype(jnp.bfloat16)
         out[:, e * half : (e + 1) * half, :] = answer.reshape(out.shape[0], half, out.shape[2])
 
 
@@ -146,11 +134,9 @@
     far = pl.BlockSpec(memory_space=pltpu.HBM)
     bf16 = jnp.bfloat16
 
-    chips = [[i, i + 1] for i in range(0, lax.axis_size("expert"), 2)]
-    chip_weights = [
-        lax.all_gather(w[0], "expert", axis=0, tiled=True, axis_index_groups=chips)
-        for w in (gate_weight, up_weight, down_weight)
-    ]
+    own = [gate_weight[0, 0], up_weight[0, 0], down_weight[0, 0]]
+    swap = [(i, i ^ 1) for i in range(lax.axis_size("expert"))]
+    sibling = [lax.ppermute(w, "expert", swap) for w in own]
     tokens = activations.reshape(held, width)
     inputs = (tokens, norm_gain, expert_ids.reshape(held, -1), route_weights.reshape(held, -1))
     payload = kernel_call(
@@ -169,21 +155,14 @@
             jax.ShapeDtypeStruct((RING, slots, width), bf16),
             jax.ShapeDtypeStruct((2, RING * slots, RING * held), bf16),
         ),
-        (place, gathered),
-        specs=[pl.BlockSpec(memory_space=pltpu.SMEM), whole],
+        (place, gathered, *sibling),
+        specs=[pl.BlockSpec(memory_space=pltpu.SMEM), whole] + [far] * 3,
     )
     arrived = exchange(outgoing, deliver)
     answers = kernel_call(
         expert_kernel,
         jax.ShapeDtypeStruct((RING, slots, width), bf16),
-        (arrived, *chip_weights),
-        specs=[whole] + [far] * 3,
-        scratch=(
-            pltpu.VMEM((2, width, 2 * hidden_units), bf16),
-            pltpu.VMEM((2, hidden_units, width), bf16),
-            pltpu.SemaphoreType.DMA((2, 3)),
-        ),
-        limit=58,
+        (arrived, *[pltpu.with_memory_space_constraint(w, pltpu.VMEM) for w in own + sibling]),
         flops=6 * RING * slots * width * hidden_units,
     )
     returned = exchange(answers, deliver)

time: 165 us -> 133 us (0.81)
  waiting for transfers between devices: 57 us -> 16.3 us
  blocking collectives: 56.4 us -> 86.4 us
  between operations: 13.2 us -> 0.1 us
  Pallas kernels: 14.4 us -> 9.79 us
  starting transfers between devices: 21.3 us -> 19.6 us
    all_gather x3 -> x0, waiting for transfers between devices: 38.8 us -> none  [on_device(): lax.all_gather(w[0], 'expert', axis=0, tiled=True, axis_index_groups=chips)]
    all_to_all x2 -> x3, blocking collectives: 56.4 us -> 86.4 us  [exchange(): lax.all_to_all(chunks, 'expert', split_axis=0, concat_axis=0, tiled=True,...]
    all_to_all x2 -> x1, starting transfers between devices: 17.8 us -> 9.91 us  [exchange(): lax.all_to_all(chunks, 'expert', split_axis=0, concat_axis=0, tiled=True,...]
    ppermute x0 -> x3, starting transfers between devices: none -> 6.24 us  [on_device(): sibling = [lax.ppermute(w, 'expert', swap) for w in own]]
    pallas_call x5, Pallas kernels: 14.4 us -> 9.79 us  [kernel_call(): pl.pallas_call(body, out_shape=out_shape, in_specs=specs or [whole] * len...]
    unnamed x3 -> x0, waiting for transfers between devices: 2.09 us -> none
    all_to_all x2 -> x1, waiting for transfers between devices: 12.2 us -> 12.3 us  [exchange(): lax.all_to_all(chunks, 'expert', split_axis=0, concat_axis=0, tiled=True,...]
  transfers between devices with their start and end apart: 6 -> 5, of which waited for: 4 -> 2; matrix products, arithmetic and copies ran while one was open for 0% -> 0% of each run, Pallas kernels for 3% -> 1%
where the time goes in v3:
time: 133 us
  blocking collectives  86.4 us (65%)
  starting transfers between devices  19.6 us (15%)
  waiting for transfers between devices  16.3 us (12%)
  Pallas kernels  9.79 us (7%)
    all_to_all x3, blocking collectives, exchange(): lax.all_to_all(chunks, 'expert', split_axis=0, concat_axis=0, tiled=True,...  86.4 us
    all_to_all x1, waiting for transfers between devices, exchange(): lax.all_to_all(chunks, 'expert', split_axis=0, concat_axis=0, tiled=True,...  12.3 us
    all_to_all x1, starting transfers between devices, exchange(): lax.all_to_all(chunks, 'expert', split_axis=0, concat_axis=0, tiled=True,...  9.91 us
    pallas_call x5, Pallas kernels, kernel_call(): pl.pallas_call(body, out_shape=out_shape, in_specs=specs or [whole] * len...  9.79 us
    ppermute x3, starting transfers between devices, on_device(): sibling = [lax.ppermute(w, 'expert', swap) for w in own]  6.24 us
    ppermute x1, waiting for transfers between devices, on_device(): return lax.ppermute(layer_out, 'segment', route).reshape(activations.shape)  3.96 us
    ppermute x1, starting transfers between devices, on_device(): return lax.ppermute(layer_out, 'segment', route).reshape(activations.shape)  3.4 us
  transfers between devices with their start and end apart: 5, of which 2 were waited for; matrix products, arithmetic and copies ran while one was open for 0% of the time, Pallas kernels for 1%

profile of v3, /device:TPU:8, one launch (start us, length us, event | category | flops | bytes accessed | tf_op | source)
XLA Modules:
  0.0 132.8 jit_solution(17607028092728698520)
XLA Ops:
  0.0 1.9 %collective-permute-start = (bf16[2048,384]{1,0:T(8,128)(2,1)}, bf16[2048,384]{1,0:T(8,128)(2,1)S(1)}, u32[]{:S(2)}, u32[]{:S(2)}) collective-permute-start(bf16[2048,384]{1,0:T(8,128)(2,1)} %bitcast.8), channel_id=1, source_target_pairs={{0,1},{1,0},{2,3},{3,2},{4,5},{5,4},{6,7},{7,6},{8,9},{9,8},{10,11... | collective-permute-start | bytes 4718600 | tf_op jit(solution)/shard_map/ppermute | solution.py:139
  1.9 2.4 %collective-permute-start.1 = (bf16[2048,384]{1,0:T(8,128)(2,1)}, bf16[2048,384]{1,0:T(8,128)(2,1)S(1)}, u32[]{:S(2)}, u32[]{:S(2)}) collective-permute-start(bf16[2048,384]{1,0:T(8,128)(2,1)} %bitcast.10), channel_id=1, source_target_pairs={{0,1},{1,0},{2,3},{3,2},{4,5},{5,4},{6,7},{7,6},{8,9},{9,8},{10,11... | collective-permute-start | bytes 4718600 | tf_op jit(solution)/shard_map/ppermute | solution.py:139
  4.3 1.9 %collective-permute-start.2 = (bf16[384,2048]{1,0:T(8,128)(2,1)}, bf16[384,2048]{1,0:T(8,128)(2,1)}, u32[]{:S(2)}, u32[]{:S(2)}) collective-permute-start(bf16[384,2048]{1,0:T(8,128)(2,1)} %bitcast.12), channel_id=1, source_target_pairs={{0,1},{1,0},{2,3},{3,2},{4,5},{5,4},{6,7},{7,6},{8,9},{9,8},{10,11... | collective-permute-start | bytes 4718600 | tf_op jit(solution)/shard_map/ppermute | solution.py:139
  6.3 1.8 %shard_map.73 = bf16[8,16,2176]{2,1,0:T(8,128)(2,1)} custom-call(bf16[16,2048]{1,0:T(8,128)(2,1)} %bitcast.14, f32[1,2048]{1,0:T(1,128)} %refs_1_.1, s32[16,8]{1,0:T(8,128)} %bitcast.17, f32[16,8]{1,0:T(8,128)} %bitcast.18), custom_call_target="tpu_custom_call" | custom-call | tf_op jit(solution)/shard_map/pallas_call | solution.py:114
  8.1 9.9 %all-to-all-start = ((bf16[8,16,2176]{2,1,0:T(8,128)(2,1)}), bf16[8,16,2176]{2,1,0:T(8,128)(2,1)}, u32[]{:S(2)}, u32[]{:S(2)}) async-start(bf16[8,16,2176]{2,1,0:T(8,128)(2,1)} %shard_map.73), calls=%async_computation | async-start | bytes 1114112 | tf_op jit(solution)/shard_map/all_to_all | solution.py:22
  18.0 12.3 %all-to-all-done.gathered = bf16[8,16,2176]{2,1,0:T(8,128)(2,1)} async-done(((bf16[8,16,2176]{2,1,0:T(8,128)(2,1)}), bf16[8,16,2176]{2,1,0:T(8,128)(2,1)}, u32[]{:S(2)}, u32[]{:S(2)}) %all-to-all-start) | async-done | bytes 557088 | tf_op jit(solution)/shard_map/all_to_all | solution.py:22
  30.3 0.0 collective-permute-done.refs_0_.refs_3_
  30.3 0.0 collective-permute-done.1.refs_1_.refs_4_
  30.3 0.0 collective-permute-done.2.refs_2_.refs_5_
  30.4 0.0 copy-start.2
  30.4 2.1 %shard_map.74 = (bf16[8,64,2048]{2,1,0:T(8,128)(2,1)S(1)}, bf16[2,512,128]{2,1,0:T(8,128)(2,1)S(1)}) custom-call(s32[1]{0:T(128)} %bitcast.1.place, bf16[8,16,2176]{2,1,0:T(8,128)(2,1)} %all-to-all-done.gathered, bf16[2048,384]{1,0:T(8,128)(2,1)S(1)} %collective-permute-done.refs_0_.refs_3_, bf16[2048,384]{1,0:T(8,128)(2,1)S(1)} %collective-permute-done.1.refs_1_.refs_4_, ...), custom_call_target="tpu_custom_call" | custom-call | tf_op jit(solution)/shard_map/pallas_call | solution.py:114
  32.5 0.0 copy-start
  32.5 0.0 copy-start.1
  32.5 38.1 %all_to_all.20.rows = bf16[8,64,2048]{2,1,0:T(8,128)(2,1)S(1)} all-to-all(bf16[8,64,2048]{2,1,0:T(8,128)(2,1)S(1)} %get-tuple-element.7), channel_id=1, replica_groups={{0,16,32,48,64,80,96,112},{2,18,34,50,66,82,98,114},{4,20,36,52,68,84,1..., dimensions={0} | all-to-all | bytes 4194304 | tf_op jit(solution)/shard_map/all_to_all | solution.py:22
  70.7 0.0 copy-done.2
  70.7 0.0 copy-done
  70.7 0.0 copy-done.1
  70.7 5.0 %shard_map.75 = bf16[8,64,2048]{2,1,0:T(8,128)(2,1)S(1)} custom-call(bf16[8,64,2048]{2,1,0:T(8,128)(2,1)S(1)} %all_to_all.20.rows, bf16[2048,384]{1,0:T(8,128)(2,1)S(1)} %bitcast.9, bf16[2048,384]{1,0:T(8,128)(2,1)S(1)} %bitcast.11, bf16[384,2048]{1,0:T(8,128)(2,1)S(1)} %bitcast.13, bf16[2048,384]{1,0:T(8,128)(2,1)S(1)} %collective-permute-done.refs_0_.refs_3_, ...), custom_call_target="tpu_custom_call" | custom-call | flops 2415919104 | tf_op jit(solution)/shard_map/pallas_call | solution.py:114
  75.7 32.6 %all_to_all.21.returned = bf16[8,64,2048]{2,1,0:T(8,128)(2,1)S(1)} all-to-all(bf16[8,64,2048]{2,1,0:T(8,128)(2,1)S(1)} %shard_map.75), channel_id=1, replica_groups={{0,16,32,48,64,80,96,112},{2,18,34,50,66,82,98,114},{4,20,36,52,68,84,1..., dimensions={0} | all-to-all | bytes 4194304 | tf_op jit(solution)/shard_map/all_to_all | solution.py:22
  108.3 0.0 copy-start.3
  108.3 0.7 shard_map.76
  109.0 15.7 %all_to_all.22.pieces = bf16[8,16,2048]{2,1,0:T(8,128)(2,1)S(1)} all-to-all(bf16[8,16,2048]{2,1,0:T(8,128)(2,1)S(1)} %shard_map.76), channel_id=1, replica_groups={{0,2,4,6,8,10,12,14},{16,18,20,22,24,26,28,30},{32,34,36,38,40,42,44,46..., dimensions={0} | all-to-all | bytes 1048576 | tf_op jit(solution)/shard_map/all_to_all | solution.py:22
  124.7 0.0 copy-done.3
  124.7 0.1 shard_map.77
  124.8 3.4 %collective-permute-start.3 = (bf16[16,2048]{1,0:T(8,128)(2,1)S(1)}, bf16[16,2048]{1,0:T(8,128)(2,1)S(1)}, u32[]{:S(2)}, u32[]{:S(2)}) collective-permute-start(bf16[16,2048]{1,0:T(8,128)(2,1)S(1)} %shard_map.77), channel_id=1, source_target_pairs={{0,128},{128,256},{256,384},{384,0},{1,129},{129,257},{257,385},{3... | collective-permute-start | bytes 196616 | tf_op jit(solution)/shard_map/ppermute | solution.py:178
  128.2 4.0 %collective-permute-done.3 = bf16[16,2048]{1,0:T(8,128)(2,1)S(1)} collective-permute-done((bf16[16,2048]{1,0:T(8,128)(2,1)S(1)}, bf16[16,2048]{1,0:T(8,128)(2,1)S(1)}, u32[]{:S(2)}, u32[]{:S(2)}) %collective-permute-start.3) | collective-permute-done | bytes 65568 | tf_op jit(solution)/shard_map/ppermute | solution.py:178
  132.2 0.6 copy.15
Async XLA Ops:
  0.0 30.3 %collective-permute-start = (bf16[2048,384]{1,0:T(8,128)(2,1)}, bf16[2048,384]{1,0:T(8,128)(2,1)S(1)}, u32[]{:S(2)}, u32[]{:S(2)}) collective-permute-start(bf16[2048,384]{1,0:T(8,128)(2,1)} %bitcast.8), channel_id=1, source_target_pairs={{0,1},{1,0},{2,3},{3,2},{4,5},{5,4},{6,7},{7,6},{8,9},{9,8},{10,11... | collective-permute-start | bytes 4718600 | tf_op jit(solution)/shard_map/ppermute | solution.py:139
  1.9 28.4 %collective-permute-start.1 = (bf16[2048,384]{1,0:T(8,128)(2,1)}, bf16[2048,384]{1,0:T(8,128)(2,1)S(1)}, u32[]{:S(2)}, u32[]{:S(2)}) collective-permute-start(bf16[2048,384]{1,0:T(8,128)(2,1)} %bitcast.10), channel_id=1, source_target_pairs={{0,1},{1,0},{2,3},{3,2},{4,5},{5,4},{6,7},{7,6},{8,9},{9,8},{10,11... | collective-permute-start | bytes 4718600 | tf_op jit(solution)/shard_map/ppermute | solution.py:139
  4.3 26.0 %collective-permute-start.2 = (bf16[384,2048]{1,0:T(8,128)(2,1)}, bf16[384,2048]{1,0:T(8,128)(2,1)}, u32[]{:S(2)}, u32[]{:S(2)}) collective-permute-start(bf16[384,2048]{1,0:T(8,128)(2,1)} %bitcast.12), channel_id=1, source_target_pairs={{0,1},{1,0},{2,3},{3,2},{4,5},{5,4},{6,7},{7,6},{8,9},{9,8},{10,11... | collective-permute-start | bytes 4718600 | tf_op jit(solution)/shard_map/ppermute | solution.py:139
  8.1 22.2 %all-to-all-start = ((bf16[8,16,2176]{2,1,0:T(8,128)(2,1)}), bf16[8,16,2176]{2,1,0:T(8,128)(2,1)}, u32[]{:S(2)}, u32[]{:S(2)}) async-start(bf16[8,16,2176]{2,1,0:T(8,128)(2,1)} %shard_map.73), calls=%async_computation | async-start | bytes 1114112 | tf_op jit(solution)/shard_map/all_to_all | solution.py:22
  30.4 40.3 %copy-start.2 = (bf16[1,1,384,2048]{3,2,1,0:T(8,128)(2,1)S(1)}, bf16[1,1,384,2048]{3,2,1,0:T(8,128)(2,1)}, u32[]{:S(2)}) copy-start(bf16[1,1,384,2048]{3,2,1,0:T(8,128)(2,1)} %param.11) | copy-start | bytes 4718596
  32.5 38.2 %copy-start = (bf16[1,1,2048,384]{3,2,1,0:T(8,128)(2,1)S(1)}, bf16[1,1,2048,384]{3,2,1,0:T(8,128)(2,1)}, u32[]{:S(2)}) copy-start(bf16[1,1,2048,384]{3,2,1,0:T(8,128)(2,1)} %param.9) | copy-start | bytes 4718596
  32.5 38.2 %copy-start.1 = (bf16[1,1,2048,384]{3,2,1,0:T(8,128)(2,1)S(1)}, bf16[1,1,2048,384]{3,2,1,0:T(8,128)(2,1)}, u32[]{:S(2)}) copy-start(bf16[1,1,2048,384]{3,2,1,0:T(8,128)(2,1)} %param.10) | copy-start | bytes 4718596
  108.3 16.5 %copy-start.3 = (bf16[1,2,8,2048]{3,2,1,0:T(8,128)(2,1)S(1)}, bf16[1,2,8,2048]{3,2,1,0:T(8,128)(2,1)}, u32[]{:S(2)}) copy-start(bf16[1,2,8,2048]{3,2,1,0:T(8,128)(2,1)} %param.7) | copy-start | bytes 196612
  124.8 7.4 %collective-permute-start.3 = (bf16[16,2048]{1,0:T(8,128)(2,1)S(1)}, bf16[16,2048]{1,0:T(8,128)(2,1)S(1)}, u32[]{:S(2)}, u32[]{:S(2)}) collective-permute-start(bf16[16,2048]{1,0:T(8,128)(2,1)S(1)} %shard_map.77), channel_id=1, source_target_pairs={{0,128},{128,256},{256,384},{384,0},{1,129},{129,257},{257,385},{3... | collective-permute-start | bytes 196616 | tf_op jit(solution)/shard_map/ppermute | solution.py:178

commit v4 on v2

--- a/solution.py
+++ b/solution.py
@@ -29,8 +29,8 @@
 
 
 def payload_kernel(*refs):
-    out, (tokens, gain, ids, route, sems) = refs[4], refs[5:]
-    copies = [pltpu.make_async_copy(refs[i], refs[5 + i], sems.at[i]) for i in range(4)]
+    out, (tokens, gain, ids, route, chunk, in_sems, out_sems) = refs[4], refs[5:]
+    copies = [pltpu.make_async_copy(refs[i], refs[5 + i], in_sems.at[i]) for i in range(4)]
     for copy in copies:
         copy.start()
     for copy in copies:
@@ -38,22 +38,22 @@
     width = tokens.shape[1]
     rows = tokens[...].astype(jnp.float32)
     inv_scale = lax.rsqrt(jnp.mean(rows * rows, axis=-1, keepdims=True) + norm_eps)
-    normed = (rows * inv_scale * gain[...]).astype(jnp.bfloat16)
+    chunk[:, :width] = (rows * inv_scale * gain[...]).astype(jnp.bfloat16)
     id_rows, weight_rows = ids[...], route[...]
     lane = lax.broadcasted_iota(jnp.int32, (rows.shape[0], 128), 1)
     dense = jnp.zeros((rows.shape[0], 128), jnp.float32)
     for k in range(id_rows.shape[1]):
         dense += jnp.where(lane % 64 == id_rows[:, k : k + 1], weight_rows[:, k : k + 1], 0.0)
-    high = dense.astype(jnp.bfloat16)
-    low = (dense - high.astype(jnp.float32)).astype(jnp.bfloat16)
-    parts = jnp.where(lane < 64, high.astype(jnp.float32), low.astype(jnp.float32))
-    parts = parts.astype(jnp.bfloat16)
-    for i in range(RING):
-        out[i, :, :width] = normed
-        out[i, :, width:] = parts
-
-
-def pack_kernel(place, gathered, out, blend):
+    high = dense.astype(jnp.bfloat16).astype(jnp.float32)
+    chunk[:, width:] = jnp.where(lane < 64, high, dense - high).astype(jnp.bfloat16)
+    copies = [pltpu.make_async_copy(chunk, out.at[i], out_sems.at[i]) for i in range(RING)]
+    for copy in copies:
+        copy.start()
+    for copy in copies:
+        copy.wait()
+
+
+def pack_kernel(place, gathered, out, blend, held, sems):
     tokens = gathered.shape[0] * gathered.shape[1]
     width = out.shape[2]
     slots = out.shape[0] * out.shape[1]
@@ -62,9 +62,9 @@
     shape = (slots, 128)
     row = lax.broadcasted_iota(jnp.int32, shape, 0)
     lane = lax.broadcasted_iota(jnp.int32, shape, 1)
-    member, which, block, rank = row >> 6, (row >> 5) & 1, (row >> 1) & 15, row & 1
+    member, other, block, rank = row >> 6, (row >> 5) & 1, (row >> 1) & 15, row & 1
     chip = jnp.where(core == 0, (member & 3) * RING + y, (z % 4) * RING + member)
-    expert = chip * 2 + which
+    expert = chip * 2 + (other ^ core)
     parts = gathered[:, :, width:].reshape(tokens, 128)
     pick_high = (lane == expert).astype(jnp.bfloat16)
     pick_low = (lane == expert + 64).astype(jnp.bfloat16)
@@ -80,19 +80,28 @@
     blend[0] = (pick * high).astype(jnp.bfloat16)
     blend[1] = (pick * low).astype(jnp.bfloat16)
     rows = gathered[:, :, :width].reshape(tokens, width)
-    out[...] = dot(pick.astype(jnp.bfloat16), rows).astype(jnp.bfloat16).reshape(out.shape)
+    pick = pick.astype(jnp.bfloat16)
+    size = out.shape[1]
+    copies = [pltpu.make_async_copy(held.at[i], out.at[i], sems.at[i]) for i in range(RING)]
+    for i in range(RING):
+        held[i] = dot(pick[i * size : (i + 1) * size], rows).astype(jnp.bfloat16)
+        copies[i].start()
+    for copy in copies:
+        copy.wait()
 
 
 def expert_kernel(rows, *refs):
-    gate_ref, up_ref, down_ref, out, gate_up, down, sems = refs
+    weights, out = refs[:6], refs[6]
+    gate_up, down, sems = refs[7:]
     hidden_units = down.shape[1]
     half = rows.shape[1] // 2
     copies = []
     for e in range(2):
+        gate_ref, up_ref, down_ref = weights[3 * e : 3 * e + 3]
         copies += [
-            pltpu.make_async_copy(gate_ref.at[e], gate_up.at[e, :, :hidden_units], sems.at[e, 0]),
-            pltpu.make_async_copy(up_ref.at[e], gate_up.at[e, :, hidden_units:], sems.at[e, 1]),
-            pltpu.make_async_copy(down_ref.at[e], down.at[e], sems.at[e, 2]),
+            pltpu.make_async_copy(gate_ref, gate_up.at[e, :, :hidden_units], sems.at[e, 0]),
+            pltpu.make_async_copy(up_ref, gate_up.at[e, :, hidden_units:], sems.at[e, 1]),
+            pltpu.make_async_copy(down_ref, down.at[e], sems.at[e, 2]),
         ]
     for copy in copies:
         copy.start()
@@ -121,13 +130,15 @@
     out[...] = total.astype(jnp.bfloat16)
 
 
-def kernel_call(body, out_shape, operands, specs=None, scratch=(), limit=24, flops=0, moved=0):
+def kernel_call(
+    body, out_shape, operands, specs=None, out_specs=None, scratch=(), limit=24, flops=0, moved=0
+):
     whole = pl.BlockSpec(memory_space=pltpu.VMEM)
     return pl.pallas_call(
         body,
         out_shape=out_shape,
         in_specs=specs or [whole] * len(operands),
-        out_specs=jax.tree.map(lambda _: whole, out_shape),
+        out_specs=out_specs or whole,
         scratch_shapes=scratch,
         compiler_params=pltpu.CompilerParams(vmem_limit_bytes=limit * MIB),
         cost_estimate=pl.CostEstimate(flops=flops, bytes_accessed=moved, transcendentals=0),
@@ -146,44 +157,49 @@
     far = pl.BlockSpec(memory_space=pltpu.HBM)
     bf16 = jnp.bfloat16
 
-    chips = [[i, i + 1] for i in range(0, lax.axis_size("expert"), 2)]
-    chip_weights = [
-        lax.all_gather(w[0], "expert", axis=0, tiled=True, axis_index_groups=chips)
-        for w in (gate_weight, up_weight, down_weight)
-    ]
+    own = [gate_weight[0, 0], up_weight[0, 0], down_weight[0, 0]]
+    swap = [(i, i ^ 1) for i in range(lax.axis_size("expert"))]
+    sibling = [lax.ppermute(w, "expert", swap) for w in own]
     tokens = activations.reshape(held, width)
     inputs = (tokens, norm_gain, expert_ids.reshape(held, -1), route_weights.reshape(held, -1))
     payload = kernel_call(
         payload_kernel,
-        jax.ShapeDtypeStruct((RING, held, width + 128), bf16),
-        inputs,
+        pltpu.HBM((RING, held, width + 128), bf16),
+        [pltpu.with_memory_space_constraint(a, pltpu.HBM) for a in inputs],
         specs=[far] * 4,
-        limit=60,
-        scratch=[pltpu.VMEM(a.shape, a.dtype) for a in inputs] + [pltpu.SemaphoreType.DMA((4,))],
+        out_specs=far,
+        scratch=[pltpu.VMEM(a.shape, a.dtype) for a in inputs]
+        + [
+            pltpu.VMEM((held, width + 128), bf16),
+            pltpu.SemaphoreType.DMA((4,)),
+            pltpu.SemaphoreType.DMA((RING,)),
+        ],
     )
     gathered = exchange(payload, spread)
     place = lax.axis_index("expert").astype(jnp.int32).reshape(1)
     outgoing, blend = kernel_call(
         pack_kernel,
         (
-            jax.ShapeDtypeStruct((RING, slots, width), bf16),
+            pltpu.HBM((RING, slots, width), bf16),
             jax.ShapeDtypeStruct((2, RING * slots, RING * held), bf16),
         ),
         (place, gathered),
         specs=[pl.BlockSpec(memory_space=pltpu.SMEM), whole],
+        out_specs=(far, whole),
+        scratch=[pltpu.VMEM((RING, slots, width), bf16), pltpu.SemaphoreType.DMA((RING,))],
     )
     arrived = exchange(outgoing, deliver)
     answers = kernel_call(
         expert_kernel,
         jax.ShapeDtypeStruct((RING, slots, width), bf16),
-        (arrived, *chip_weights),
-        specs=[whole] + [far] * 3,
+        (arrived, *[pltpu.with_memory_space_constraint(w, pltpu.HBM) for w in own + sibling]),
+        specs=[whole] + [far] * 6,
         scratch=(
             pltpu.VMEM((2, width, 2 * hidden_units), bf16),
             pltpu.VMEM((2, hidden_units, width), bf16),
             pltpu.SemaphoreType.DMA((2, 3)),
         ),
-        limit=58,
+        limit=32,
         flops=6 * RING * slots * width * hidden_units,
     )
     returned = exchange(answers, deliver)

time: 165 us -> 128 us (0.78)
  waiting for transfers between devices: 57 us -> 39 us
  between operations: 13.2 us -> 0.09 us
  blocking collectives: 56.4 us -> 48.3 us
  starting transfers between devices: 21.3 us -> 27.5 us
  Pallas kernels: 14.4 us -> 11.1 us
    all_gather x3 -> x0, waiting for transfers between devices: 38.8 us -> none  [on_device(): lax.all_gather(w[0], 'expert', axis=0, tiled=True, axis_index_groups=chips)]
    all_to_all x2, waiting for transfers between devices: 12.2 us -> 32.4 us  [exchange(): lax.all_to_all(chunks, 'expert', split_axis=0, concat_axis=0, tiled=True,...]
    all_to_all x2, blocking collectives: 56.4 us -> 48.3 us  [exchange(): lax.all_to_all(chunks, 'expert', split_axis=0, concat_axis=0, tiled=True,...]
    ppermute x0 -> x3, starting transfers between devices: none -> 6.24 us  [on_device(): sibling = [lax.ppermute(w, 'expert', swap) for w in own]]
    pallas_call x5, Pallas kernels: 14.4 us -> 11.1 us  [kernel_call(): pl.pallas_call(body, out_shape=out_shape, in_specs=specs or [whole] * len...]
    ppermute x0 -> x3, waiting for transfers between devices: none -> 2.7 us  [on_device(): sibling = [lax.ppermute(w, 'expert', swap) for w in own]]
    unnamed x3 -> x0, waiting for transfers between devices: 2.09 us -> none
  transfers between devices with their start and end apart: 6 -> 6, of which waited for: 4 -> 5; matrix products, arithmetic and copies ran while one was open for 0% -> 0% of each run, Pallas kernels for 3% -> 0%
where the time goes in v4:
time: 128 us
  blocking collectives  48.3 us (38%)
  waiting for transfers between devices  39 us (30%)
  starting transfers between devices  27.5 us (21%)
  Pallas kernels  11.1 us (9%)
  local copies, waits for them, and re-layouts  1.78 us (1%)
    all_to_all x2, blocking collectives, exchange(): lax.all_to_all(chunks, 'expert', split_axis=0, concat_axis=0, tiled=True,...  48.3 us
    all_to_all x2, waiting for transfers between devices, exchange(): lax.all_to_all(chunks, 'expert', split_axis=0, concat_axis=0, tiled=True,...  32.4 us
    all_to_all x2, starting transfers between devices, exchange(): lax.all_to_all(chunks, 'expert', split_axis=0, concat_axis=0, tiled=True,...  17.9 us
    pallas_call x5, Pallas kernels, kernel_call(): pl.pallas_call(body, out_shape=out_shape, in_specs=specs or [whole] * len...  11.1 us
    ppermute x3, starting transfers between devices, on_device(): sibling = [lax.ppermute(w, 'expert', swap) for w in own]  6.24 us
    ppermute x1, waiting for transfers between devices, on_device(): return lax.ppermute(layer_out, 'segment', route).reshape(activations.shape)  3.96 us
    ppermute x1, starting transfers between devices, on_device(): return lax.ppermute(layer_out, 'segment', route).reshape(activations.shape)  3.4 us
    ppermute x3, waiting for transfers between devices, on_device(): sibling = [lax.ppermute(w, 'expert', swap) for w in own]  2.7 us
  transfers between devices with their start and end apart: 6, of which 5 were waited for; matrix products, arithmetic and copies ran while one was open for 0% of the time, Pallas kernels for 0%

profile of v4, /device:TPU:8, one launch (start us, length us, event | category | flops | bytes accessed | tf_op | source)
XLA Modules:
  0.0 127.8 jit_solution(11179923505556388310)
XLA Ops:
  0.0 1.9 %shard_map.73 = bf16[8,16,2176]{2,1,0:T(8,128)(2,1)} custom-call(bf16[16,2048]{1,0:T(8,128)(2,1)} %bitcast.8, f32[1,2048]{1,0:T(1,128)} %refs_1_.1, s32[16,8]{1,0:T(8,128)} %bitcast.17, f32[16,8]{1,0:T(8,128)} %bitcast.18), custom_call_target="tpu_custom_call" | custom-call | tf_op jit(solution)/shard_map/pallas_call | solution.py:137
  1.9 9.3 %all-to-all-start = ((bf16[8,16,2176]{2,1,0:T(8,128)(2,1)}), bf16[8,16,2176]{2,1,0:T(8,128)(2,1)S(1)}, u32[]{:S(2)}, u32[]{:S(2)}) async-start(bf16[8,16,2176]{2,1,0:T(8,128)(2,1)} %shard_map.73), calls=%async_computation | async-start | bytes 1114112 | tf_op jit(solution)/shard_map/all_to_all | solution.py:22
  11.2 12.2 %all-to-all-done.gathered = bf16[8,16,2176]{2,1,0:T(8,128)(2,1)S(1)} async-done(((bf16[8,16,2176]{2,1,0:T(8,128)(2,1)}), bf16[8,16,2176]{2,1,0:T(8,128)(2,1)S(1)}, u32[]{:S(2)}, u32[]{:S(2)}) %all-to-all-start) | async-done | bytes 557088 | tf_op jit(solution)/shard_map/all_to_all | solution.py:22
  23.4 1.9 %shard_map.74 = (bf16[8,64,2048]{2,1,0:T(8,128)(2,1)}, bf16[2,512,128]{2,1,0:T(8,128)(2,1)S(1)}) custom-call(s32[1]{0:T(128)} %bitcast.1.place, bf16[8,16,2176]{2,1,0:T(8,128)(2,1)S(1)} %all-to-all-done.gathered), custom_call_target="tpu_custom_call" | custom-call | tf_op jit(solution)/shard_map/pallas_call | solution.py:137
  25.3 8.6 %all-to-all-start.1 = ((bf16[8,64,2048]{2,1,0:T(8,128)(2,1)}), bf16[8,64,2048]{2,1,0:T(8,128)(2,1)S(1)}, u32[]{:S(2)}, u32[]{:S(2)}) async-start(bf16[8,64,2048]{2,1,0:T(8,128)(2,1)} %get-tuple-element.7), calls=%async_computation.1 | async-start | bytes 4194304 | tf_op jit(solution)/shard_map/all_to_all | solution.py:22
  33.9 1.9 %collective-permute-start = (bf16[2048,384]{1,0:T(8,128)(2,1)}, bf16[2048,384]{1,0:T(8,128)(2,1)S(1)}, u32[]{:S(2)}, u32[]{:S(2)}) collective-permute-start(bf16[2048,384]{1,0:T(8,128)(2,1)} %bitcast.10), channel_id=1, source_target_pairs={{0,1},{1,0},{2,3},{3,2},{4,5},{5,4},{6,7},{7,6},{8,9},{9,8},{10,11... | collective-permute-start | bytes 4718600 | tf_op jit(solution)/shard_map/ppermute | solution.py:162
  35.8 2.4 %collective-permute-start.1 = (bf16[2048,384]{1,0:T(8,128)(2,1)}, bf16[2048,384]{1,0:T(8,128)(2,1)S(1)}, u32[]{:S(2)}, u32[]{:S(2)}) collective-permute-start(bf16[2048,384]{1,0:T(8,128)(2,1)} %bitcast.12), channel_id=1, source_target_pairs={{0,1},{1,0},{2,3},{3,2},{4,5},{5,4},{6,7},{7,6},{8,9},{9,8},{10,11... | collective-permute-start | bytes 4718600 | tf_op jit(solution)/shard_map/ppermute | solution.py:162
  38.2 1.9 %collective-permute-start.2 = (bf16[384,2048]{1,0:T(8,128)(2,1)}, bf16[384,2048]{1,0:T(8,128)(2,1)}, u32[]{:S(2)}, u32[]{:S(2)}) collective-permute-start(bf16[384,2048]{1,0:T(8,128)(2,1)} %bitcast.14), channel_id=1, source_target_pairs={{0,1},{1,0},{2,3},{3,2},{4,5},{5,4},{6,7},{7,6},{8,9},{9,8},{10,11... | collective-permute-start | bytes 4718600 | tf_op jit(solution)/shard_map/ppermute | solution.py:162
  40.2 0.0 collective-permute-done.refs_3_
  40.2 0.0 copy-start.1
  40.2 1.5 %collective-permute-done.1.refs_4_ = bf16[2048,384]{1,0:T(8,128)(2,1)S(1)} collective-permute-done((bf16[2048,384]{1,0:T(8,128)(2,1)}, bf16[2048,384]{1,0:T(8,128)(2,1)S(1)}, u32[]{:S(2)}, u32[]{:S(2)}) %collective-permute-start.1) | collective-permute-done | bytes 1572896 | tf_op jit(solution)/shard_map/ppermute | solution.py:162
  41.7 0.0 copy-done.1
  41.7 0.0 copy-start.2
  41.7 1.1 copy-done.2
  42.8 1.2 collective-permute-done.2.refs_5_
  44.0 20.1 %all-to-all-done.1.rows = bf16[8,64,2048]{2,1,0:T(8,128)(2,1)S(1)} async-done(((bf16[8,64,2048]{2,1,0:T(8,128)(2,1)}), bf16[8,64,2048]{2,1,0:T(8,128)(2,1)S(1)}, u32[]{:S(2)}, u32[]{:S(2)}) %all-to-all-start.1) | async-done | bytes 2097184 | tf_op jit(solution)/shard_map/all_to_all | solution.py:22
  64.2 6.4 %shard_map.75 = bf16[8,64,2048]{2,1,0:T(8,128)(2,1)S(1)} custom-call(bf16[8,64,2048]{2,1,0:T(8,128)(2,1)S(1)} %all-to-all-done.1.rows, bf16[2048,384]{1,0:T(8,128)(2,1)} %bitcast.11, bf16[2048,384]{1,0:T(8,128)(2,1)} %bitcast.13, bf16[384,2048]{1,0:T(8,128)(2,1)} %bitcast.15, bf16[2048,384]{1,0:T(8,128)(2,1)} %copy-done.1, bf16[2048,384]{1,0:T(8,128)(2,1)} %copy-done.2, ...), custom_call_target="tpu_custom_call" | custom-call | flops 2415919104 | tf_op jit(solution)/shard_map/pallas_call | solution.py:137
  70.6 32.6 %all_to_all.20.returned = bf16[8,64,2048]{2,1,0:T(8,128)(2,1)S(1)} all-to-all(bf16[8,64,2048]{2,1,0:T(8,128)(2,1)S(1)} %shard_map.75), channel_id=1, replica_groups={{0,16,32,48,64,80,96,112},{2,18,34,50,66,82,98,114},{4,20,36,52,68,84,1..., dimensions={0} | all-to-all | bytes 4194304 | tf_op jit(solution)/shard_map/all_to_all | solution.py:22
  103.2 0.0 copy-start
  103.2 0.7 shard_map.76
  104.0 15.7 %all_to_all.21.pieces = bf16[8,16,2048]{2,1,0:T(8,128)(2,1)S(1)} all-to-all(bf16[8,16,2048]{2,1,0:T(8,128)(2,1)S(1)} %shard_map.76), channel_id=1, replica_groups={{0,2,4,6,8,10,12,14},{16,18,20,22,24,26,28,30},{32,34,36,38,40,42,44,46..., dimensions={0} | all-to-all | bytes 1048576 | tf_op jit(solution)/shard_map/all_to_all | solution.py:22
  119.7 0.0 copy-done
  119.7 0.1 shard_map.77
  119.8 3.4 %collective-permute-start.3 = (bf16[16,2048]{1,0:T(8,128)(2,1)S(1)}, bf16[16,2048]{1,0:T(8,128)(2,1)S(1)}, u32[]{:S(2)}, u32[]{:S(2)}) collective-permute-start(bf16[16,2048]{1,0:T(8,128)(2,1)S(1)} %shard_map.77), channel_id=1, source_target_pairs={{0,128},{128,256},{256,384},{384,0},{1,129},{129,257},{257,385},{3... | collective-permute-start | bytes 196616 | tf_op jit(solution)/shard_map/ppermute | solution.py:215
  123.2 4.0 %collective-permute-done.3 = bf16[16,2048]{1,0:T(8,128)(2,1)S(1)} collective-permute-done((bf16[16,2048]{1,0:T(8,128)(2,1)S(1)}, bf16[16,2048]{1,0:T(8,128)(2,1)S(1)}, u32[]{:S(2)}, u32[]{:S(2)}) %collective-permute-start.3) | collective-permute-done | bytes 65568 | tf_op jit(solution)/shard_map/ppermute | solution.py:215
  127.1 0.6 copy.15
Async XLA Ops:
  1.9 21.5 %all-to-all-start = ((bf16[8,16,2176]{2,1,0:T(8,128)(2,1)}), bf16[8,16,2176]{2,1,0:T(8,128)(2,1)S(1)}, u32[]{:S(2)}, u32[]{:S(2)}) async-start(bf16[8,16,2176]{2,1,0:T(8,128)(2,1)} %shard_map.73), calls=%async_computation | async-start | bytes 1114112 | tf_op jit(solution)/shard_map/all_to_all | solution.py:22
  25.3 38.9 %all-to-all-start.1 = ((bf16[8,64,2048]{2,1,0:T(8,128)(2,1)}), bf16[8,64,2048]{2,1,0:T(8,128)(2,1)S(1)}, u32[]{:S(2)}, u32[]{:S(2)}) async-start(bf16[8,64,2048]{2,1,0:T(8,128)(2,1)} %get-tuple-element.7), calls=%async_computation.1 | async-start | bytes 4194304 | tf_op jit(solution)/shard_map/all_to_all | solution.py:22
  33.9 6.3 %collective-permute-start = (bf16[2048,384]{1,0:T(8,128)(2,1)}, bf16[2048,384]{1,0:T(8,128)(2,1)S(1)}, u32[]{:S(2)}, u32[]{:S(2)}) collective-permute-start(bf16[2048,384]{1,0:T(8,128)(2,1)} %bitcast.10), channel_id=1, source_target_pairs={{0,1},{1,0},{2,3},{3,2},{4,5},{5,4},{6,7},{7,6},{8,9},{9,8},{10,11... | collective-permute-start | bytes 4718600 | tf_op jit(solution)/shard_map/ppermute | solution.py:162
  35.8 5.8 %collective-permute-start.1 = (bf16[2048,384]{1,0:T(8,128)(2,1)}, bf16[2048,384]{1,0:T(8,128)(2,1)S(1)}, u32[]{:S(2)}, u32[]{:S(2)}) collective-permute-start(bf16[2048,384]{1,0:T(8,128)(2,1)} %bitcast.12), channel_id=1, source_target_pairs={{0,1},{1,0},{2,3},{3,2},{4,5},{5,4},{6,7},{7,6},{8,9},{9,8},{10,11... | collective-permute-start | bytes 4718600 | tf_op jit(solution)/shard_map/ppermute | solution.py:162
  38.2 5.8 %collective-permute-start.2 = (bf16[384,2048]{1,0:T(8,128)(2,1)}, bf16[384,2048]{1,0:T(8,128)(2,1)}, u32[]{:S(2)}, u32[]{:S(2)}) collective-permute-start(bf16[384,2048]{1,0:T(8,128)(2,1)} %bitcast.14), channel_id=1, source_target_pairs={{0,1},{1,0},{2,3},{3,2},{4,5},{5,4},{6,7},{7,6},{8,9},{9,8},{10,11... | collective-permute-start | bytes 4718600 | tf_op jit(solution)/shard_map/ppermute | solution.py:162
  40.2 1.5 %copy-start.1 = (bf16[2048,384]{1,0:T(8,128)(2,1)}, bf16[2048,384]{1,0:T(8,128)(2,1)S(1)}, u32[]{:S(2)}) copy-start(bf16[2048,384]{1,0:T(8,128)(2,1)S(1)} %collective-permute-done.refs_3_) | copy-start | bytes 4718596
  41.7 1.1 copy-start.2
  103.2 16.5 %copy-start = (bf16[1,2,8,2048]{3,2,1,0:T(8,128)(2,1)S(1)}, bf16[1,2,8,2048]{3,2,1,0:T(8,128)(2,1)}, u32[]{:S(2)}) copy-start(bf16[1,2,8,2048]{3,2,1,0:T(8,128)(2,1)} %param.7) | copy-start | bytes 196612
  119.8 7.4 %collective-permute-start.3 = (bf16[16,2048]{1,0:T(8,128)(2,1)S(1)}, bf16[16,2048]{1,0:T(8,128)(2,1)S(1)}, u32[]{:S(2)}, u32[]{:S(2)}) collective-permute-start(bf16[16,2048]{1,0:T(8,128)(2,1)S(1)} %shard_map.77), channel_id=1, source_target_pairs={{0,128},{128,256},{256,384},{384,0},{1,129},{129,257},{257,385},{3... | collective-permute-start | bytes 196616 | tf_op jit(solution)/shard_map/ppermute | solution.py:215

commit v5 on v4

--- a/solution.py
+++ b/solution.py
@@ -55,64 +55,77 @@
 
 def pack_kernel(place, gathered, out, blend, held, sems):
     tokens = gathered.shape[0] * gathered.shape[1]
-    width = out.shape[2]
-    slots = out.shape[0] * out.shape[1]
+    width, size = out.shape[2], out.shape[1]
     mine = place[0]
     z, y, core = mine // 16, (mine // 2) % RING, mine % 2
-    shape = (slots, 128)
-    row = lax.broadcasted_iota(jnp.int32, shape, 0)
-    lane = lax.broadcasted_iota(jnp.int32, shape, 1)
-    member, other, block, rank = row >> 6, (row >> 5) & 1, (row >> 1) & 15, row & 1
-    chip = jnp.where(core == 0, (member & 3) * RING + y, (z % 4) * RING + member)
-    expert = chip * 2 + (other ^ core)
-    parts = gathered[:, :, width:].reshape(tokens, 128)
-    pick_high = (lane == expert).astype(jnp.bfloat16)
-    pick_low = (lane == expert + 64).astype(jnp.bfloat16)
-    high = dot(pick_high, parts, ((1,), (1,)))
-    low = dot(pick_low, parts, ((1,), (1,)))
-    named = jnp.where((high != 0.0) & ((lane >> 3) == block), 1.0, 0.0)
+    row = lax.broadcasted_iota(jnp.int32, (size, 128), 0)
+    lane = lax.broadcasted_iota(jnp.int32, (size, 128), 1)
+    other, block, rank = row >> 5, (row >> 1) & 15, (row & 1).astype(jnp.float32)
+    same_block = (lane >> 3) == block
     before = (
         lax.broadcasted_iota(jnp.int32, (128, 128), 0)
         < lax.broadcasted_iota(jnp.int32, (128, 128), 1)
     ).astype(jnp.bfloat16)
-    earlier = dot(named.astype(jnp.bfloat16), before)
-    pick = jnp.where(earlier == rank.astype(jnp.float32), named, 0.0)
-    blend[0] = (pick * high).astype(jnp.bfloat16)
-    blend[1] = (pick * low).astype(jnp.bfloat16)
     rows = gathered[:, :, :width].reshape(tokens, width)
-    pick = pick.astype(jnp.bfloat16)
-    size = out.shape[1]
-    copies = [pltpu.make_async_copy(held.at[i], out.at[i], sems.at[i]) for i in range(RING)]
-    for i in range(RING):
-        held[i] = dot(pick[i * size : (i + 1) * size], rows).astype(jnp.bfloat16)
-        copies[i].start()
+    parts = gathered[:, :, width:].reshape(tokens, 128)
+    mixes, copies = [], []
+    for member in range(RING):
+        chip = jnp.where(core == 0, (member & 3) * RING + y, (z % 4) * RING + member)
+        expert = chip * 2 + (other ^ core)
+        high = dot((lane == expert).astype(jnp.bfloat16), parts, ((1,), (1,)))
+        low = dot((lane == expert + 64).astype(jnp.bfloat16), parts, ((1,), (1,)))
+        named = jnp.where((high != 0.0) & same_block, 1.0, 0.0)
+        earlier = dot(named.astype(jnp.bfloat16), before)
+        pick = jnp.where(earlier == rank, named, 0.0)
+        held[member] = dot(pick.astype(jnp.bfloat16), rows).astype(jnp.bfloat16)
+        copies.append(pltpu.make_async_copy(held.at[member], out.at[member], sems.at[member]))
+        copies[member].start()
+        mixes.append((pick * high, pick * low))
+    for member in range(RING):
+        for part in range(2):
+            chunk = mixes[member][part].astype(jnp.bfloat16)
+            blend[part, member * size : (member + 1) * size] = chunk
     for copy in copies:
         copy.wait()
 
 
 def expert_kernel(rows, *refs):
     weights, out = refs[:6], refs[6]
-    gate_up, down, sems = refs[7:]
-    hidden_units = down.shape[1]
+    gate_up, down, sems, down_sems = refs[7:]
+    hidden_units, width = down.shape[1:]
     half = rows.shape[1] // 2
-    copies = []
+    arrivals, down_arrivals = [], []
+    for e, parts in ((0, 4), (1, 2)):
+        size = width // parts
+        for k in range(parts):
+            span = pl.ds(k * size, size)
+            pair = [
+                pltpu.make_async_copy(
+                    weights[3 * e + i].at[span],
+                    gate_up.at[e, span, i * hidden_units : (i + 1) * hidden_units],
+                    sems.at[e, k, i],
+                )
+                for i in range(2)
+            ]
+            arrivals.append((e, k * size, size, pair))
     for e in range(2):
-        gate_ref, up_ref, down_ref = weights[3 * e : 3 * e + 3]
-        copies += [
-            pltpu.make_async_copy(gate_ref, gate_up.at[e, :, :hidden_units], sems.at[e, 0]),
-            pltpu.make_async_copy(up_ref, gate_up.at[e, :, hidden_units:], sems.at[e, 1]),
-            pltpu.make_async_copy(down_ref, down.at[e], sems.at[e, 2]),
-        ]
-    for copy in copies:
+        down_arrivals.append(pltpu.make_async_copy(weights[3 * e + 2], down.at[e], down_sems.at[e]))
+    for _, _, _, pair in arrivals:
+        for copy in pair:
+            copy.start()
+    for copy in down_arrivals:
         copy.start()
+    sums = [None, None]
+    for e, first, size, pair in arrivals:
+        for copy in pair:
+            copy.wait()
+        x = rows[:, e * half : (e + 1) * half, first : first + size].reshape(-1, size)
+        term = dot(x, gate_up[e, first : first + size])
+        sums[e] = term if sums[e] is None else sums[e] + term
     for e in range(2):
-        x = rows[:, e * half : (e + 1) * half, :].reshape(-1, rows.shape[2])
-        copies[3 * e].wait()
-        copies[3 * e + 1].wait()
-        both = dot(x, gate_up[e])
-        gate, up = both[:, :hidden_units], both[:, hidden_units:]
+        gate, up = sums[e][:, :hidden_units], sums[e][:, hidden_units:]
         hidden = (gate / (1.0 + jnp.exp(-gate)) * up).astype(jnp.bfloat16)
-        copies[3 * e + 2].wait()
+        down_arrivals[e].wait()
         answer = dot(hidden, down[e]).astype(jnp.bfloat16)
         out[:, e * half : (e + 1) * half, :] = answer.reshape(out.shape[0], half, out.shape[2])
 
@@ -197,7 +210,8 @@
         scratch=(
             pltpu.VMEM((2, width, 2 * hidden_units), bf16),
             pltpu.VMEM((2, hidden_units, width), bf16),
-            pltpu.SemaphoreType.DMA((2, 3)),
+            pltpu.SemaphoreType.DMA((2, 4, 2)),
+            pltpu.SemaphoreType.DMA((2,)),
         ),
         limit=32,
         flops=6 * RING * slots * width * hidden_units,

time: 128 us -> 130 us (1.016)
  Pallas kernels: 11.1 us -> 12.5 us
    pallas_call x5, Pallas kernels: 11.1 us -> 12.5 us  [kernel_call(): pl.pallas_call(body, out_shape=out_shape, in_specs=specs or [whole] * len...]
where the time goes in v5:
time: 130 us; the launch traced here: 129 us
  blocking collectives  48.3 us (37%)
  waiting for transfers between devices  39 us (30%)
  starting transfers between devices  27.5 us (21%)
  Pallas kernels  12.5 us (10%)
  local copies, waits for them, and re-layouts  1.78 us (1%)
    all_to_all x2, blocking collectives, exchange(): lax.all_to_all(chunks, 'expert', split_axis=0, concat_axis=0, tiled=True,...  48.3 us
    all_to_all x2, waiting for transfers between devices, exchange(): lax.all_to_all(chunks, 'expert', split_axis=0, concat_axis=0, tiled=True,...  32.4 us
    all_to_all x2, starting transfers between devices, exchange(): lax.all_to_all(chunks, 'expert', split_axis=0, concat_axis=0, tiled=True,...  17.9 us
    pallas_call x5, Pallas kernels, kernel_call(): pl.pallas_call(body, out_shape=out_shape, in_specs=specs or [whole] * len...  12.5 us
    ppermute x3, starting transfers between devices, on_device(): sibling = [lax.ppermute(w, 'expert', swap) for w in own]  6.24 us
    ppermute x1, waiting for transfers between devices, on_device(): return lax.ppermute(layer_out, 'segment', route).reshape(activations.shape)  3.96 us
    ppermute x1, starting transfers between devices, on_device(): return lax.ppermute(layer_out, 'segment', route).reshape(activations.shape)  3.4 us
    ppermute x3, waiting for transfers between devices, on_device(): sibling = [lax.ppermute(w, 'expert', swap) for w in own]  2.7 us
  transfers between devices with their start and end apart: 6, of which 5 were waited for; matrix products, arithmetic and copies ran while one was open for 0% of the time, Pallas kernels for 0%

profile of v5, /device:TPU:8, one launch (start us, length us, event | category | flops | bytes accessed | tf_op | source)
XLA Modules:
  0.0 129.2 jit_solution(1691209801974233040)
XLA Ops:
  0.0 1.9 %shard_map.73 = bf16[8,16,2176]{2,1,0:T(8,128)(2,1)} custom-call(bf16[16,2048]{1,0:T(8,128)(2,1)} %bitcast.8, f32[1,2048]{1,0:T(1,128)} %refs_1_.1, s32[16,8]{1,0:T(8,128)} %bitcast.17, f32[16,8]{1,0:T(8,128)} %bitcast.18), custom_call_target="tpu_custom_call" | custom-call | tf_op jit(solution)/shard_map/pallas_call | solution.py:150
  1.9 9.3 %all-to-all-start = ((bf16[8,16,2176]{2,1,0:T(8,128)(2,1)}), bf16[8,16,2176]{2,1,0:T(8,128)(2,1)S(1)}, u32[]{:S(2)}, u32[]{:S(2)}) async-start(bf16[8,16,2176]{2,1,0:T(8,128)(2,1)} %shard_map.73), calls=%async_computation | async-start | bytes 1114112 | tf_op jit(solution)/shard_map/all_to_all | solution.py:22
  11.2 12.2 %all-to-all-done.gathered = bf16[8,16,2176]{2,1,0:T(8,128)(2,1)S(1)} async-done(((bf16[8,16,2176]{2,1,0:T(8,128)(2,1)}), bf16[8,16,2176]{2,1,0:T(8,128)(2,1)S(1)}, u32[]{:S(2)}, u32[]{:S(2)}) %all-to-all-start) | async-done | bytes 557088 | tf_op jit(solution)/shard_map/all_to_all | solution.py:22
  23.4 3.6 %shard_map.74 = (bf16[8,64,2048]{2,1,0:T(8,128)(2,1)}, bf16[2,512,128]{2,1,0:T(8,128)(2,1)S(1)}) custom-call(s32[1]{0:T(128)} %bitcast.1.place, bf16[8,16,2176]{2,1,0:T(8,128)(2,1)S(1)} %all-to-all-done.gathered), custom_call_target="tpu_custom_call" | custom-call | tf_op jit(solution)/shard_map/pallas_call | solution.py:150
  27.0 8.6 %all-to-all-start.1 = ((bf16[8,64,2048]{2,1,0:T(8,128)(2,1)}), bf16[8,64,2048]{2,1,0:T(8,128)(2,1)S(1)}, u32[]{:S(2)}, u32[]{:S(2)}) async-start(bf16[8,64,2048]{2,1,0:T(8,128)(2,1)} %get-tuple-element.7), calls=%async_computation.1 | async-start | bytes 4194304 | tf_op jit(solution)/shard_map/all_to_all | solution.py:22
  35.6 1.9 %collective-permute-start = (bf16[2048,384]{1,0:T(8,128)(2,1)}, bf16[2048,384]{1,0:T(8,128)(2,1)S(1)}, u32[]{:S(2)}, u32[]{:S(2)}) collective-permute-start(bf16[2048,384]{1,0:T(8,128)(2,1)} %bitcast.10), channel_id=1, source_target_pairs={{0,1},{1,0},{2,3},{3,2},{4,5},{5,4},{6,7},{7,6},{8,9},{9,8},{10,11... | collective-permute-start | bytes 4718600 | tf_op jit(solution)/shard_map/ppermute | solution.py:175
  37.5 2.4 %collective-permute-start.1 = (bf16[2048,384]{1,0:T(8,128)(2,1)}, bf16[2048,384]{1,0:T(8,128)(2,1)S(1)}, u32[]{:S(2)}, u32[]{:S(2)}) collective-permute-start(bf16[2048,384]{1,0:T(8,128)(2,1)} %bitcast.12), channel_id=1, source_target_pairs={{0,1},{1,0},{2,3},{3,2},{4,5},{5,4},{6,7},{7,6},{8,9},{9,8},{10,11... | collective-permute-start | bytes 4718600 | tf_op jit(solution)/shard_map/ppermute | solution.py:175
  40.0 1.9 %collective-permute-start.2 = (bf16[384,2048]{1,0:T(8,128)(2,1)}, bf16[384,2048]{1,0:T(8,128)(2,1)}, u32[]{:S(2)}, u32[]{:S(2)}) collective-permute-start(bf16[384,2048]{1,0:T(8,128)(2,1)} %bitcast.14), channel_id=1, source_target_pairs={{0,1},{1,0},{2,3},{3,2},{4,5},{5,4},{6,7},{7,6},{8,9},{9,8},{10,11... | collective-permute-start | bytes 4718600 | tf_op jit(solution)/shard_map/ppermute | solution.py:175
  41.9 0.0 collective-permute-done.refs_3_
  41.9 0.0 copy-start.1
  41.9 1.5 %collective-permute-done.1.refs_4_ = bf16[2048,384]{1,0:T(8,128)(2,1)S(1)} collective-permute-done((bf16[2048,384]{1,0:T(8,128)(2,1)}, bf16[2048,384]{1,0:T(8,128)(2,1)S(1)}, u32[]{:S(2)}, u32[]{:S(2)}) %collective-permute-start.1) | collective-permute-done | bytes 1572896 | tf_op jit(solution)/shard_map/ppermute | solution.py:175
  43.4 0.0 copy-done.1
  43.4 0.0 copy-start.2
  43.4 1.1 copy-done.2
  44.5 1.2 collective-permute-done.2.refs_5_
  45.8 20.1 %all-to-all-done.1.rows = bf16[8,64,2048]{2,1,0:T(8,128)(2,1)S(1)} async-done(((bf16[8,64,2048]{2,1,0:T(8,128)(2,1)}), bf16[8,64,2048]{2,1,0:T(8,128)(2,1)S(1)}, u32[]{:S(2)}, u32[]{:S(2)}) %all-to-all-start.1) | async-done | bytes 2097184 | tf_op jit(solution)/shard_map/all_to_all | solution.py:22
  65.9 6.2 %shard_map.75 = bf16[8,64,2048]{2,1,0:T(8,128)(2,1)S(1)} custom-call(bf16[8,64,2048]{2,1,0:T(8,128)(2,1)S(1)} %all-to-all-done.1.rows, bf16[2048,384]{1,0:T(8,128)(2,1)} %bitcast.11, bf16[2048,384]{1,0:T(8,128)(2,1)} %bitcast.13, bf16[384,2048]{1,0:T(8,128)(2,1)} %bitcast.15, bf16[2048,384]{1,0:T(8,128)(2,1)} %copy-done.1, bf16[2048,384]{1,0:T(8,128)(2,1)} %copy-done.2, ...), custom_call_target="tpu_custom_call" | custom-call | flops 2415919104 | tf_op jit(solution)/shard_map/pallas_call | solution.py:150
  72.1 32.6 %all_to_all.20.returned = bf16[8,64,2048]{2,1,0:T(8,128)(2,1)S(1)} all-to-all(bf16[8,64,2048]{2,1,0:T(8,128)(2,1)S(1)} %shard_map.75), channel_id=1, replica_groups={{0,16,32,48,64,80,96,112},{2,18,34,50,66,82,98,114},{4,20,36,52,68,84,1..., dimensions={0} | all-to-all | bytes 4194304 | tf_op jit(solution)/shard_map/all_to_all | solution.py:22
  104.6 0.0 copy-start
  104.6 0.7 shard_map.76
  105.4 15.7 %all_to_all.21.pieces = bf16[8,16,2048]{2,1,0:T(8,128)(2,1)S(1)} all-to-all(bf16[8,16,2048]{2,1,0:T(8,128)(2,1)S(1)} %shard_map.76), channel_id=1, replica_groups={{0,2,4,6,8,10,12,14},{16,18,20,22,24,26,28,30},{32,34,36,38,40,42,44,46..., dimensions={0} | all-to-all | bytes 1048576 | tf_op jit(solution)/shard_map/all_to_all | solution.py:22
  121.1 0.0 copy-done
  121.1 0.1 shard_map.77
  121.2 3.4 %collective-permute-start.3 = (bf16[16,2048]{1,0:T(8,128)(2,1)S(1)}, bf16[16,2048]{1,0:T(8,128)(2,1)S(1)}, u32[]{:S(2)}, u32[]{:S(2)}) collective-permute-start(bf16[16,2048]{1,0:T(8,128)(2,1)S(1)} %shard_map.77), channel_id=1, source_target_pairs={{0,128},{128,256},{256,384},{384,0},{1,129},{129,257},{257,385},{3... | collective-permute-start | bytes 196616 | tf_op jit(solution)/shard_map/ppermute | solution.py:229
  124.6 4.0 %collective-permute-done.3 = bf16[16,2048]{1,0:T(8,128)(2,1)S(1)} collective-permute-done((bf16[16,2048]{1,0:T(8,128)(2,1)S(1)}, bf16[16,2048]{1,0:T(8,128)(2,1)S(1)}, u32[]{:S(2)}, u32[]{:S(2)}) %collective-permute-start.3) | collective-permute-done | bytes 65568 | tf_op jit(solution)/shard_map/ppermute | solution.py:229
  128.6 0.6 copy.15
Async XLA Ops:
  1.9 21.5 %all-to-all-start = ((bf16[8,16,2176]{2,1,0:T(8,128)(2,1)}), bf16[8,16,2176]{2,1,0:T(8,128)(2,1)S(1)}, u32[]{:S(2)}, u32[]{:S(2)}) async-start(bf16[8,16,2176]{2,1,0:T(8,128)(2,1)} %shard_map.73), calls=%async_computation | async-start | bytes 1114112 | tf_op jit(solution)/shard_map/all_to_all | solution.py:22
  27.0 38.9 %all-to-all-start.1 = ((bf16[8,64,2048]{2,1,0:T(8,128)(2,1)}), bf16[8,64,2048]{2,1,0:T(8,128)(2,1)S(1)}, u32[]{:S(2)}, u32[]{:S(2)}) async-start(bf16[8,64,2048]{2,1,0:T(8,128)(2,1)} %get-tuple-element.7), calls=%async_computation.1 | async-start | bytes 4194304 | tf_op jit(solution)/shard_map/all_to_all | solution.py:22
  35.6 6.3 %collective-permute-start = (bf16[2048,384]{1,0:T(8,128)(2,1)}, bf16[2048,384]{1,0:T(8,128)(2,1)S(1)}, u32[]{:S(2)}, u32[]{:S(2)}) collective-permute-start(bf16[2048,384]{1,0:T(8,128)(2,1)} %bitcast.10), channel_id=1, source_target_pairs={{0,1},{1,0},{2,3},{3,2},{4,5},{5,4},{6,7},{7,6},{8,9},{9,8},{10,11... | collective-permute-start | bytes 4718600 | tf_op jit(solution)/shard_map/ppermute | solution.py:175
  37.5 5.8 %collective-permute-start.1 = (bf16[2048,384]{1,0:T(8,128)(2,1)}, bf16[2048,384]{1,0:T(8,128)(2,1)S(1)}, u32[]{:S(2)}, u32[]{:S(2)}) collective-permute-start(bf16[2048,384]{1,0:T(8,128)(2,1)} %bitcast.12), channel_id=1, source_target_pairs={{0,1},{1,0},{2,3},{3,2},{4,5},{5,4},{6,7},{7,6},{8,9},{9,8},{10,11... | collective-permute-start | bytes 4718600 | tf_op jit(solution)/shard_map/ppermute | solution.py:175
  40.0 5.8 %collective-permute-start.2 = (bf16[384,2048]{1,0:T(8,128)(2,1)}, bf16[384,2048]{1,0:T(8,128)(2,1)}, u32[]{:S(2)}, u32[]{:S(2)}) collective-permute-start(bf16[384,2048]{1,0:T(8,128)(2,1)} %bitcast.14), channel_id=1, source_target_pairs={{0,1},{1,0},{2,3},{3,2},{4,5},{5,4},{6,7},{7,6},{8,9},{9,8},{10,11... | collective-permute-start | bytes 4718600 | tf_op jit(solution)/shard_map/ppermute | solution.py:175
  41.9 1.5 %copy-start.1 = (bf16[2048,384]{1,0:T(8,128)(2,1)}, bf16[2048,384]{1,0:T(8,128)(2,1)S(1)}, u32[]{:S(2)}) copy-start(bf16[2048,384]{1,0:T(8,128)(2,1)S(1)} %collective-permute-done.refs_3_) | copy-start | bytes 4718596
  43.4 1.1 copy-start.2
  104.6 16.5 %copy-start = (bf16[1,2,8,2048]{3,2,1,0:T(8,128)(2,1)S(1)}, bf16[1,2,8,2048]{3,2,1,0:T(8,128)(2,1)}, u32[]{:S(2)}) copy-start(bf16[1,2,8,2048]{3,2,1,0:T(8,128)(2,1)} %param.7) | copy-start | bytes 196612
  121.2 7.4 %collective-permute-start.3 = (bf16[16,2048]{1,0:T(8,128)(2,1)S(1)}, bf16[16,2048]{1,0:T(8,128)(2,1)S(1)}, u32[]{:S(2)}, u32[]{:S(2)}) collective-permute-start(bf16[16,2048]{1,0:T(8,128)(2,1)S(1)} %shard_map.77), channel_id=1, source_target_pairs={{0,128},{128,256},{256,384},{384,0},{1,129},{129,257},{257,385},{3... | collective-permute-start | bytes 196616 | tf_op jit(solution)/shard_map/ppermute | solution.py:229

commit v6 on v4

--- a/solution.py
+++ b/solution.py
@@ -53,67 +53,73 @@
         copy.wait()
 
 
-def pack_kernel(place, gathered, out, blend, held, sems):
-    tokens = gathered.shape[0] * gathered.shape[1]
-    width = out.shape[2]
-    slots = out.shape[0] * out.shape[1]
+def mask_kernel(place, masks):
     mine = place[0]
     z, y, core = mine // 16, (mine // 2) % RING, mine % 2
-    shape = (slots, 128)
+    shape = masks.shape[1:]
     row = lax.broadcasted_iota(jnp.int32, shape, 0)
     lane = lax.broadcasted_iota(jnp.int32, shape, 1)
-    member, other, block, rank = row >> 6, (row >> 5) & 1, (row >> 1) & 15, row & 1
+    member, other = row >> 6, (row >> 5) & 1
     chip = jnp.where(core == 0, (member & 3) * RING + y, (z % 4) * RING + member)
     expert = chip * 2 + (other ^ core)
-    parts = gathered[:, :, width:].reshape(tokens, 128)
-    pick_high = (lane == expert).astype(jnp.bfloat16)
-    pick_low = (lane == expert + 64).astype(jnp.bfloat16)
-    high = dot(pick_high, parts, ((1,), (1,)))
-    low = dot(pick_low, parts, ((1,), (1,)))
-    named = jnp.where((high != 0.0) & ((lane >> 3) == block), 1.0, 0.0)
+    masks[0] = (lane == expert).astype(jnp.bfloat16)
+    masks[1] = (lane == expert + 64).astype(jnp.bfloat16)
+
+
+def pack_kernel(masks, gathered, *refs):
+    out, blend, rows, parts, sems = refs[-5:]
+    width = out.shape[2]
+    copies = [
+        pltpu.make_async_copy(gathered.at[:, :, width:], parts, sems.at[0]),
+        pltpu.make_async_copy(gathered.at[:, :, :width], rows, sems.at[1]),
+    ]
+    for copy in copies:
+        copy.start()
+    shape = masks.shape[1:]
+    row = lax.broadcasted_iota(jnp.int32, shape, 0)
+    lane = lax.broadcasted_iota(jnp.int32, shape, 1)
+    same_block = (lane >> 3) == ((row >> 1) & 15)
+    rank = (row & 1).astype(jnp.float32)
     before = (
         lax.broadcasted_iota(jnp.int32, (128, 128), 0)
         < lax.broadcasted_iota(jnp.int32, (128, 128), 1)
     ).astype(jnp.bfloat16)
+    copies[0].wait()
+    weight_parts = parts[...].reshape(-1, 128)
+    high = dot(masks[0], weight_parts, ((1,), (1,)))
+    low = dot(masks[1], weight_parts, ((1,), (1,)))
+    named = jnp.where((high != 0.0) & same_block, 1.0, 0.0)
     earlier = dot(named.astype(jnp.bfloat16), before)
-    pick = jnp.where(earlier == rank.astype(jnp.float32), named, 0.0)
+    pick = jnp.where(earlier == rank, named, 0.0)
     blend[0] = (pick * high).astype(jnp.bfloat16)
     blend[1] = (pick * low).astype(jnp.bfloat16)
-    rows = gathered[:, :, :width].reshape(tokens, width)
-    pick = pick.astype(jnp.bfloat16)
-    size = out.shape[1]
-    copies = [pltpu.make_async_copy(held.at[i], out.at[i], sems.at[i]) for i in range(RING)]
-    for i in range(RING):
-        held[i] = dot(pick[i * size : (i + 1) * size], rows).astype(jnp.bfloat16)
-        copies[i].start()
-    for copy in copies:
-        copy.wait()
+    copies[1].wait()
+    picked = dot(pick.astype(jnp.bfloat16), rows[...].reshape(-1, width))
+    out[...] = picked.astype(jnp.bfloat16).reshape(out.shape)
 
 
 def expert_kernel(rows, *refs):
-    weights, out = refs[:6], refs[6]
-    gate_up, down, sems = refs[7:]
-    hidden_units = down.shape[1]
+    weights, out = list(refs[:6]), refs[6]
+    gate_own, down_sibling, sems = refs[7:]
+    copies = [
+        pltpu.make_async_copy(weights[0], gate_own, sems.at[0]),
+        pltpu.make_async_copy(weights[5], down_sibling, sems.at[1]),
+    ]
+    for copy in copies:
+        copy.start()
+    weights[0], weights[5] = gate_own, down_sibling
     half = rows.shape[1] // 2
-    copies = []
-    for e in range(2):
-        gate_ref, up_ref, down_ref = weights[3 * e : 3 * e + 3]
-        copies += [
-            pltpu.make_async_copy(gate_ref, gate_up.at[e, :, :hidden_units], sems.at[e, 0]),
-            pltpu.make_async_copy(up_ref, gate_up.at[e, :, hidden_units:], sems.at[e, 1]),
-            pltpu.make_async_copy(down_ref, down.at[e], sems.at[e, 2]),
-        ]
-    for copy in copies:
-        copy.start()
+    hidden = []
     for e in range(2):
         x = rows[:, e * half : (e + 1) * half, :].reshape(-1, rows.shape[2])
-        copies[3 * e].wait()
-        copies[3 * e + 1].wait()
-        both = dot(x, gate_up[e])
-        gate, up = both[:, :hidden_units], both[:, hidden_units:]
-        hidden = (gate / (1.0 + jnp.exp(-gate)) * up).astype(jnp.bfloat16)
-        copies[3 * e + 2].wait()
-        answer = dot(hidden, down[e]).astype(jnp.bfloat16)
+        up = dot(x, weights[3 * e + 1][...])
+        if e == 0:
+            copies[0].wait()
+        gate = dot(x, weights[3 * e][...])
+        hidden.append((gate / (1.0 + jnp.exp(-gate)) * up).astype(jnp.bfloat16))
+    copies[1].wait()
+    for e in range(2):
+        answer = dot(hidden[e], weights[3 * e + 2][...]).astype(jnp.bfloat16)
         out[:, e * half : (e + 1) * half, :] = answer.reshape(out.shape[0], half, out.shape[2])
 
 
@@ -177,29 +183,45 @@
     )
     gathered = exchange(payload, spread)
     place = lax.axis_index("expert").astype(jnp.int32).reshape(1)
+    masks = kernel_call(
+        mask_kernel,
+        jax.ShapeDtypeStruct((2, RING * slots, RING * held), bf16),
+        (place,),
+        specs=[pl.BlockSpec(memory_space=pltpu.SMEM)],
+        flops=20 * 10**9,
+    )
     outgoing, blend = kernel_call(
         pack_kernel,
         (
-            pltpu.HBM((RING, slots, width), bf16),
+            jax.ShapeDtypeStruct((RING, slots, width), bf16),
             jax.ShapeDtypeStruct((2, RING * slots, RING * held), bf16),
         ),
-        (place, gathered),
-        specs=[pl.BlockSpec(memory_space=pltpu.SMEM), whole],
-        out_specs=(far, whole),
-        scratch=[pltpu.VMEM((RING, slots, width), bf16), pltpu.SemaphoreType.DMA((RING,))],
+        (masks, gathered, *sibling),
+        specs=[whole] + [far] * 4,
+        out_specs=(whole, whole),
+        scratch=[
+            pltpu.VMEM((RING, held, width), bf16),
+            pltpu.VMEM((RING, held, 128), bf16),
+            pltpu.SemaphoreType.DMA((2,)),
+        ],
     )
     arrived = exchange(outgoing, deliver)
     answers = kernel_call(
         expert_kernel,
         jax.ShapeDtypeStruct((RING, slots, width), bf16),
-        (arrived, *[pltpu.with_memory_space_constraint(w, pltpu.HBM) for w in own + sibling]),
-        specs=[whole] + [far] * 6,
-        scratch=(
-            pltpu.VMEM((2, width, 2 * hidden_units), bf16),
-            pltpu.VMEM((2, hidden_units, width), bf16),
-            pltpu.SemaphoreType.DMA((2, 3)),
+        (
+            arrived,
+            *[
+                pltpu.with_memory_space_constraint(w, pltpu.HBM if i in (0, 5) else pltpu.VMEM)
+                for i, w in enumerate(own + sibling)
+            ],
         ),
-        limit=32,
+        specs=[whole] + [far if i in (0, 5) else whole for i in range(6)],
+        scratch=[
+            pltpu.VMEM((width, hidden_units), bf16),
+            pltpu.VMEM((hidden_units, width), bf16),
+            pltpu.SemaphoreType.DMA((2,)),
+        ],
         flops=6 * RING * slots * width * hidden_units,
     )
     returned = exchange(answers, deliver)

time: 128 us -> 128 us (level)
  blocking collectives: 48.3 us -> 87.4 us
  waiting for transfers between devices: 39 us -> 9.85 us
  starting transfers between devices: 27.5 us -> 19.6 us
  Pallas kernels: 11.1 us -> 9.78 us
    all_to_all x2 -> x3, blocking collectives: 48.3 us -> 87.4 us  [exchange(): lax.all_to_all(chunks, 'expert', split_axis=0, concat_axis=0, tiled=True,...]
    all_to_all x2 -> x1, waiting for transfers between devices: 32.4 us -> 5.88 us  [exchange(): lax.all_to_all(chunks, 'expert', split_axis=0, concat_axis=0, tiled=True,...]
    all_to_all x2 -> x1, starting transfers between devices: 17.9 us -> 9.91 us  [exchange(): lax.all_to_all(chunks, 'expert', split_axis=0, concat_axis=0, tiled=True,...]
    ppermute x3, waiting for transfers between devices: 2.7 us -> 0.01 us  [on_device(): sibling = [lax.ppermute(w, 'expert', swap) for w in own]]
    pallas_call x5 -> x6, Pallas kernels: 11.1 us -> 9.78 us  [kernel_call(): pl.pallas_call(body, out_shape=out_shape, in_specs=specs or [whole] * len...]
  transfers between devices with their start and end apart: 6 -> 5, of which waited for: 5 -> 2; matrix products, arithmetic and copies ran while one was open for 0% -> 0% of each run, Pallas kernels for 0% -> 0%
where the time goes in v6:
time: 128 us; the launch traced here: 127 us
  blocking collectives  87.4 us (68%)
  starting transfers between devices  19.6 us (15%)
  waiting for transfers between devices  9.85 us (8%)
  Pallas kernels  9.78 us (8%)
    all_to_all x3, blocking collectives, exchange(): lax.all_to_all(chunks, 'expert', split_axis=0, concat_axis=0, tiled=True,...  87.4 us
    all_to_all x1, starting transfers between devices, exchange(): lax.all_to_all(chunks, 'expert', split_axis=0, concat_axis=0, tiled=True,...  9.91 us
    pallas_call x6, Pallas kernels, kernel_call(): pl.pallas_call(body, out_shape=out_shape, in_specs=specs or [whole] * len...  9.78 us
    ppermute x3, starting transfers between devices, on_device(): sibling = [lax.ppermute(w, 'expert', swap) for w in own]  6.24 us
    all_to_all x1, waiting for transfers between devices, exchange(): lax.all_to_all(chunks, 'expert', split_axis=0, concat_axis=0, tiled=True,...  5.88 us
    ppermute x1, waiting for transfers between devices, on_device(): return lax.ppermute(layer_out, 'segment', route).reshape(activations.shape)  3.96 us
    ppermute x1, starting transfers between devices, on_device(): return lax.ppermute(layer_out, 'segment', route).reshape(activations.shape)  3.4 us
  transfers between devices with their start and end apart: 5, of which 2 were waited for; matrix products, arithmetic and copies ran while one was open for 0% of the time, Pallas kernels for 0%

profile of v6, /device:TPU:8, one launch (start us, length us, event | category | flops | bytes accessed | tf_op | source)
XLA Modules:
  0.0 127.3 jit_solution(12704180034852963646)
XLA Ops:
  0.0 1.9 %shard_map.74 = bf16[8,16,2176]{2,1,0:T(8,128)(2,1)} custom-call(bf16[16,2048]{1,0:T(8,128)(2,1)} %bitcast.12, f32[1,2048]{1,0:T(1,128)} %refs_1_.1, s32[16,8]{1,0:T(8,128)} %bitcast.15, f32[16,8]{1,0:T(8,128)} %bitcast.16), custom_call_target="tpu_custom_call" | custom-call | tf_op jit(solution)/shard_map/pallas_call | solution.py:143
  1.9 9.9 %all-to-all-start = ((bf16[8,16,2176]{2,1,0:T(8,128)(2,1)}), bf16[8,16,2176]{2,1,0:T(8,128)(2,1)}, u32[]{:S(2)}, u32[]{:S(2)}) async-start(bf16[8,16,2176]{2,1,0:T(8,128)(2,1)} %shard_map.74), calls=%async_computation | async-start | bytes 1114112 | tf_op jit(solution)/shard_map/all_to_all | solution.py:22
  11.8 1.9 %collective-permute-start = (bf16[2048,384]{1,0:T(8,128)(2,1)}, bf16[2048,384]{1,0:T(8,128)(2,1)S(1)}, u32[]{:S(2)}, u32[]{:S(2)}) collective-permute-start(bf16[2048,384]{1,0:T(8,128)(2,1)} %bitcast.4.refs_0_), channel_id=1, source_target_pairs={{0,1},{1,0},{2,3},{3,2},{4,5},{5,4},{6,7},{7,6},{8,9},{9,8},{10,11... | collective-permute-start | bytes 4718600 | tf_op jit(solution)/shard_map/ppermute | solution.py:168
  13.7 2.4 %collective-permute-start.1 = (bf16[2048,384]{1,0:T(8,128)(2,1)}, bf16[2048,384]{1,0:T(8,128)(2,1)S(1)}, u32[]{:S(2)}, u32[]{:S(2)}) collective-permute-start(bf16[2048,384]{1,0:T(8,128)(2,1)} %bitcast.8), channel_id=1, source_target_pairs={{0,1},{1,0},{2,3},{3,2},{4,5},{5,4},{6,7},{7,6},{8,9},{9,8},{10,11... | collective-permute-start | bytes 4718600 | tf_op jit(solution)/shard_map/ppermute | solution.py:168
  16.1 1.9 %collective-permute-start.2 = (bf16[384,2048]{1,0:T(8,128)(2,1)}, bf16[384,2048]{1,0:T(8,128)(2,1)}, u32[]{:S(2)}, u32[]{:S(2)}) collective-permute-start(bf16[384,2048]{1,0:T(8,128)(2,1)} %bitcast.10), channel_id=1, source_target_pairs={{0,1},{1,0},{2,3},{3,2},{4,5},{5,4},{6,7},{7,6},{8,9},{9,8},{10,11... | collective-permute-start | bytes 4718600 | tf_op jit(solution)/shard_map/ppermute | solution.py:168
  18.1 0.2 shard_map.73.masks
  18.2 5.9 %all-to-all-done.gathered = bf16[8,16,2176]{2,1,0:T(8,128)(2,1)} async-done(((bf16[8,16,2176]{2,1,0:T(8,128)(2,1)}), bf16[8,16,2176]{2,1,0:T(8,128)(2,1)}, u32[]{:S(2)}, u32[]{:S(2)}) %all-to-all-start) | async-done | bytes 557088 | tf_op jit(solution)/shard_map/all_to_all | solution.py:22
  24.1 0.0 collective-permute-done.refs_0_.refs_3_
  24.1 0.0 collective-permute-done.1.refs_1_.refs_4_
  24.1 0.0 collective-permute-done.2.refs_2_.refs_5_
  24.1 1.8 %shard_map.75 = (bf16[8,64,2048]{2,1,0:T(8,128)(2,1)S(1)}, bf16[2,512,128]{2,1,0:T(8,128)(2,1)S(1)}) custom-call(bf16[2,512,128]{2,1,0:T(8,128)(2,1)S(1)} %shard_map.73.masks, bf16[8,16,2176]{2,1,0:T(8,128)(2,1)} %all-to-all-done.gathered, bf16[2048,384]{1,0:T(8,128)(2,1)S(1)} %collective-permute-done.refs_0_.refs_3_, ...), custom_call_target="tpu_custom_call" | custom-call | tf_op jit(solution)/shard_map/pallas_call | solution.py:143
  26.0 0.0 copy-start
  26.0 0.0 copy-start.1
  26.0 38.2 %all_to_all.20.rows = bf16[8,64,2048]{2,1,0:T(8,128)(2,1)S(1)} all-to-all(bf16[8,64,2048]{2,1,0:T(8,128)(2,1)S(1)} %get-tuple-element.7), channel_id=1, replica_groups={{0,16,32,48,64,80,96,112},{2,18,34,50,66,82,98,114},{4,20,36,52,68,84,1..., dimensions={0} | all-to-all | bytes 4194304 | tf_op jit(solution)/shard_map/all_to_all | solution.py:22
  64.2 0.0 copy-done
  64.2 0.0 copy-done.1
  64.2 5.1 %shard_map.76 = bf16[8,64,2048]{2,1,0:T(8,128)(2,1)S(1)} custom-call(bf16[8,64,2048]{2,1,0:T(8,128)(2,1)S(1)} %all_to_all.20.rows, bf16[2048,384]{1,0:T(8,128)(2,1)} %bitcast.4.refs_0_, bf16[2048,384]{1,0:T(8,128)(2,1)S(1)} %bitcast.9, bf16[384,2048]{1,0:T(8,128)(2,1)S(1)} %bitcast.11, bf16[2048,384]{1,0:T(8,128)(2,1)S(1)} %collective-permute-done.refs_0_.refs_3_, ...), custom_call_target="tpu_custom_call" | custom-call | flops 2415919104 | tf_op jit(solution)/shard_map/pallas_call | solution.py:143
  69.2 32.6 %all_to_all.21.returned = bf16[8,64,2048]{2,1,0:T(8,128)(2,1)S(1)} all-to-all(bf16[8,64,2048]{2,1,0:T(8,128)(2,1)S(1)} %shard_map.76), channel_id=1, replica_groups={{0,16,32,48,64,80,96,112},{2,18,34,50,66,82,98,114},{4,20,36,52,68,84,1..., dimensions={0} | all-to-all | bytes 4194304 | tf_op jit(solution)/shard_map/all_to_all | solution.py:22
  101.8 0.0 copy-start.2
  101.8 0.7 shard_map.77
  102.6 16.7 %all_to_all.22.pieces = bf16[8,16,2048]{2,1,0:T(8,128)(2,1)S(1)} all-to-all(bf16[8,16,2048]{2,1,0:T(8,128)(2,1)S(1)} %shard_map.77), channel_id=1, replica_groups={{0,2,4,6,8,10,12,14},{16,18,20,22,24,26,28,30},{32,34,36,38,40,42,44,46..., dimensions={0} | all-to-all | bytes 1048576 | tf_op jit(solution)/shard_map/all_to_all | solution.py:22
  119.2 0.0 copy-done.2
  119.2 0.1 shard_map.78
  119.3 3.4 %collective-permute-start.3 = (bf16[16,2048]{1,0:T(8,128)(2,1)S(1)}, bf16[16,2048]{1,0:T(8,128)(2,1)S(1)}, u32[]{:S(2)}, u32[]{:S(2)}) collective-permute-start(bf16[16,2048]{1,0:T(8,128)(2,1)S(1)} %shard_map.78), channel_id=1, source_target_pairs={{0,128},{128,256},{256,384},{384,0},{1,129},{129,257},{257,385},{3... | collective-permute-start | bytes 196616 | tf_op jit(solution)/shard_map/ppermute | solution.py:237
  122.7 4.0 %collective-permute-done.3 = bf16[16,2048]{1,0:T(8,128)(2,1)S(1)} collective-permute-done((bf16[16,2048]{1,0:T(8,128)(2,1)S(1)}, bf16[16,2048]{1,0:T(8,128)(2,1)S(1)}, u32[]{:S(2)}, u32[]{:S(2)}) %collective-permute-start.3) | collective-permute-done | bytes 65568 | tf_op jit(solution)/shard_map/ppermute | solution.py:237
  126.7 0.6 copy.15
Async XLA Ops:
  1.9 22.2 %all-to-all-start = ((bf16[8,16,2176]{2,1,0:T(8,128)(2,1)}), bf16[8,16,2176]{2,1,0:T(8,128)(2,1)}, u32[]{:S(2)}, u32[]{:S(2)}) async-start(bf16[8,16,2176]{2,1,0:T(8,128)(2,1)} %shard_map.74), calls=%async_computation | async-start | bytes 1114112 | tf_op jit(solution)/shard_map/all_to_all | solution.py:22
  11.8 12.3 %collective-permute-start = (bf16[2048,384]{1,0:T(8,128)(2,1)}, bf16[2048,384]{1,0:T(8,128)(2,1)S(1)}, u32[]{:S(2)}, u32[]{:S(2)}) collective-permute-start(bf16[2048,384]{1,0:T(8,128)(2,1)} %bitcast.4.refs_0_), channel_id=1, source_target_pairs={{0,1},{1,0},{2,3},{3,2},{4,5},{5,4},{6,7},{7,6},{8,9},{9,8},{10,11... | collective-permute-start | bytes 4718600 | tf_op jit(solution)/shard_map/ppermute | solution.py:168
  13.7 10.4 %collective-permute-start.1 = (bf16[2048,384]{1,0:T(8,128)(2,1)}, bf16[2048,384]{1,0:T(8,128)(2,1)S(1)}, u32[]{:S(2)}, u32[]{:S(2)}) collective-permute-start(bf16[2048,384]{1,0:T(8,128)(2,1)} %bitcast.8), channel_id=1, source_target_pairs={{0,1},{1,0},{2,3},{3,2},{4,5},{5,4},{6,7},{7,6},{8,9},{9,8},{10,11... | collective-permute-start | bytes 4718600 | tf_op jit(solution)/shard_map/ppermute | solution.py:168
  16.1 8.0 %collective-permute-start.2 = (bf16[384,2048]{1,0:T(8,128)(2,1)}, bf16[384,2048]{1,0:T(8,128)(2,1)}, u32[]{:S(2)}, u32[]{:S(2)}) collective-permute-start(bf16[384,2048]{1,0:T(8,128)(2,1)} %bitcast.10), channel_id=1, source_target_pairs={{0,1},{1,0},{2,3},{3,2},{4,5},{5,4},{6,7},{7,6},{8,9},{9,8},{10,11... | collective-permute-start | bytes 4718600 | tf_op jit(solution)/shard_map/ppermute | solution.py:168
  26.0 38.2 %copy-start = (bf16[1,1,2048,384]{3,2,1,0:T(8,128)(2,1)S(1)}, bf16[1,1,2048,384]{3,2,1,0:T(8,128)(2,1)}, u32[]{:S(2)}) copy-start(bf16[1,1,2048,384]{3,2,1,0:T(8,128)(2,1)} %param.10) | copy-start | bytes 4718596
  26.0 38.2 %copy-start.1 = (bf16[1,1,384,2048]{3,2,1,0:T(8,128)(2,1)S(1)}, bf16[1,1,384,2048]{3,2,1,0:T(8,128)(2,1)}, u32[]{:S(2)}) copy-start(bf16[1,1,384,2048]{3,2,1,0:T(8,128)(2,1)} %param.11) | copy-start | bytes 4718596
  101.8 17.4 %copy-start.2 = (bf16[1,2,8,2048]{3,2,1,0:T(8,128)(2,1)S(1)}, bf16[1,2,8,2048]{3,2,1,0:T(8,128)(2,1)}, u32[]{:S(2)}) copy-start(bf16[1,2,8,2048]{3,2,1,0:T(8,128)(2,1)} %param.7) | copy-start | bytes 196612
  119.3 7.4 %collective-permute-start.3 = (bf16[16,2048]{1,0:T(8,128)(2,1)S(1)}, bf16[16,2048]{1,0:T(8,128)(2,1)S(1)}, u32[]{:S(2)}, u32[]{:S(2)}) collective-permute-start(bf16[16,2048]{1,0:T(8,128)(2,1)S(1)} %shard_map.78), channel_id=1, source_target_pairs={{0,128},{128,256},{256,384},{384,0},{1,129},{129,257},{257,385},{3... | collective-permute-start | bytes 196616 | tf_op jit(solution)/shard_map/ppermute | solution.py:237

commit v7 on v6

--- a/solution.py
+++ b/solution.py
@@ -67,12 +67,14 @@
 
 
 def pack_kernel(masks, gathered, *refs):
-    out, blend, rows, parts, sems = refs[-5:]
+    gate_ref, _, _, down_ref, out, blend, gate_held, down_held, rows, parts, sems = refs
     width = out.shape[2]
     copies = [
         pltpu.make_async_copy(gathered.at[:, :, width:], parts, sems.at[0]),
         pltpu.make_async_copy(gathered.at[:, :, :width], rows, sems.at[1]),
     ]
+    copies.append(pltpu.make_async_copy(gate_ref, gate_held, sems.at[2]))
+    copies.append(pltpu.make_async_copy(down_ref, down_held, sems.at[3]))
     for copy in copies:
         copy.start()
     shape = masks.shape[1:]
@@ -96,30 +98,22 @@
     copies[1].wait()
     picked = dot(pick.astype(jnp.bfloat16), rows[...].reshape(-1, width))
     out[...] = picked.astype(jnp.bfloat16).reshape(out.shape)
+    copies[2].wait()
+    copies[3].wait()
 
 
 def expert_kernel(rows, *refs):
-    weights, out = list(refs[:6]), refs[6]
-    gate_own, down_sibling, sems = refs[7:]
-    copies = [
-        pltpu.make_async_copy(weights[0], gate_own, sems.at[0]),
-        pltpu.make_async_copy(weights[5], down_sibling, sems.at[1]),
-    ]
-    for copy in copies:
-        copy.start()
-    weights[0], weights[5] = gate_own, down_sibling
+    weights, out = refs[:6], refs[6]
     half = rows.shape[1] // 2
     hidden = []
     for e in range(2):
         x = rows[:, e * half : (e + 1) * half, :].reshape(-1, rows.shape[2])
-        up = dot(x, weights[3 * e + 1][...])
-        if e == 0:
-            copies[0].wait()
-        gate = dot(x, weights[3 * e][...])
+        gate_up = jnp.concatenate([weights[3 * e][0, 0], weights[3 * e + 1][0, 0]], axis=1)
+        both = dot(x, gate_up)
+        gate, up = jnp.split(both, 2, axis=1)
         hidden.append((gate / (1.0 + jnp.exp(-gate)) * up).astype(jnp.bfloat16))
-    copies[1].wait()
     for e in range(2):
-        answer = dot(hidden[e], weights[3 * e + 2][...]).astype(jnp.bfloat16)
+        answer = dot(hidden[e], weights[3 * e + 2][0, 0]).astype(jnp.bfloat16)
         out[:, e * half : (e + 1) * half, :] = answer.reshape(out.shape[0], half, out.shape[2])
 
 
@@ -163,7 +157,7 @@
     far = pl.BlockSpec(memory_space=pltpu.HBM)
     bf16 = jnp.bfloat16
 
-    own = [gate_weight[0, 0], up_weight[0, 0], down_weight[0, 0]]
+    own = [gate_weight, up_weight, down_weight]
     swap = [(i, i ^ 1) for i in range(lax.axis_size("expert"))]
     sibling = [lax.ppermute(w, "expert", swap) for w in own]
     tokens = activations.reshape(held, width)
@@ -190,38 +184,28 @@
         specs=[pl.BlockSpec(memory_space=pltpu.SMEM)],
         flops=20 * 10**9,
     )
-    outgoing, blend = kernel_call(
+    outgoing, blend, own[0], sibling[2] = kernel_call(
         pack_kernel,
         (
             jax.ShapeDtypeStruct((RING, slots, width), bf16),
             jax.ShapeDtypeStruct((2, RING * slots, RING * held), bf16),
+            pltpu.VMEM(gate_weight.shape, bf16),
+            pltpu.VMEM(down_weight.shape, bf16),
         ),
-        (masks, gathered, *sibling),
-        specs=[whole] + [far] * 4,
-        out_specs=(whole, whole),
+        (masks, gathered, own[0], *sibling),
+        specs=[whole] + [far] * 5,
+        out_specs=(whole,) * 4,
         scratch=[
             pltpu.VMEM((RING, held, width), bf16),
             pltpu.VMEM((RING, held, 128), bf16),
-            pltpu.SemaphoreType.DMA((2,)),
+            pltpu.SemaphoreType.DMA((4,)),
         ],
     )
     arrived = exchange(outgoing, deliver)
     answers = kernel_call(
         expert_kernel,
         jax.ShapeDtypeStruct((RING, slots, width), bf16),
-        (
-            arrived,
-            *[
-                pltpu.with_memory_space_constraint(w, pltpu.HBM if i in (0, 5) else pltpu.VMEM)
-                for i, w in enumerate(own + sibling)
-            ],
-        ),
-        specs=[whole] + [far if i in (0, 5) else whole for i in range(6)],
-        scratch=[
-            pltpu.VMEM((width, hidden_units), bf16),
-            pltpu.VMEM((hidden_units, width), bf16),
-            pltpu.SemaphoreType.DMA((2,)),
-        ],
+        (arrived, *[pltpu.with_memory_space_constraint(w, pltpu.VMEM) for w in own + sibling]),
         flops=6 * RING * slots * width * hidden_units,
     )
     returned = exchange(answers, deliver)

time: 128 us -> 126 us (0.984)
  Pallas kernels: 9.78 us -> 7.86 us
    pallas_call x6, Pallas kernels: 9.78 us -> 7.86 us  [kernel_call(): pl.pallas_call(body, out_shape=out_shape, in_specs=specs or [whole] * len...]
where the time goes in v7:
time: 126 us; the launch traced here: 125 us
  blocking collectives  87.4 us (69%)
  starting transfers between devices  19.5 us (15%)
  waiting for transfers between devices  9.85 us (8%)
  Pallas kernels  7.86 us (6%)
    all_to_all x3, blocking collectives, exchange(): lax.all_to_all(chunks, 'expert', split_axis=0, concat_axis=0, tiled=True,...  87.4 us
    all_to_all x1, starting transfers between devices, exchange(): lax.all_to_all(chunks, 'expert', split_axis=0, concat_axis=0, tiled=True,...  9.91 us
    pallas_call x6, Pallas kernels, kernel_call(): pl.pallas_call(body, out_shape=out_shape, in_specs=specs or [whole] * len...  7.86 us
    ppermute x3, starting transfers between devices, on_device(): sibling = [lax.ppermute(w, 'expert', swap) for w in own]  6.24 us
    all_to_all x1, waiting for transfers between devices, exchange(): lax.all_to_all(chunks, 'expert', split_axis=0, concat_axis=0, tiled=True,...  5.88 us
    ppermute x1, waiting for transfers between devices, on_device(): return lax.ppermute(layer_out, 'segment', route).reshape(activations.shape)  3.97 us
    ppermute x1, starting transfers between devices, on_device(): return lax.ppermute(layer_out, 'segment', route).reshape(activations.shape)  3.4 us
  transfers between devices with their start and end apart: 5, of which 2 were waited for; matrix products, arithmetic and copies ran while one was open for 0% of the time, Pallas kernels for 0%

profile of v7, /device:TPU:8, one launch (start us, length us, event | category | flops | bytes accessed | tf_op | source)
XLA Modules:
  0.0 125.4 jit_solution(13197960592602439865)
XLA Ops:
  0.0 1.9 %shard_map.74 = bf16[8,16,2176]{2,1,0:T(8,128)(2,1)} custom-call(bf16[16,2048]{1,0:T(8,128)(2,1)} %bitcast.5, f32[1,2048]{1,0:T(1,128)} %refs_1_.2, s32[16,8]{1,0:T(8,128)} %bitcast.8, f32[16,8]{1,0:T(8,128)} %bitcast.9), custom_call_target="tpu_custom_call" | custom-call | tf_op jit(solution)/shard_map/pallas_call | solution.py:137
  1.9 9.9 %all-to-all-start = ((bf16[8,16,2176]{2,1,0:T(8,128)(2,1)}), bf16[8,16,2176]{2,1,0:T(8,128)(2,1)}, u32[]{:S(2)}, u32[]{:S(2)}) async-start(bf16[8,16,2176]{2,1,0:T(8,128)(2,1)} %shard_map.74), calls=%async_computation | async-start | bytes 1114112 | tf_op jit(solution)/shard_map/all_to_all | solution.py:22
  11.8 1.9 %collective-permute-start = (bf16[1,1,2048,384]{3,2,1,0:T(8,128)(2,1)}, bf16[1,1,2048,384]{3,2,1,0:T(8,128)(2,1)S(1)}, u32[]{:S(2)}, u32[]{:S(2)}) collective-permute-start(bf16[1,1,2048,384]{3,2,1,0:T(8,128)(2,1)} %refs_0_.1), channel_id=1, source_target_pairs={{0,1},{1,0},{2,3},{3,2},{4,5},{5,4},{6,7},{7,6},{8,9},{9,8},{10,11... | collective-permute-start | bytes 4718600 | tf_op jit(solution)/shard_map/ppermute | solution.py:162
  13.7 2.4 %collective-permute-start.1 = (bf16[1,1,2048,384]{3,2,1,0:T(8,128)(2,1)}, bf16[1,1,2048,384]{3,2,1,0:T(8,128)(2,1)S(1)}, u32[]{:S(2)}, u32[]{:S(2)}) collective-permute-start(bf16[1,1,2048,384]{3,2,1,0:T(8,128)(2,1)} %refs_1_.3), channel_id=1, source_target_pairs={{0,1},{1,0},{2,3},{3,2},{4,5},{5,4},{6,7},{7,6},{8,9},{9,8},{10,11... | collective-permute-start | bytes 4718600 | tf_op jit(solution)/shard_map/ppermute | solution.py:162
  16.1 1.9 %collective-permute-start.2 = (bf16[1,1,384,2048]{3,2,1,0:T(8,128)(2,1)}, bf16[1,1,384,2048]{3,2,1,0:T(8,128)(2,1)}, u32[]{:S(2)}, u32[]{:S(2)}) collective-permute-start(bf16[1,1,384,2048]{3,2,1,0:T(8,128)(2,1)} %refs_2_.1), channel_id=1, source_target_pairs={{0,1},{1,0},{2,3},{3,2},{4,5},{5,4},{6,7},{7,6},{8,9},{9,8},{10,11... | collective-permute-start | bytes 4718600 | tf_op jit(solution)/shard_map/ppermute | solution.py:162
  18.1 0.2 shard_map.73.masks
  18.2 5.9 %all-to-all-done.gathered = bf16[8,16,2176]{2,1,0:T(8,128)(2,1)} async-done(((bf16[8,16,2176]{2,1,0:T(8,128)(2,1)}), bf16[8,16,2176]{2,1,0:T(8,128)(2,1)}, u32[]{:S(2)}, u32[]{:S(2)}) %all-to-all-start) | async-done | bytes 557088 | tf_op jit(solution)/shard_map/all_to_all | solution.py:22
  24.1 0.0 collective-permute-done.refs_1_.refs_3_
  24.1 0.0 collective-permute-done.1.refs_2_.refs_4_
  24.1 0.0 collective-permute-done.2.refs_3_
  24.1 2.1 %shard_map.75 = (bf16[8,64,2048]{2,1,0:T(8,128)(2,1)S(1)}, bf16[2,512,128]{2,1,0:T(8,128)(2,1)S(1)}, bf16[1,1,2048,384]{3,2,1,0:T(8,128)(2,1)S(1)}, bf16[1,1,384,2048]{3,2,1,0:T(8,128)(2,1)S(1)}) custom-call(bf16[2,512,128]{2,1,0:T(8,128)(2,1)S(1)} %shard_map.73.masks, bf16[8,16,2176]{2,1,0:T(8,128)(2,1)} %all-to-all-done.gathered, ...), custom_call_target="tpu_custom_call" | custom-call | tf_op jit(solution)/shard_map/pallas_call | solution.py:137
  26.2 0.0 copy-start
  26.3 0.0 copy-start.1
  26.3 38.1 %all_to_all.20.rows = bf16[8,64,2048]{2,1,0:T(8,128)(2,1)S(1)} all-to-all(bf16[8,64,2048]{2,1,0:T(8,128)(2,1)S(1)} %get-tuple-element.9), channel_id=1, replica_groups={{0,16,32,48,64,80,96,112},{2,18,34,50,66,82,98,114},{4,20,36,52,68,84,1..., dimensions={0} | all-to-all | bytes 4194304 | tf_op jit(solution)/shard_map/all_to_all | solution.py:22
  64.4 0.0 copy-done
  64.4 0.0 copy-done.1
  64.4 2.9 %shard_map.76 = bf16[8,64,2048]{2,1,0:T(8,128)(2,1)S(1)} custom-call(bf16[8,64,2048]{2,1,0:T(8,128)(2,1)S(1)} %all_to_all.20.rows, bf16[1,1,2048,384]{3,2,1,0:T(8,128)(2,1)S(1)} %get-tuple-element.10.refs_0_, bf16[1,1,2048,384]{3,2,1,0:T(8,128)(2,1)S(1)} %copy-done, bf16[1,1,384,2048]{3,2,1,0:T(8,128)(2,1)S(1)} %copy-done.1, ...), custom_call_target="tpu_custom_call" | custom-call | flops 2415919104 | tf_op jit(solution)/shard_map/pallas_call | solution.py:137
  67.3 32.6 %all_to_all.21.returned = bf16[8,64,2048]{2,1,0:T(8,128)(2,1)S(1)} all-to-all(bf16[8,64,2048]{2,1,0:T(8,128)(2,1)S(1)} %shard_map.76), channel_id=1, replica_groups={{0,16,32,48,64,80,96,112},{2,18,34,50,66,82,98,114},{4,20,36,52,68,84,1..., dimensions={0} | all-to-all | bytes 4194304 | tf_op jit(solution)/shard_map/all_to_all | solution.py:22
  99.9 0.0 copy-start.2
  99.9 0.7 shard_map.77
  100.6 16.7 %all_to_all.22.pieces = bf16[8,16,2048]{2,1,0:T(8,128)(2,1)S(1)} all-to-all(bf16[8,16,2048]{2,1,0:T(8,128)(2,1)S(1)} %shard_map.77), channel_id=1, replica_groups={{0,2,4,6,8,10,12,14},{16,18,20,22,24,26,28,30},{32,34,36,38,40,42,44,46..., dimensions={0} | all-to-all | bytes 1048576 | tf_op jit(solution)/shard_map/all_to_all | solution.py:22
  117.3 0.0 copy-done.2
  117.3 0.1 shard_map.78
  117.4 3.4 %collective-permute-start.3 = (bf16[16,2048]{1,0:T(8,128)(2,1)S(1)}, bf16[16,2048]{1,0:T(8,128)(2,1)S(1)}, u32[]{:S(2)}, u32[]{:S(2)}) collective-permute-start(bf16[16,2048]{1,0:T(8,128)(2,1)S(1)} %shard_map.78), channel_id=1, source_target_pairs={{0,128},{128,256},{256,384},{384,0},{1,129},{129,257},{257,385},{3... | collective-permute-start | bytes 196616 | tf_op jit(solution)/shard_map/ppermute | solution.py:221
  120.8 4.0 %collective-permute-done.3 = bf16[16,2048]{1,0:T(8,128)(2,1)S(1)} collective-permute-done((bf16[16,2048]{1,0:T(8,128)(2,1)S(1)}, bf16[16,2048]{1,0:T(8,128)(2,1)S(1)}, u32[]{:S(2)}, u32[]{:S(2)}) %collective-permute-start.3) | collective-permute-done | bytes 65568 | tf_op jit(solution)/shard_map/ppermute | solution.py:221
  124.8 0.6 copy.15
Async XLA Ops:
  1.9 22.2 %all-to-all-start = ((bf16[8,16,2176]{2,1,0:T(8,128)(2,1)}), bf16[8,16,2176]{2,1,0:T(8,128)(2,1)}, u32[]{:S(2)}, u32[]{:S(2)}) async-start(bf16[8,16,2176]{2,1,0:T(8,128)(2,1)} %shard_map.74), calls=%async_computation | async-start | bytes 1114112 | tf_op jit(solution)/shard_map/all_to_all | solution.py:22
  11.8 12.3 %collective-permute-start = (bf16[1,1,2048,384]{3,2,1,0:T(8,128)(2,1)}, bf16[1,1,2048,384]{3,2,1,0:T(8,128)(2,1)S(1)}, u32[]{:S(2)}, u32[]{:S(2)}) collective-permute-start(bf16[1,1,2048,384]{3,2,1,0:T(8,128)(2,1)} %refs_0_.1), channel_id=1, source_target_pairs={{0,1},{1,0},{2,3},{3,2},{4,5},{5,4},{6,7},{7,6},{8,9},{9,8},{10,11... | collective-permute-start | bytes 4718600 | tf_op jit(solution)/shard_map/ppermute | solution.py:162
  13.7 10.4 %collective-permute-start.1 = (bf16[1,1,2048,384]{3,2,1,0:T(8,128)(2,1)}, bf16[1,1,2048,384]{3,2,1,0:T(8,128)(2,1)S(1)}, u32[]{:S(2)}, u32[]{:S(2)}) collective-permute-start(bf16[1,1,2048,384]{3,2,1,0:T(8,128)(2,1)} %refs_1_.3), channel_id=1, source_target_pairs={{0,1},{1,0},{2,3},{3,2},{4,5},{5,4},{6,7},{7,6},{8,9},{9,8},{10,11... | collective-permute-start | bytes 4718600 | tf_op jit(solution)/shard_map/ppermute | solution.py:162
  16.1 8.0 %collective-permute-start.2 = (bf16[1,1,384,2048]{3,2,1,0:T(8,128)(2,1)}, bf16[1,1,384,2048]{3,2,1,0:T(8,128)(2,1)}, u32[]{:S(2)}, u32[]{:S(2)}) collective-permute-start(bf16[1,1,384,2048]{3,2,1,0:T(8,128)(2,1)} %refs_2_.1), channel_id=1, source_target_pairs={{0,1},{1,0},{2,3},{3,2},{4,5},{5,4},{6,7},{7,6},{8,9},{9,8},{10,11... | collective-permute-start | bytes 4718600 | tf_op jit(solution)/shard_map/ppermute | solution.py:162
  26.2 38.2 %copy-start = (bf16[1,1,2048,384]{3,2,1,0:T(8,128)(2,1)S(1)}, bf16[1,1,2048,384]{3,2,1,0:T(8,128)(2,1)}, u32[]{:S(2)}) copy-start(bf16[1,1,2048,384]{3,2,1,0:T(8,128)(2,1)} %refs_1_.3) | copy-start | bytes 4718596
  26.3 38.2 %copy-start.1 = (bf16[1,1,384,2048]{3,2,1,0:T(8,128)(2,1)S(1)}, bf16[1,1,384,2048]{3,2,1,0:T(8,128)(2,1)}, u32[]{:S(2)}) copy-start(bf16[1,1,384,2048]{3,2,1,0:T(8,128)(2,1)} %refs_2_.1) | copy-start | bytes 4718596
  99.9 17.4 %copy-start.2 = (bf16[1,2,8,2048]{3,2,1,0:T(8,128)(2,1)S(1)}, bf16[1,2,8,2048]{3,2,1,0:T(8,128)(2,1)}, u32[]{:S(2)}) copy-start(bf16[1,2,8,2048]{3,2,1,0:T(8,128)(2,1)} %param.7) | copy-start | bytes 196612
  117.4 7.4 %collective-permute-start.3 = (bf16[16,2048]{1,0:T(8,128)(2,1)S(1)}, bf16[16,2048]{1,0:T(8,128)(2,1)S(1)}, u32[]{:S(2)}, u32[]{:S(2)}) collective-permute-start(bf16[16,2048]{1,0:T(8,128)(2,1)S(1)} %shard_map.78), channel_id=1, source_target_pairs={{0,128},{128,256},{256,384},{384,0},{1,129},{129,257},{257,385},{3... | collective-permute-start | bytes 196616 | tf_op jit(solution)/shard_map/ppermute | solution.py:221

commit v8 on v7

--- a/solution.py
+++ b/solution.py
@@ -60,7 +60,7 @@
     row = lax.broadcasted_iota(jnp.int32, shape, 0)
     lane = lax.broadcasted_iota(jnp.int32, shape, 1)
     member, other = row >> 6, (row >> 5) & 1
-    chip = jnp.where(core == 0, (member & 3) * RING + y, (z % 4) * RING + member)
+    chip = jnp.where(core == 0, (z % 4) * RING + member, (member & 3) * RING + y)
     expert = chip * 2 + (other ^ core)
     masks[0] = (lane == expert).astype(jnp.bfloat16)
     masks[1] = (lane == expert + 64).astype(jnp.bfloat16)
@@ -152,7 +152,7 @@
     hidden_units = gate_weight.shape[3]
     held = micro * block_tokens
     slots = RING * micro * 2 * CAP
-    spread, deliver = ring_groups("y"), ring_groups("z")
+    spread, deliver = ring_groups("z"), ring_groups("y")
     whole = pl.BlockSpec(memory_space=pltpu.VMEM)
     far = pl.BlockSpec(memory_space=pltpu.HBM)
     bf16 = jnp.bfloat16

time: 126 us -> 126 us (level)
  blocking collectives: 87.4 us -> 85.5 us
  waiting for transfers between devices: 9.85 us -> 11.3 us
    all_to_all x3, blocking collectives: 87.4 us -> 85.5 us  [exchange(): lax.all_to_all(chunks, 'expert', split_axis=0, concat_axis=0, tiled=True,...]
    all_to_all x1, waiting for transfers between devices: 5.88 us -> 7.31 us  [exchange(): lax.all_to_all(chunks, 'expert', split_axis=0, concat_axis=0, tiled=True,...]
where the time goes in v8:
time: 126 us; the launch traced here: 125 us
  blocking collectives  85.5 us (68%)
  starting transfers between devices  20 us (16%)
  waiting for transfers between devices  11.3 us (9%)
  Pallas kernels  7.85 us (6%)
    all_to_all x3, blocking collectives, exchange(): lax.all_to_all(chunks, 'expert', split_axis=0, concat_axis=0, tiled=True,...  85.5 us
    all_to_all x1, starting transfers between devices, exchange(): lax.all_to_all(chunks, 'expert', split_axis=0, concat_axis=0, tiled=True,...  10.3 us
    pallas_call x6, Pallas kernels, kernel_call(): pl.pallas_call(body, out_shape=out_shape, in_specs=specs or [whole] * len...  7.85 us
    all_to_all x1, waiting for transfers between devices, exchange(): lax.all_to_all(chunks, 'expert', split_axis=0, concat_axis=0, tiled=True,...  7.31 us
    ppermute x3, starting transfers between devices, on_device(): sibling = [lax.ppermute(w, 'expert', swap) for w in own]  6.24 us
    ppermute x1, waiting for transfers between devices, on_device(): return lax.ppermute(layer_out, 'segment', route).reshape(activations.shape)  3.96 us
    ppermute x1, starting transfers between devices, on_device(): return lax.ppermute(layer_out, 'segment', route).reshape(activations.shape)  3.4 us
  transfers between devices with their start and end apart: 5, of which 2 were waited for; matrix products, arithmetic and copies ran while one was open for 0% of the time, Pallas kernels for 0%

profile of v8, /device:TPU:8, one launch (start us, length us, event | category | flops | bytes accessed | tf_op | source)
XLA Modules:
  0.0 125.4 jit_solution(9499897878379522444)
XLA Ops:
  0.0 1.9 %shard_map.74 = bf16[8,16,2176]{2,1,0:T(8,128)(2,1)} custom-call(bf16[16,2048]{1,0:T(8,128)(2,1)} %bitcast.5, f32[1,2048]{1,0:T(1,128)} %refs_1_.2, s32[16,8]{1,0:T(8,128)} %bitcast.8, f32[16,8]{1,0:T(8,128)} %bitcast.9), custom_call_target="tpu_custom_call" | custom-call | tf_op jit(solution)/shard_map/pallas_call | solution.py:137
  1.9 10.3 %all-to-all-start = ((bf16[8,16,2176]{2,1,0:T(8,128)(2,1)}), bf16[8,16,2176]{2,1,0:T(8,128)(2,1)}, u32[]{:S(2)}, u32[]{:S(2)}) async-start(bf16[8,16,2176]{2,1,0:T(8,128)(2,1)} %shard_map.74), calls=%async_computation | async-start | bytes 1114112 | tf_op jit(solution)/shard_map/all_to_all | solution.py:22
  12.2 1.9 %collective-permute-start = (bf16[1,1,2048,384]{3,2,1,0:T(8,128)(2,1)}, bf16[1,1,2048,384]{3,2,1,0:T(8,128)(2,1)S(1)}, u32[]{:S(2)}, u32[]{:S(2)}) collective-permute-start(bf16[1,1,2048,384]{3,2,1,0:T(8,128)(2,1)} %refs_0_.1), channel_id=1, source_target_pairs={{0,1},{1,0},{2,3},{3,2},{4,5},{5,4},{6,7},{7,6},{8,9},{9,8},{10,11... | collective-permute-start | bytes 4718600 | tf_op jit(solution)/shard_map/ppermute | solution.py:162
  14.1 2.4 %collective-permute-start.1 = (bf16[1,1,2048,384]{3,2,1,0:T(8,128)(2,1)}, bf16[1,1,2048,384]{3,2,1,0:T(8,128)(2,1)S(1)}, u32[]{:S(2)}, u32[]{:S(2)}) collective-permute-start(bf16[1,1,2048,384]{3,2,1,0:T(8,128)(2,1)} %refs_1_.3), channel_id=1, source_target_pairs={{0,1},{1,0},{2,3},{3,2},{4,5},{5,4},{6,7},{7,6},{8,9},{9,8},{10,11... | collective-permute-start | bytes 4718600 | tf_op jit(solution)/shard_map/ppermute | solution.py:162
  16.6 1.9 %collective-permute-start.2 = (bf16[1,1,384,2048]{3,2,1,0:T(8,128)(2,1)}, bf16[1,1,384,2048]{3,2,1,0:T(8,128)(2,1)}, u32[]{:S(2)}, u32[]{:S(2)}) collective-permute-start(bf16[1,1,384,2048]{3,2,1,0:T(8,128)(2,1)} %refs_2_.1), channel_id=1, source_target_pairs={{0,1},{1,0},{2,3},{3,2},{4,5},{5,4},{6,7},{7,6},{8,9},{9,8},{10,11... | collective-permute-start | bytes 4718600 | tf_op jit(solution)/shard_map/ppermute | solution.py:162
  18.5 0.2 shard_map.73.masks
  18.7 7.3 %all-to-all-done.gathered = bf16[8,16,2176]{2,1,0:T(8,128)(2,1)} async-done(((bf16[8,16,2176]{2,1,0:T(8,128)(2,1)}), bf16[8,16,2176]{2,1,0:T(8,128)(2,1)}, u32[]{:S(2)}, u32[]{:S(2)}) %all-to-all-start) | async-done | bytes 557088 | tf_op jit(solution)/shard_map/all_to_all | solution.py:22
  26.0 0.0 collective-permute-done.refs_1_.refs_3_
  26.0 0.0 collective-permute-done.1.refs_2_.refs_4_
  26.0 0.0 collective-permute-done.2.refs_3_
  26.0 2.1 %shard_map.75 = (bf16[8,64,2048]{2,1,0:T(8,128)(2,1)S(1)}, bf16[2,512,128]{2,1,0:T(8,128)(2,1)S(1)}, bf16[1,1,2048,384]{3,2,1,0:T(8,128)(2,1)S(1)}, bf16[1,1,384,2048]{3,2,1,0:T(8,128)(2,1)S(1)}) custom-call(bf16[2,512,128]{2,1,0:T(8,128)(2,1)S(1)} %shard_map.73.masks, bf16[8,16,2176]{2,1,0:T(8,128)(2,1)} %all-to-all-done.gathered, ...), custom_call_target="tpu_custom_call" | custom-call | tf_op jit(solution)/shard_map/pallas_call | solution.py:137
  28.1 0.0 copy-start
  28.1 0.0 copy-start.1
  28.1 36.3 %all_to_all.20.rows = bf16[8,64,2048]{2,1,0:T(8,128)(2,1)S(1)} all-to-all(bf16[8,64,2048]{2,1,0:T(8,128)(2,1)S(1)} %get-tuple-element.9), channel_id=1, replica_groups={{0,2,4,6,8,10,12,14},{16,18,20,22,24,26,28,30},{32,34,36,38,40,42,44,46..., dimensions={0} | all-to-all | bytes 4194304 | tf_op jit(solution)/shard_map/all_to_all | solution.py:22
  64.4 0.0 copy-done
  64.4 0.0 copy-done.1
  64.4 2.9 %shard_map.76 = bf16[8,64,2048]{2,1,0:T(8,128)(2,1)S(1)} custom-call(bf16[8,64,2048]{2,1,0:T(8,128)(2,1)S(1)} %all_to_all.20.rows, bf16[1,1,2048,384]{3,2,1,0:T(8,128)(2,1)S(1)} %get-tuple-element.10.refs_0_, bf16[1,1,2048,384]{3,2,1,0:T(8,128)(2,1)S(1)} %copy-done, bf16[1,1,384,2048]{3,2,1,0:T(8,128)(2,1)S(1)} %copy-done.1, ...), custom_call_target="tpu_custom_call" | custom-call | flops 2415919104 | tf_op jit(solution)/shard_map/pallas_call | solution.py:137
  67.3 32.6 %all_to_all.21.returned = bf16[8,64,2048]{2,1,0:T(8,128)(2,1)S(1)} all-to-all(bf16[8,64,2048]{2,1,0:T(8,128)(2,1)S(1)} %shard_map.76), channel_id=1, replica_groups={{0,2,4,6,8,10,12,14},{16,18,20,22,24,26,28,30},{32,34,36,38,40,42,44,46..., dimensions={0} | all-to-all | bytes 4194304 | tf_op jit(solution)/shard_map/all_to_all | solution.py:22
  99.9 0.0 copy-start.2
  99.9 0.7 shard_map.77
  100.6 16.7 %all_to_all.22.pieces = bf16[8,16,2048]{2,1,0:T(8,128)(2,1)S(1)} all-to-all(bf16[8,16,2048]{2,1,0:T(8,128)(2,1)S(1)} %shard_map.77), channel_id=1, replica_groups={{0,16,32,48,64,80,96,112},{2,18,34,50,66,82,98,114},{4,20,36,52,68,84,1..., dimensions={0} | all-to-all | bytes 1048576 | tf_op jit(solution)/shard_map/all_to_all | solution.py:22
  117.3 0.0 copy-done.2
  117.3 0.1 shard_map.78
  117.4 3.4 %collective-permute-start.3 = (bf16[16,2048]{1,0:T(8,128)(2,1)S(1)}, bf16[16,2048]{1,0:T(8,128)(2,1)S(1)}, u32[]{:S(2)}, u32[]{:S(2)}) collective-permute-start(bf16[16,2048]{1,0:T(8,128)(2,1)S(1)} %shard_map.78), channel_id=1, source_target_pairs={{0,128},{128,256},{256,384},{384,0},{1,129},{129,257},{257,385},{3... | collective-permute-start | bytes 196616 | tf_op jit(solution)/shard_map/ppermute | solution.py:221
  120.8 4.0 %collective-permute-done.3 = bf16[16,2048]{1,0:T(8,128)(2,1)S(1)} collective-permute-done((bf16[16,2048]{1,0:T(8,128)(2,1)S(1)}, bf16[16,2048]{1,0:T(8,128)(2,1)S(1)}, u32[]{:S(2)}, u32[]{:S(2)}) %collective-permute-start.3) | collective-permute-done | bytes 65568 | tf_op jit(solution)/shard_map/ppermute | solution.py:221
  124.8 0.6 copy.15
Async XLA Ops:
  1.9 24.1 %all-to-all-start = ((bf16[8,16,2176]{2,1,0:T(8,128)(2,1)}), bf16[8,16,2176]{2,1,0:T(8,128)(2,1)}, u32[]{:S(2)}, u32[]{:S(2)}) async-start(bf16[8,16,2176]{2,1,0:T(8,128)(2,1)} %shard_map.74), calls=%async_computation | async-start | bytes 1114112 | tf_op jit(solution)/shard_map/all_to_all | solution.py:22
  12.2 13.8 %collective-permute-start = (bf16[1,1,2048,384]{3,2,1,0:T(8,128)(2,1)}, bf16[1,1,2048,384]{3,2,1,0:T(8,128)(2,1)S(1)}, u32[]{:S(2)}, u32[]{:S(2)}) collective-permute-start(bf16[1,1,2048,384]{3,2,1,0:T(8,128)(2,1)} %refs_0_.1), channel_id=1, source_target_pairs={{0,1},{1,0},{2,3},{3,2},{4,5},{5,4},{6,7},{7,6},{8,9},{9,8},{10,11... | collective-permute-start | bytes 4718600 | tf_op jit(solution)/shard_map/ppermute | solution.py:162
  14.1 11.8 %collective-permute-start.1 = (bf16[1,1,2048,384]{3,2,1,0:T(8,128)(2,1)}, bf16[1,1,2048,384]{3,2,1,0:T(8,128)(2,1)S(1)}, u32[]{:S(2)}, u32[]{:S(2)}) collective-permute-start(bf16[1,1,2048,384]{3,2,1,0:T(8,128)(2,1)} %refs_1_.3), channel_id=1, source_target_pairs={{0,1},{1,0},{2,3},{3,2},{4,5},{5,4},{6,7},{7,6},{8,9},{9,8},{10,11... | collective-permute-start | bytes 4718600 | tf_op jit(solution)/shard_map/ppermute | solution.py:162
  16.6 9.4 %collective-permute-start.2 = (bf16[1,1,384,2048]{3,2,1,0:T(8,128)(2,1)}, bf16[1,1,384,2048]{3,2,1,0:T(8,128)(2,1)}, u32[]{:S(2)}, u32[]{:S(2)}) collective-permute-start(bf16[1,1,384,2048]{3,2,1,0:T(8,128)(2,1)} %refs_2_.1), channel_id=1, source_target_pairs={{0,1},{1,0},{2,3},{3,2},{4,5},{5,4},{6,7},{7,6},{8,9},{9,8},{10,11... | collective-permute-start | bytes 4718600 | tf_op jit(solution)/shard_map/ppermute | solution.py:162
  28.1 36.3 %copy-start = (bf16[1,1,2048,384]{3,2,1,0:T(8,128)(2,1)S(1)}, bf16[1,1,2048,384]{3,2,1,0:T(8,128)(2,1)}, u32[]{:S(2)}) copy-start(bf16[1,1,2048,384]{3,2,1,0:T(8,128)(2,1)} %refs_1_.3) | copy-start | bytes 4718596
  28.1 36.3 %copy-start.1 = (bf16[1,1,384,2048]{3,2,1,0:T(8,128)(2,1)S(1)}, bf16[1,1,384,2048]{3,2,1,0:T(8,128)(2,1)}, u32[]{:S(2)}) copy-start(bf16[1,1,384,2048]{3,2,1,0:T(8,128)(2,1)} %refs_2_.1) | copy-start | bytes 4718596
  99.9 17.4 %copy-start.2 = (bf16[1,2,8,2048]{3,2,1,0:T(8,128)(2,1)S(1)}, bf16[1,2,8,2048]{3,2,1,0:T(8,128)(2,1)}, u32[]{:S(2)}) copy-start(bf16[1,2,8,2048]{3,2,1,0:T(8,128)(2,1)} %param.7) | copy-start | bytes 196612
  117.4 7.4 %collective-permute-start.3 = (bf16[16,2048]{1,0:T(8,128)(2,1)S(1)}, bf16[16,2048]{1,0:T(8,128)(2,1)S(1)}, u32[]{:S(2)}, u32[]{:S(2)}) collective-permute-start(bf16[16,2048]{1,0:T(8,128)(2,1)S(1)} %shard_map.78), channel_id=1, source_target_pairs={{0,128},{128,256},{256,384},{384,0},{1,129},{129,257},{257,385},{3... | collective-permute-start | bytes 196616 | tf_op jit(solution)/shard_map/ppermute | solution.py:221

commit v9 on v8

--- a/solution.py
+++ b/solution.py
@@ -53,7 +53,29 @@
         copy.wait()
 
 
-def mask_kernel(place, masks):
+def weight_parts(gate, up, down, buffer):
+    width, hidden_units = gate.shape
+    lanes = 2 * hidden_units
+    parts = [
+        (gate, buffer.at[:width, :hidden_units]),
+        (up, buffer.at[:width, hidden_units:]),
+    ]
+    for k in range(pl.cdiv(width, lanes)):
+        size = min(lanes, width - k * lanes)
+        rows = pl.ds(width + k * hidden_units, hidden_units)
+        parts.append((down.at[:, k * lanes : k * lanes + size], buffer.at[rows, :size]))
+    return parts
+
+
+def mask_kernel(place, gate_ref, up_ref, down_ref, masks, buffer, sems):
+    parts = weight_parts(gate_ref.at[0, 0], up_ref.at[0, 0], down_ref.at[0, 0], buffer)
+    hidden_units = down_ref.shape[2]
+    used = parts[-1][1].shape[1]
+    tail = buffer.at[buffer.shape[0] - hidden_units :, used:]
+    parts.append((down_ref.at[0, 0, :, : tail.shape[1]], tail))
+    copies = [pltpu.make_async_copy(a, b, sems.at[i]) for i, (a, b) in enumerate(parts)]
+    for copy in copies:
+        copy.start()
     mine = place[0]
     z, y, core = mine // 16, (mine // 2) % RING, mine % 2
     shape = masks.shape[1:]
@@ -64,19 +86,15 @@
     expert = chip * 2 + (other ^ core)
     masks[0] = (lane == expert).astype(jnp.bfloat16)
     masks[1] = (lane == expert + 64).astype(jnp.bfloat16)
-
-
-def pack_kernel(masks, gathered, *refs):
-    gate_ref, _, _, down_ref, out, blend, gate_held, down_held, rows, parts, sems = refs
+    for copy in copies:
+        copy.wait()
+
+
+def pack_kernel(masks, gathered, gate_ref, out, blend, gate_held, sem):
+    copy = pltpu.make_async_copy(gate_ref, gate_held, sem)
+    copy.start()
+    tokens = gathered.shape[0] * gathered.shape[1]
     width = out.shape[2]
-    copies = [
-        pltpu.make_async_copy(gathered.at[:, :, width:], parts, sems.at[0]),
-        pltpu.make_async_copy(gathered.at[:, :, :width], rows, sems.at[1]),
-    ]
-    copies.append(pltpu.make_async_copy(gate_ref, gate_held, sems.at[2]))
-    copies.append(pltpu.make_async_copy(down_ref, down_held, sems.at[3]))
-    for copy in copies:
-        copy.start()
     shape = masks.shape[1:]
     row = lax.broadcasted_iota(jnp.int32, shape, 0)
     lane = lax.broadcasted_iota(jnp.int32, shape, 1)
@@ -86,35 +104,44 @@
         lax.broadcasted_iota(jnp.int32, (128, 128), 0)
         < lax.broadcasted_iota(jnp.int32, (128, 128), 1)
     ).astype(jnp.bfloat16)
-    copies[0].wait()
-    weight_parts = parts[...].reshape(-1, 128)
-    high = dot(masks[0], weight_parts, ((1,), (1,)))
-    low = dot(masks[1], weight_parts, ((1,), (1,)))
+    parts = gathered[:, :, width:].reshape(tokens, 128)
+    high = dot(masks[0], parts, ((1,), (1,)))
+    low = dot(masks[1], parts, ((1,), (1,)))
     named = jnp.where((high != 0.0) & same_block, 1.0, 0.0)
     earlier = dot(named.astype(jnp.bfloat16), before)
     pick = jnp.where(earlier == rank, named, 0.0)
     blend[0] = (pick * high).astype(jnp.bfloat16)
     blend[1] = (pick * low).astype(jnp.bfloat16)
-    copies[1].wait()
-    picked = dot(pick.astype(jnp.bfloat16), rows[...].reshape(-1, width))
+    picked = dot(pick.astype(jnp.bfloat16), gathered[:, :, :width].reshape(tokens, width))
     out[...] = picked.astype(jnp.bfloat16).reshape(out.shape)
-    copies[2].wait()
-    copies[3].wait()
-
-
-def expert_kernel(rows, *refs):
-    weights, out = refs[:6], refs[6]
+    copy.wait()
+
+
+def expert_kernel(rows, gate_ref, up_ref, down_ref, swapped, out, gate_up, down, sems):
+    hidden_units = down.shape[0]
+    parts = weight_parts(gate_up.at[:, :hidden_units], gate_up.at[:, hidden_units:], down, swapped)
+    copies = [pltpu.make_async_copy(b, a, sems.at[i]) for i, (a, b) in enumerate(parts)]
+    for copy in copies:
+        copy.start()
     half = rows.shape[1] // 2
-    hidden = []
-    for e in range(2):
+
+    def hidden_rows(e, weight):
         x = rows[:, e * half : (e + 1) * half, :].reshape(-1, rows.shape[2])
-        gate_up = jnp.concatenate([weights[3 * e][0, 0], weights[3 * e + 1][0, 0]], axis=1)
-        both = dot(x, gate_up)
-        gate, up = jnp.split(both, 2, axis=1)
-        hidden.append((gate / (1.0 + jnp.exp(-gate)) * up).astype(jnp.bfloat16))
-    for e in range(2):
-        answer = dot(hidden[e], weights[3 * e + 2][0, 0]).astype(jnp.bfloat16)
+        gate, up = jnp.split(dot(x, weight), 2, axis=1)
+        return (gate / (1.0 + jnp.exp(-gate)) * up).astype(jnp.bfloat16)
+
+    def finish(e, hidden, weight):
+        answer = dot(hidden, weight).astype(jnp.bfloat16)
         out[:, e * half : (e + 1) * half, :] = answer.reshape(out.shape[0], half, out.shape[2])
+
+    own = hidden_rows(0, jnp.concatenate([gate_ref[0, 0], up_ref[0, 0]], axis=1))
+    finish(0, own, down_ref[0, 0])
+    for copy in copies[:2]:
+        copy.wait()
+    sibling = hidden_rows(1, gate_up[...])
+    for copy in copies[2:]:
+        copy.wait()
+    finish(1, sibling, down[...])
 
 
 def mix_kernel(returned, blend, out):
@@ -159,7 +186,6 @@
 
     own = [gate_weight, up_weight, down_weight]
     swap = [(i, i ^ 1) for i in range(lax.axis_size("expert"))]
-    sibling = [lax.ppermute(w, "expert", swap) for w in own]
     tokens = activations.reshape(held, width)
     inputs = (tokens, norm_gain, expert_ids.reshape(held, -1), route_weights.reshape(held, -1))
     payload = kernel_call(
@@ -177,35 +203,48 @@
     )
     gathered = exchange(payload, spread)
     place = lax.axis_index("expert").astype(jnp.int32).reshape(1)
-    masks = kernel_call(
+    lanes = 2 * hidden_units
+    masks, buffer = kernel_call(
         mask_kernel,
-        jax.ShapeDtypeStruct((2, RING * slots, RING * held), bf16),
-        (place,),
-        specs=[pl.BlockSpec(memory_space=pltpu.SMEM)],
+        (
+            jax.ShapeDtypeStruct((2, RING * slots, RING * held), bf16),
+            pltpu.HBM((width + pl.cdiv(width, lanes) * hidden_units, lanes), bf16),
+        ),
+        (place, *[pltpu.with_memory_space_constraint(w, pltpu.HBM) for w in own]),
+        specs=[pl.BlockSpec(memory_space=pltpu.SMEM)] + [far] * 3,
+        out_specs=(whole, far),
+        scratch=[pltpu.SemaphoreType.DMA((8,))],
         flops=20 * 10**9,
     )
-    outgoing, blend, own[0], sibling[2] = kernel_call(
+    swapped = lax.ppermute(buffer, "expert", swap)
+    outgoing, blend, own[0] = kernel_call(
         pack_kernel,
         (
             jax.ShapeDtypeStruct((RING, slots, width), bf16),
             jax.ShapeDtypeStruct((2, RING * slots, RING * held), bf16),
             pltpu.VMEM(gate_weight.shape, bf16),
-            pltpu.VMEM(down_weight.shape, bf16),
-        ),
-        (masks, gathered, own[0], *sibling),
-        specs=[whole] + [far] * 5,
-        out_specs=(whole,) * 4,
-        scratch=[
-            pltpu.VMEM((RING, held, width), bf16),
-            pltpu.VMEM((RING, held, 128), bf16),
-            pltpu.SemaphoreType.DMA((4,)),
-        ],
+        ),
+        (masks, gathered, own[0]),
+        specs=[whole, whole, pl.BlockSpec(memory_space=pl.ANY)],
+        out_specs=(whole,) * 3,
+        scratch=[pltpu.SemaphoreType.DMA],
+        flops=200 * 10**9,
     )
     arrived = exchange(outgoing, deliver)
     answers = kernel_call(
         expert_kernel,
         jax.ShapeDtypeStruct((RING, slots, width), bf16),
-        (arrived, *[pltpu.with_memory_space_constraint(w, pltpu.VMEM) for w in own + sibling]),
+        (
+            arrived,
+            *[pltpu.with_memory_space_constraint(w, pltpu.VMEM) for w in own],
+            pltpu.with_memory_space_constraint(swapped, pltpu.HBM),
+        ),
+        specs=[whole] * 4 + [far],
+        scratch=[
+            pltpu.VMEM((width, lanes), bf16),
+            pltpu.VMEM((hidden_units, width), bf16),
+            pltpu.SemaphoreType.DMA((8,)),
+        ],
         flops=6 * RING * slots * width * hidden_units,
     )
     returned = exchange(answers, deliver)

time: 126 us -> 268 us (2.13)
  Pallas kernels: 7.85 us -> 158 us
  waiting for transfers between devices: 11.3 us -> 3.97 us
  starting transfers between devices: 20 us -> 15.6 us
  blocking collectives: 85.5 us -> 89.2 us
    pallas_call x6, Pallas kernels: 7.85 us -> 158 us  [kernel_call(): pl.pallas_call(body, out_shape=out_shape, in_specs=specs or [whole] * len...]
    all_to_all x1, waiting for transfers between devices: 7.31 us -> 0.01 us  [exchange(): lax.all_to_all(chunks, 'expert', split_axis=0, concat_axis=0, tiled=True,...]
    ppermute x3 -> x1, starting transfers between devices: 6.24 us -> 1.92 us  [on_device(): swapped = lax.ppermute(buffer, 'expert', swap)]
    all_to_all x3, blocking collectives: 85.5 us -> 89.2 us  [exchange(): lax.all_to_all(chunks, 'expert', split_axis=0, concat_axis=0, tiled=True,...]
  transfers between devices with their start and end apart: 5 -> 3, of which waited for: 2 -> 1; matrix products, arithmetic and copies ran while one was open for 0% -> 0% of each run, Pallas kernels for 0% -> 56%
where the time goes in v9:
time: 268 us
  Pallas kernels  158 us (59%)
  blocking collectives  89.2 us (33%)
  starting transfers between devices  15.6 us (6%)
  waiting for transfers between devices  3.97 us (1%)
    pallas_call x6, Pallas kernels, kernel_call(): pl.pallas_call(body, out_shape=out_shape, in_specs=specs or [whole] * len...  158 us
    all_to_all x3, blocking collectives, exchange(): lax.all_to_all(chunks, 'expert', split_axis=0, concat_axis=0, tiled=True,...  89.2 us
    all_to_all x1, starting transfers between devices, exchange(): lax.all_to_all(chunks, 'expert', split_axis=0, concat_axis=0, tiled=True,...  10.3 us
  transfers between devices with their start and end apart: 3, of which 1 were waited for; matrix products, arithmetic and copies ran while one was open for 0% of the time, Pallas kernels for 56%

profile of v9, /device:TPU:8, one launch (start us, length us, event | category | flops | bytes accessed | tf_op | source)
XLA Modules:
  0.0 267.8 jit_solution(12192184834938297087)
XLA Ops:
  0.0 1.9 shard_map.74
  1.9 10.3 %all-to-all-start = ((bf16[8,16,2176]{2,1,0:T(8,128)(2,1)}), bf16[8,16,2176]{2,1,0:T(8,128)(2,1)S(1)}, u32[]{:S(2)}, u32[]{:S(2)}) async-start(bf16[8,16,2176]{2,1,0:T(8,128)(2,1)} %shard_map.74), calls=%async_computation | async-start | bytes 1114112 | tf_op jit(solution)/shard_map/all_to_all | solution.py:22
  12.2 0.0 copy-start.3
  12.2 150.1 %shard_map.73 = (bf16[2,512,128]{2,1,0:T(8,128)(2,1)S(1)}, bf16[3200,768]{1,0:T(8,128)(2,1)}) custom-call(s32[1]{0:T(128)} %bitcast.1.place, bf16[1,1,2048,384]{3,2,1,0:T(8,128)(2,1)} %gate_ref.3, bf16[1,1,2048,384]{3,2,1,0:T(8,128)(2,1)} %up_ref.3, bf16[1,1,384,2048]{3,2,1,0:T(8,128)(2,1)} %down_ref.3), custom_call_target="tpu_custom_call" | custom-call | flops 20000000000 | tf_op jit(solution)/shard_map/pallas_call | solution.py:164
  162.3 1.9 collective-permute-start
  164.2 0.0 all-to-all-done.gathered
  164.2 0.0 copy-done.3
  164.2 1.1 shard_map.75
  165.3 0.0 copy-start
  165.4 0.0 copy-start.1
  165.4 36.3 %all_to_all.20.rows = bf16[8,64,2048]{2,1,0:T(8,128)(2,1)S(1)} all-to-all(bf16[8,64,2048]{2,1,0:T(8,128)(2,1)S(1)} %get-tuple-element.11), channel_id=1, replica_groups={{0,2,4,6,8,10,12,14},{16,18,20,22,24,26,28,30},{32,34,36,38,40,42,44,46..., dimensions={0} | all-to-all | bytes 4194304 | tf_op jit(solution)/shard_map/all_to_all | solution.py:22
  201.7 0.0 collective-permute-done.swapped
  201.7 0.0 copy-done
  201.7 0.0 copy-done.1
  201.7 4.4 %shard_map.76 = bf16[8,64,2048]{2,1,0:T(8,128)(2,1)S(1)} custom-call(bf16[8,64,2048]{2,1,0:T(8,128)(2,1)S(1)} %all_to_all.20.rows, bf16[1,1,2048,384]{3,2,1,0:T(8,128)(2,1)S(1)} %get-tuple-element.12.gate_ref, bf16[1,1,2048,384]{3,2,1,0:T(8,128)(2,1)S(1)} %copy-done, bf16[1,1,384,2048]{3,2,1,0:T(8,128)(2,1)S(1)} %copy-done.1, ...), custom_call_target="tpu_custom_call" | custom-call | flops 2415919104 | tf_op jit(solution)/shard_map/pallas_call | solution.py:164
  206.1 32.6 %all_to_all.21.returned = bf16[8,64,2048]{2,1,0:T(8,128)(2,1)S(1)} all-to-all(bf16[8,64,2048]{2,1,0:T(8,128)(2,1)S(1)} %shard_map.76), channel_id=1, replica_groups={{0,2,4,6,8,10,12,14},{16,18,20,22,24,26,28,30},{32,34,36,38,40,42,44,46..., dimensions={0} | all-to-all | bytes 4194304 | tf_op jit(solution)/shard_map/all_to_all | solution.py:22
  238.7 0.0 copy-start.2
  238.7 0.7 shard_map.77
  239.5 20.3 %all_to_all.22.pieces = bf16[8,16,2048]{2,1,0:T(8,128)(2,1)S(1)} all-to-all(bf16[8,16,2048]{2,1,0:T(8,128)(2,1)S(1)} %shard_map.77), channel_id=1, replica_groups={{0,16,32,48,64,80,96,112},{2,18,34,50,66,82,98,114},{4,20,36,52,68,84,1..., dimensions={0} | all-to-all | bytes 1048576 | tf_op jit(solution)/shard_map/all_to_all | solution.py:22
  259.7 0.0 copy-done.2
  259.8 0.1 shard_map.78
  259.8 3.4 %collective-permute-start.1 = (bf16[16,2048]{1,0:T(8,128)(2,1)S(1)}, bf16[16,2048]{1,0:T(8,128)(2,1)S(1)}, u32[]{:S(2)}, u32[]{:S(2)}) collective-permute-start(bf16[16,2048]{1,0:T(8,128)(2,1)S(1)} %shard_map.78), channel_id=1, source_target_pairs={{0,128},{128,256},{256,384},{384,0},{1,129},{129,257},{257,385},{3... | collective-permute-start | bytes 196616 | tf_op jit(solution)/shard_map/ppermute | solution.py:260
  263.2 4.0 %collective-permute-done.1 = bf16[16,2048]{1,0:T(8,128)(2,1)S(1)} collective-permute-done((bf16[16,2048]{1,0:T(8,128)(2,1)S(1)}, bf16[16,2048]{1,0:T(8,128)(2,1)S(1)}, u32[]{:S(2)}, u32[]{:S(2)}) %collective-permute-start.1) | collective-permute-done | bytes 65568 | tf_op jit(solution)/shard_map/ppermute | solution.py:260
  267.2 0.6 copy.15
Async XLA Ops:
  1.9 162.3 %all-to-all-start = ((bf16[8,16,2176]{2,1,0:T(8,128)(2,1)}), bf16[8,16,2176]{2,1,0:T(8,128)(2,1)S(1)}, u32[]{:S(2)}, u32[]{:S(2)}) async-start(bf16[8,16,2176]{2,1,0:T(8,128)(2,1)} %shard_map.74), calls=%async_computation | async-start | bytes 1114112 | tf_op jit(solution)/shard_map/all_to_all | solution.py:22
  12.2 152.0 %copy-start.3 = (bf16[1,1,2048,384]{3,2,1,0:T(8,128)(2,1)S(1)}, bf16[1,1,2048,384]{3,2,1,0:T(8,128)(2,1)}, u32[]{:S(2)}) copy-start(bf16[1,1,2048,384]{3,2,1,0:T(8,128)(2,1)} %gate_ref.3) | copy-start | bytes 4718596
  162.3 39.4 %collective-permute-start = (bf16[3200,768]{1,0:T(8,128)(2,1)}, bf16[3200,768]{1,0:T(8,128)(2,1)}, u32[]{:S(2)}, u32[]{:S(2)}) collective-permute-start(bf16[3200,768]{1,0:T(8,128)(2,1)} %get-tuple-element.13), channel_id=1, source_target_pairs={{0,1},{1,0},{2,3},{3,2},{4,5},{5,4},{6,7},{7,6},{8,9},{9,8},{10,11... | collective-permute-start | bytes 14745608 | tf_op jit(solution)/shard_map/ppermute | solution.py:219
  165.3 36.3 %copy-start = (bf16[1,1,2048,384]{3,2,1,0:T(8,128)(2,1)S(1)}, bf16[1,1,2048,384]{3,2,1,0:T(8,128)(2,1)}, u32[]{:S(2)}) copy-start(bf16[1,1,2048,384]{3,2,1,0:T(8,128)(2,1)} %up_ref.3) | copy-start | bytes 4718596
  165.4 36.3 %copy-start.1 = (bf16[1,1,384,2048]{3,2,1,0:T(8,128)(2,1)S(1)}, bf16[1,1,384,2048]{3,2,1,0:T(8,128)(2,1)}, u32[]{:S(2)}) copy-start(bf16[1,1,384,2048]{3,2,1,0:T(8,128)(2,1)} %down_ref.3) | copy-start | bytes 4718596
  238.7 21.0 %copy-start.2 = (bf16[1,2,8,2048]{3,2,1,0:T(8,128)(2,1)S(1)}, bf16[1,2,8,2048]{3,2,1,0:T(8,128)(2,1)}, u32[]{:S(2)}) copy-start(bf16[1,2,8,2048]{3,2,1,0:T(8,128)(2,1)} %param.7) | copy-start | bytes 196612
  259.8 7.4 %collective-permute-start.1 = (bf16[16,2048]{1,0:T(8,128)(2,1)S(1)}, bf16[16,2048]{1,0:T(8,128)(2,1)S(1)}, u32[]{:S(2)}, u32[]{:S(2)}) collective-permute-start(bf16[16,2048]{1,0:T(8,128)(2,1)S(1)} %shard_map.78), channel_id=1, source_target_pairs={{0,128},{128,256},{256,384},{384,0},{1,129},{129,257},{257,385},{3... | collective-permute-start | bytes 196616 | tf_op jit(solution)/shard_map/ppermute | solution.py:260

commit v10 on v9

--- a/solution.py
+++ b/solution.py
@@ -67,14 +67,14 @@
     return parts
 
 
-def mask_kernel(place, gate_ref, up_ref, down_ref, masks, buffer, sems):
-    parts = weight_parts(gate_ref.at[0, 0], up_ref.at[0, 0], down_ref.at[0, 0], buffer)
-    hidden_units = down_ref.shape[2]
+def mask_kernel(place, gate_ref, up_ref, down_ref, masks, buffer, held, in_sems, out_sems):
+    width, hidden_units = gate_ref.shape[2:]
+    parts = weight_parts(gate_ref.at[0, 0], up_ref.at[0, 0], down_ref.at[0, 0], held)
     used = parts[-1][1].shape[1]
-    tail = buffer.at[buffer.shape[0] - hidden_units :, used:]
+    tail = held.at[held.shape[0] - hidden_units :, used:]
     parts.append((down_ref.at[0, 0, :, : tail.shape[1]], tail))
-    copies = [pltpu.make_async_copy(a, b, sems.at[i]) for i, (a, b) in enumerate(parts)]
-    for copy in copies:
+    arrivals = [pltpu.make_async_copy(a, b, in_sems.at[i]) for i, (a, b) in enumerate(parts)]
+    for copy in arrivals:
         copy.start()
     mine = place[0]
     z, y, core = mine // 16, (mine // 2) % RING, mine % 2
@@ -86,7 +86,21 @@
     expert = chip * 2 + (other ^ core)
     masks[0] = (lane == expert).astype(jnp.bfloat16)
     masks[1] = (lane == expert + 64).astype(jnp.bfloat16)
-    for copy in copies:
+    departures = []
+    for i, (first, size, waits) in enumerate(
+        [(0, width, arrivals[:2])]
+        + [
+            (width + k * hidden_units, hidden_units, arrivals[2 + k : 3 + k])
+            for k in range(len(arrivals) - 4)
+        ]
+        + [(held.shape[0] - hidden_units, hidden_units, arrivals[-2:])]
+    ):
+        for copy in waits:
+            copy.wait()
+        span = pl.ds(first, size)
+        departures.append(pltpu.make_async_copy(held.at[span], buffer.at[span], out_sems.at[i]))
+        departures[i].start()
+    for copy in departures:
         copy.wait()
 
 
@@ -213,7 +227,11 @@
         (place, *[pltpu.with_memory_space_constraint(w, pltpu.HBM) for w in own]),
         specs=[pl.BlockSpec(memory_space=pltpu.SMEM)] + [far] * 3,
         out_specs=(whole, far),
-        scratch=[pltpu.SemaphoreType.DMA((8,))],
+        scratch=[
+            pltpu.VMEM((width + pl.cdiv(width, lanes) * hidden_units, lanes), bf16),
+            pltpu.SemaphoreType.DMA((8,)),
+            pltpu.SemaphoreType.DMA((8,)),
+        ],
         flops=20 * 10**9,
     )
     swapped = lax.ppermute(buffer, "expert", swap)

time: 268 us -> 125 us (0.47)
  Pallas kernels: 158 us -> 12.6 us
  waiting for transfers between devices: 3.97 us -> 11.3 us
  blocking collectives: 89.2 us -> 84.6 us
    pallas_call x6, Pallas kernels: 158 us -> 12.6 us  [kernel_call(): pl.pallas_call(body, out_shape=out_shape, in_specs=specs or [whole] * len...]
    all_to_all x1, waiting for transfers between devices: 0.01 us -> 7.37 us  [exchange(): lax.all_to_all(chunks, 'expert', split_axis=0, concat_axis=0, tiled=True,...]
    all_to_all x3, blocking collectives: 89.2 us -> 84.6 us  [exchange(): lax.all_to_all(chunks, 'expert', split_axis=0, concat_axis=0, tiled=True,...]
  transfers between devices with their start and end apart: 3 -> 3, of which waited for: 1 -> 2; matrix products, arithmetic and copies ran while one was open for 0% -> 0% of each run, Pallas kernels for 56% -> 4%
where the time goes in v10:
time: 125 us
  blocking collectives  84.6 us (68%)
  starting transfers between devices  15.6 us (12%)
  Pallas kernels  12.6 us (10%)
  waiting for transfers between devices  11.3 us (9%)
    all_to_all x3, blocking collectives, exchange(): lax.all_to_all(chunks, 'expert', split_axis=0, concat_axis=0, tiled=True,...  84.6 us
    pallas_call x6, Pallas kernels, kernel_call(): pl.pallas_call(body, out_shape=out_shape, in_specs=specs or [whole] * len...  12.6 us
    all_to_all x1, starting transfers between devices, exchange(): lax.all_to_all(chunks, 'expert', split_axis=0, concat_axis=0, tiled=True,...  10.3 us
    all_to_all x1, waiting for transfers between devices, exchange(): lax.all_to_all(chunks, 'expert', split_axis=0, concat_axis=0, tiled=True,...  7.37 us
    ppermute x1, waiting for transfers between devices, on_device(): return lax.ppermute(layer_out, 'segment', route).reshape(activations.shape)  3.96 us
    ppermute x1, starting transfers between devices, on_device(): return lax.ppermute(layer_out, 'segment', route).reshape(activations.shape)  3.4 us
  transfers between devices with their start and end apart: 3, of which 2 were waited for; matrix products, arithmetic and copies ran while one was open for 0% of the time, Pallas kernels for 4%

profile of v10, /device:TPU:8, one launch (start us, length us, event | category | flops | bytes accessed | tf_op | source)
XLA Modules:
  0.0 124.8 jit_solution(14105852834255855727)
XLA Ops:
  0.0 1.9 %shard_map.74 = bf16[8,16,2176]{2,1,0:T(8,128)(2,1)} custom-call(bf16[16,2048]{1,0:T(8,128)(2,1)} %bitcast.5, f32[1,2048]{1,0:T(1,128)} %refs_1_.1, s32[16,8]{1,0:T(8,128)} %bitcast.8, f32[16,8]{1,0:T(8,128)} %bitcast.9), custom_call_target="tpu_custom_call" | custom-call | tf_op jit(solution)/shard_map/pallas_call | solution.py:178
  1.9 10.3 %all-to-all-start = ((bf16[8,16,2176]{2,1,0:T(8,128)(2,1)}), bf16[8,16,2176]{2,1,0:T(8,128)(2,1)S(1)}, u32[]{:S(2)}, u32[]{:S(2)}) async-start(bf16[8,16,2176]{2,1,0:T(8,128)(2,1)} %shard_map.74), calls=%async_computation | async-start | bytes 1114112 | tf_op jit(solution)/shard_map/all_to_all | solution.py:22
  12.2 0.0 copy-start.3
  12.2 4.3 %shard_map.73 = (bf16[2,512,128]{2,1,0:T(8,128)(2,1)S(1)}, bf16[3200,768]{1,0:T(8,128)(2,1)}) custom-call(s32[1]{0:T(128)} %bitcast.1.place, bf16[1,1,2048,384]{3,2,1,0:T(8,128)(2,1)} %gate_ref.3, bf16[1,1,2048,384]{3,2,1,0:T(8,128)(2,1)} %up_ref.3, bf16[1,1,384,2048]{3,2,1,0:T(8,128)(2,1)} %down_ref.3), custom_call_target="tpu_custom_call" | custom-call | flops 20000000000 | tf_op jit(solution)/shard_map/pallas_call | solution.py:178
  16.5 1.9 %collective-permute-start = (bf16[3200,768]{1,0:T(8,128)(2,1)}, bf16[3200,768]{1,0:T(8,128)(2,1)}, u32[]{:S(2)}, u32[]{:S(2)}) collective-permute-start(bf16[3200,768]{1,0:T(8,128)(2,1)} %get-tuple-element.13), channel_id=1, source_target_pairs={{0,1},{1,0},{2,3},{3,2},{4,5},{5,4},{6,7},{7,6},{8,9},{9,8},{10,11... | collective-permute-start | bytes 14745608 | tf_op jit(solution)/shard_map/ppermute | solution.py:237
  18.5 7.4 %all-to-all-done.gathered = bf16[8,16,2176]{2,1,0:T(8,128)(2,1)S(1)} async-done(((bf16[8,16,2176]{2,1,0:T(8,128)(2,1)}), bf16[8,16,2176]{2,1,0:T(8,128)(2,1)S(1)}, u32[]{:S(2)}, u32[]{:S(2)}) %all-to-all-start) | async-done | bytes 557088 | tf_op jit(solution)/shard_map/all_to_all | solution.py:22
  25.8 0.0 copy-done.3
  25.9 1.1 shard_map.75
  27.0 0.0 copy-start
  27.0 0.0 copy-start.1
  27.0 36.3 %all_to_all.20.rows = bf16[8,64,2048]{2,1,0:T(8,128)(2,1)S(1)} all-to-all(bf16[8,64,2048]{2,1,0:T(8,128)(2,1)S(1)} %get-tuple-element.11), channel_id=1, replica_groups={{0,2,4,6,8,10,12,14},{16,18,20,22,24,26,28,30},{32,34,36,38,40,42,44,46..., dimensions={0} | all-to-all | bytes 4194304 | tf_op jit(solution)/shard_map/all_to_all | solution.py:22
  63.3 0.0 collective-permute-done.swapped
  63.3 0.0 copy-done
  63.3 0.0 copy-done.1
  63.3 4.4 %shard_map.76 = bf16[8,64,2048]{2,1,0:T(8,128)(2,1)S(1)} custom-call(bf16[8,64,2048]{2,1,0:T(8,128)(2,1)S(1)} %all_to_all.20.rows, bf16[1,1,2048,384]{3,2,1,0:T(8,128)(2,1)S(1)} %get-tuple-element.12.gate_ref, bf16[1,1,2048,384]{3,2,1,0:T(8,128)(2,1)S(1)} %copy-done, bf16[1,1,384,2048]{3,2,1,0:T(8,128)(2,1)S(1)} %copy-done.1, ...), custom_call_target="tpu_custom_call" | custom-call | flops 2415919104 | tf_op jit(solution)/shard_map/pallas_call | solution.py:178
  67.7 32.6 %all_to_all.21.returned = bf16[8,64,2048]{2,1,0:T(8,128)(2,1)S(1)} all-to-all(bf16[8,64,2048]{2,1,0:T(8,128)(2,1)S(1)} %shard_map.76), channel_id=1, replica_groups={{0,2,4,6,8,10,12,14},{16,18,20,22,24,26,28,30},{32,34,36,38,40,42,44,46..., dimensions={0} | all-to-all | bytes 4194304 | tf_op jit(solution)/shard_map/all_to_all | solution.py:22
  100.3 0.0 copy-start.2
  100.3 0.7 shard_map.77
  101.1 15.7 %all_to_all.22.pieces = bf16[8,16,2048]{2,1,0:T(8,128)(2,1)S(1)} all-to-all(bf16[8,16,2048]{2,1,0:T(8,128)(2,1)S(1)} %shard_map.77), channel_id=1, replica_groups={{0,16,32,48,64,80,96,112},{2,18,34,50,66,82,98,114},{4,20,36,52,68,84,1..., dimensions={0} | all-to-all | bytes 1048576 | tf_op jit(solution)/shard_map/all_to_all | solution.py:22
  116.8 0.0 copy-done.2
  116.8 0.1 shard_map.78
  116.8 3.4 %collective-permute-start.1 = (bf16[16,2048]{1,0:T(8,128)(2,1)S(1)}, bf16[16,2048]{1,0:T(8,128)(2,1)S(1)}, u32[]{:S(2)}, u32[]{:S(2)}) collective-permute-start(bf16[16,2048]{1,0:T(8,128)(2,1)S(1)} %shard_map.78), channel_id=1, source_target_pairs={{0,128},{128,256},{256,384},{384,0},{1,129},{129,257},{257,385},{3... | collective-permute-start | bytes 196616 | tf_op jit(solution)/shard_map/ppermute | solution.py:278
  120.3 4.0 %collective-permute-done.1 = bf16[16,2048]{1,0:T(8,128)(2,1)S(1)} collective-permute-done((bf16[16,2048]{1,0:T(8,128)(2,1)S(1)}, bf16[16,2048]{1,0:T(8,128)(2,1)S(1)}, u32[]{:S(2)}, u32[]{:S(2)}) %collective-permute-start.1) | collective-permute-done | bytes 65568 | tf_op jit(solution)/shard_map/ppermute | solution.py:278
  124.2 0.6 copy.15
Async XLA Ops:
  1.9 24.0 %all-to-all-start = ((bf16[8,16,2176]{2,1,0:T(8,128)(2,1)}), bf16[8,16,2176]{2,1,0:T(8,128)(2,1)S(1)}, u32[]{:S(2)}, u32[]{:S(2)}) async-start(bf16[8,16,2176]{2,1,0:T(8,128)(2,1)} %shard_map.74), calls=%async_computation | async-start | bytes 1114112 | tf_op jit(solution)/shard_map/all_to_all | solution.py:22
  12.2 13.6 %copy-start.3 = (bf16[1,1,2048,384]{3,2,1,0:T(8,128)(2,1)S(1)}, bf16[1,1,2048,384]{3,2,1,0:T(8,128)(2,1)}, u32[]{:S(2)}) copy-start(bf16[1,1,2048,384]{3,2,1,0:T(8,128)(2,1)} %gate_ref.3) | copy-start | bytes 4718596
  16.5 46.7 %collective-permute-start = (bf16[3200,768]{1,0:T(8,128)(2,1)}, bf16[3200,768]{1,0:T(8,128)(2,1)}, u32[]{:S(2)}, u32[]{:S(2)}) collective-permute-start(bf16[3200,768]{1,0:T(8,128)(2,1)} %get-tuple-element.13), channel_id=1, source_target_pairs={{0,1},{1,0},{2,3},{3,2},{4,5},{5,4},{6,7},{7,6},{8,9},{9,8},{10,11... | collective-permute-start | bytes 14745608 | tf_op jit(solution)/shard_map/ppermute | solution.py:237
  27.0 36.3 %copy-start = (bf16[1,1,2048,384]{3,2,1,0:T(8,128)(2,1)S(1)}, bf16[1,1,2048,384]{3,2,1,0:T(8,128)(2,1)}, u32[]{:S(2)}) copy-start(bf16[1,1,2048,384]{3,2,1,0:T(8,128)(2,1)} %up_ref.3) | copy-start | bytes 4718596
  27.0 36.3 %copy-start.1 = (bf16[1,1,384,2048]{3,2,1,0:T(8,128)(2,1)S(1)}, bf16[1,1,384,2048]{3,2,1,0:T(8,128)(2,1)}, u32[]{:S(2)}) copy-start(bf16[1,1,384,2048]{3,2,1,0:T(8,128)(2,1)} %down_ref.3) | copy-start | bytes 4718596
  100.3 16.4 %copy-start.2 = (bf16[1,2,8,2048]{3,2,1,0:T(8,128)(2,1)S(1)}, bf16[1,2,8,2048]{3,2,1,0:T(8,128)(2,1)}, u32[]{:S(2)}) copy-start(bf16[1,2,8,2048]{3,2,1,0:T(8,128)(2,1)} %param.7) | copy-start | bytes 196612
  116.8 7.4 %collective-permute-start.1 = (bf16[16,2048]{1,0:T(8,128)(2,1)S(1)}, bf16[16,2048]{1,0:T(8,128)(2,1)S(1)}, u32[]{:S(2)}, u32[]{:S(2)}) collective-permute-start(bf16[16,2048]{1,0:T(8,128)(2,1)S(1)} %shard_map.78), channel_id=1, source_target_pairs={{0,128},{128,256},{256,384},{384,0},{1,129},{129,257},{257,385},{3... | collective-permute-start | bytes 196616 | tf_op jit(solution)/shard_map/ppermute | solution.py:278

commit v11 on v10

--- a/solution.py
+++ b/solution.py
@@ -9,6 +9,7 @@
 RING = 8
 CAP = 2
 MIB = 1 << 20
+BLOCKS = 4
 
 
 def ring_groups(first_axis):
@@ -53,29 +54,44 @@
         copy.wait()
 
 
-def weight_parts(gate, up, down, buffer):
-    width, hidden_units = gate.shape
+def buffer_spans(width, hidden_units):
     lanes = 2 * hidden_units
-    parts = [
-        (gate, buffer.at[:width, :hidden_units]),
-        (up, buffer.at[:width, hidden_units:]),
-    ]
+    size = width // BLOCKS
+    upper = [pl.ds(k * size, size) for k in range(BLOCKS)]
+    lower = []
     for k in range(pl.cdiv(width, lanes)):
-        size = min(lanes, width - k * lanes)
-        rows = pl.ds(width + k * hidden_units, hidden_units)
-        parts.append((down.at[:, k * lanes : k * lanes + size], buffer.at[rows, :size]))
-    return parts
+        used = min(lanes, width - k * lanes)
+        lower.append((pl.ds(width + k * hidden_units, hidden_units), k * lanes, used))
+    return upper, lower
 
 
 def mask_kernel(place, gate_ref, up_ref, down_ref, masks, buffer, held, in_sems, out_sems):
     width, hidden_units = gate_ref.shape[2:]
-    parts = weight_parts(gate_ref.at[0, 0], up_ref.at[0, 0], down_ref.at[0, 0], held)
-    used = parts[-1][1].shape[1]
-    tail = held.at[held.shape[0] - hidden_units :, used:]
-    parts.append((down_ref.at[0, 0, :, : tail.shape[1]], tail))
-    arrivals = [pltpu.make_async_copy(a, b, in_sems.at[i]) for i, (a, b) in enumerate(parts)]
-    for copy in arrivals:
-        copy.start()
+    lanes = 2 * hidden_units
+    upper, lower = buffer_spans(width, hidden_units)
+    gate_ref, up_ref, down_ref = (r.at[0, 0] for r in (gate_ref, up_ref, down_ref))
+    moves = [
+        (
+            span,
+            [
+                (gate_ref.at[span], held.at[span, :hidden_units]),
+                (up_ref.at[span], held.at[span, hidden_units:]),
+            ],
+        )
+        for span in upper
+    ]
+    for span, first, used in lower:
+        pieces = [(down_ref.at[:, first : first + used], held.at[span, :used])]
+        if used < lanes:
+            pieces.append((down_ref.at[:, : lanes - used], held.at[span, used:]))
+        moves.append((span, pieces))
+    arrivals = [
+        [pltpu.make_async_copy(a, b, in_sems.at[i, j]) for j, (a, b) in enumerate(pieces)]
+        for i, (_, pieces) in enumerate(moves)
+    ]
+    for group in arrivals:
+        for copy in group:
+            copy.start()
     mine = place[0]
     z, y, core = mine // 16, (mine // 2) % RING, mine % 2
     shape = masks.shape[1:]
@@ -87,17 +103,9 @@
     masks[0] = (lane == expert).astype(jnp.bfloat16)
     masks[1] = (lane == expert + 64).astype(jnp.bfloat16)
     departures = []
-    for i, (first, size, waits) in enumerate(
-        [(0, width, arrivals[:2])]
-        + [
-            (width + k * hidden_units, hidden_units, arrivals[2 + k : 3 + k])
-            for k in range(len(arrivals) - 4)
-        ]
-        + [(held.shape[0] - hidden_units, hidden_units, arrivals[-2:])]
-    ):
-        for copy in waits:
+    for i, (span, _) in enumerate(moves):
+        for copy in arrivals[i]:
             copy.wait()
-        span = pl.ds(first, size)
         departures.append(pltpu.make_async_copy(held.at[span], buffer.at[span], out_sems.at[i]))
         departures[i].start()
     for copy in departures:
@@ -132,30 +140,38 @@
 
 
 def expert_kernel(rows, gate_ref, up_ref, down_ref, swapped, out, gate_up, down, sems):
-    hidden_units = down.shape[0]
-    parts = weight_parts(gate_up.at[:, :hidden_units], gate_up.at[:, hidden_units:], down, swapped)
-    copies = [pltpu.make_async_copy(b, a, sems.at[i]) for i, (a, b) in enumerate(parts)]
-    for copy in copies:
+    hidden_units, width = down.shape
+    upper, lower = buffer_spans(width, hidden_units)
+    arrivals = [(swapped.at[span], gate_up.at[span]) for span in upper]
+    arrivals += [
+        (swapped.at[span, :used], down.at[:, first : first + used]) for span, first, used in lower
+    ]
+    arrivals = [pltpu.make_async_copy(a, b, sems.at[i]) for i, (a, b) in enumerate(arrivals)]
+    for copy in arrivals:
         copy.start()
     half = rows.shape[1] // 2
 
-    def hidden_rows(e, weight):
-        x = rows[:, e * half : (e + 1) * half, :].reshape(-1, rows.shape[2])
-        gate, up = jnp.split(dot(x, weight), 2, axis=1)
+    def slot_rows(e, first, size):
+        return rows[:, e * half : (e + 1) * half, first : first + size].reshape(-1, size)
+
+    def activated(both):
+        gate, up = jnp.split(both, 2, axis=1)
         return (gate / (1.0 + jnp.exp(-gate)) * up).astype(jnp.bfloat16)
 
     def finish(e, hidden, weight):
         answer = dot(hidden, weight).astype(jnp.bfloat16)
         out[:, e * half : (e + 1) * half, :] = answer.reshape(out.shape[0], half, out.shape[2])
 
-    own = hidden_rows(0, jnp.concatenate([gate_ref[0, 0], up_ref[0, 0]], axis=1))
-    finish(0, own, down_ref[0, 0])
-    for copy in copies[:2]:
-        copy.wait()
-    sibling = hidden_rows(1, gate_up[...])
-    for copy in copies[2:]:
-        copy.wait()
-    finish(1, sibling, down[...])
+    own = jnp.concatenate([gate_ref[0, 0], up_ref[0, 0]], axis=1)
+    finish(0, activated(dot(slot_rows(0, 0, width), own)), down_ref[0, 0])
+    total = None
+    for copy, span in zip(arrivals, upper):
+        copy.wait()
+        term = dot(slot_rows(1, span.start, span.size), gate_up[span])
+        total = term if total is None else total + term
+    for copy in arrivals[len(upper) :]:
+        copy.wait()
+    finish(1, activated(total), down[...])
 
 
 def mix_kernel(returned, blend, out):
@@ -229,8 +245,8 @@
         out_specs=(whole, far),
         scratch=[
             pltpu.VMEM((width + pl.cdiv(width, lanes) * hidden_units, lanes), bf16),
-            pltpu.SemaphoreType.DMA((8,)),
-            pltpu.SemaphoreType.DMA((8,)),
+            pltpu.SemaphoreType.DMA((BLOCKS + 4, 2)),
+            pltpu.SemaphoreType.DMA((BLOCKS + 4,)),
         ],
         flops=20 * 10**9,
     )
@@ -261,7 +277,7 @@
         scratch=[
             pltpu.VMEM((width, lanes), bf16),
             pltpu.VMEM((hidden_units, width), bf16),
-            pltpu.SemaphoreType.DMA((8,)),
+            pltpu.SemaphoreType.DMA((BLOCKS + 4,)),
         ],
         flops=6 * RING * slots * width * hidden_units,
     )

time: 125 us -> 125 us (level)
  no operation moved by 1% of the time
where the time goes in v11:
time: 125 us
  blocking collectives  84.6 us (68%)
  starting transfers between devices  15.6 us (12%)
  Pallas kernels  12.8 us (10%)
  waiting for transfers between devices  11.3 us (9%)
    all_to_all x3, blocking collectives, exchange(): lax.all_to_all(chunks, 'expert', split_axis=0, concat_axis=0, tiled=True,...  84.6 us
    pallas_call x6, Pallas kernels, kernel_call(): pl.pallas_call(body, out_shape=out_shape, in_specs=specs or [whole] * len...  12.8 us
    all_to_all x1, starting transfers between devices, exchange(): lax.all_to_all(chunks, 'expert', split_axis=0, concat_axis=0, tiled=True,...  10.3 us
    all_to_all x1, waiting for transfers between devices, exchange(): lax.all_to_all(chunks, 'expert', split_axis=0, concat_axis=0, tiled=True,...  7.29 us
    ppermute x1, waiting for transfers between devices, on_device(): return lax.ppermute(layer_out, 'segment', route).reshape(activations.shape)  3.96 us
    ppermute x1, starting transfers between devices, on_device(): return lax.ppermute(layer_out, 'segment', route).reshape(activations.shape)  3.4 us
  transfers between devices with their start and end apart: 3, of which 2 were waited for; matrix products, arithmetic and copies ran while one was open for 0% of the time, Pallas kernels for 4%

profile of v11, /device:TPU:8, one launch (start us, length us, event | category | flops | bytes accessed | tf_op | source)
XLA Modules:
  0.0 125.0 jit_solution(16537655127450559609)
XLA Ops:
  0.0 1.9 %shard_map.74 = bf16[8,16,2176]{2,1,0:T(8,128)(2,1)} custom-call(bf16[16,2048]{1,0:T(8,128)(2,1)} %bitcast.5, f32[1,2048]{1,0:T(1,128)} %refs_1_.1, s32[16,8]{1,0:T(8,128)} %bitcast.8, f32[16,8]{1,0:T(8,128)} %bitcast.9), custom_call_target="tpu_custom_call" | custom-call | tf_op jit(solution)/shard_map/pallas_call | solution.py:194
  1.9 10.3 %all-to-all-start = ((bf16[8,16,2176]{2,1,0:T(8,128)(2,1)}), bf16[8,16,2176]{2,1,0:T(8,128)(2,1)S(1)}, u32[]{:S(2)}, u32[]{:S(2)}) async-start(bf16[8,16,2176]{2,1,0:T(8,128)(2,1)} %shard_map.74), calls=%async_computation | async-start | bytes 1114112 | tf_op jit(solution)/shard_map/all_to_all | solution.py:23
  12.2 0.0 copy-start.3
  12.2 4.4 %shard_map.73 = (bf16[2,512,128]{2,1,0:T(8,128)(2,1)S(1)}, bf16[3200,768]{1,0:T(8,128)(2,1)}) custom-call(s32[1]{0:T(128)} %bitcast.1.place, bf16[1,1,2048,384]{3,2,1,0:T(8,128)(2,1)} %gate_ref.3, bf16[1,1,2048,384]{3,2,1,0:T(8,128)(2,1)} %up_ref.3, bf16[1,1,384,2048]{3,2,1,0:T(8,128)(2,1)} %down_ref.3), custom_call_target="tpu_custom_call" | custom-call | flops 20000000000 | tf_op jit(solution)/shard_map/pallas_call | solution.py:194
  16.6 1.9 %collective-permute-start = (bf16[3200,768]{1,0:T(8,128)(2,1)}, bf16[3200,768]{1,0:T(8,128)(2,1)}, u32[]{:S(2)}, u32[]{:S(2)}) collective-permute-start(bf16[3200,768]{1,0:T(8,128)(2,1)} %get-tuple-element.13), channel_id=1, source_target_pairs={{0,1},{1,0},{2,3},{3,2},{4,5},{5,4},{6,7},{7,6},{8,9},{9,8},{10,11... | collective-permute-start | bytes 14745608 | tf_op jit(solution)/shard_map/ppermute | solution.py:253
  18.6 7.3 %all-to-all-done.gathered = bf16[8,16,2176]{2,1,0:T(8,128)(2,1)S(1)} async-done(((bf16[8,16,2176]{2,1,0:T(8,128)(2,1)}), bf16[8,16,2176]{2,1,0:T(8,128)(2,1)S(1)}, u32[]{:S(2)}, u32[]{:S(2)}) %all-to-all-start) | async-done | bytes 557088 | tf_op jit(solution)/shard_map/all_to_all | solution.py:23
  25.8 0.0 copy-done.3
  25.9 1.1 shard_map.75
  27.0 0.0 copy-start
  27.0 0.0 copy-start.1
  27.0 36.3 %all_to_all.20.rows = bf16[8,64,2048]{2,1,0:T(8,128)(2,1)S(1)} all-to-all(bf16[8,64,2048]{2,1,0:T(8,128)(2,1)S(1)} %get-tuple-element.11), channel_id=1, replica_groups={{0,2,4,6,8,10,12,14},{16,18,20,22,24,26,28,30},{32,34,36,38,40,42,44,46..., dimensions={0} | all-to-all | bytes 4194304 | tf_op jit(solution)/shard_map/all_to_all | solution.py:23
  63.3 0.0 collective-permute-done.swapped
  63.3 0.0 copy-done
  63.3 0.0 copy-done.1
  63.3 4.6 %shard_map.76 = bf16[8,64,2048]{2,1,0:T(8,128)(2,1)S(1)} custom-call(bf16[8,64,2048]{2,1,0:T(8,128)(2,1)S(1)} %all_to_all.20.rows, bf16[1,1,2048,384]{3,2,1,0:T(8,128)(2,1)S(1)} %get-tuple-element.12.gate_ref, bf16[1,1,2048,384]{3,2,1,0:T(8,128)(2,1)S(1)} %copy-done, bf16[1,1,384,2048]{3,2,1,0:T(8,128)(2,1)S(1)} %copy-done.1, ...), custom_call_target="tpu_custom_call" | custom-call | flops 2415919104 | tf_op jit(solution)/shard_map/pallas_call | solution.py:194
  67.9 32.6 %all_to_all.21.returned = bf16[8,64,2048]{2,1,0:T(8,128)(2,1)S(1)} all-to-all(bf16[8,64,2048]{2,1,0:T(8,128)(2,1)S(1)} %shard_map.76), channel_id=1, replica_groups={{0,2,4,6,8,10,12,14},{16,18,20,22,24,26,28,30},{32,34,36,38,40,42,44,46..., dimensions={0} | all-to-all | bytes 4194304 | tf_op jit(solution)/shard_map/all_to_all | solution.py:23
  100.5 0.0 copy-start.2
  100.5 0.7 shard_map.77
  101.2 15.7 %all_to_all.22.pieces = bf16[8,16,2048]{2,1,0:T(8,128)(2,1)S(1)} all-to-all(bf16[8,16,2048]{2,1,0:T(8,128)(2,1)S(1)} %shard_map.77), channel_id=1, replica_groups={{0,16,32,48,64,80,96,112},{2,18,34,50,66,82,98,114},{4,20,36,52,68,84,1..., dimensions={0} | all-to-all | bytes 1048576 | tf_op jit(solution)/shard_map/all_to_all | solution.py:23
  116.9 0.0 copy-done.2
  116.9 0.1 shard_map.78
  117.0 3.4 %collective-permute-start.1 = (bf16[16,2048]{1,0:T(8,128)(2,1)S(1)}, bf16[16,2048]{1,0:T(8,128)(2,1)S(1)}, u32[]{:S(2)}, u32[]{:S(2)}) collective-permute-start(bf16[16,2048]{1,0:T(8,128)(2,1)S(1)} %shard_map.78), channel_id=1, source_target_pairs={{0,128},{128,256},{256,384},{384,0},{1,129},{129,257},{257,385},{3... | collective-permute-start | bytes 196616 | tf_op jit(solution)/shard_map/ppermute | solution.py:294
  120.4 4.0 %collective-permute-done.1 = bf16[16,2048]{1,0:T(8,128)(2,1)S(1)} collective-permute-done((bf16[16,2048]{1,0:T(8,128)(2,1)S(1)}, bf16[16,2048]{1,0:T(8,128)(2,1)S(1)}, u32[]{:S(2)}, u32[]{:S(2)}) %collective-permute-start.1) | collective-permute-done | bytes 65568 | tf_op jit(solution)/shard_map/ppermute | solution.py:294
  124.4 0.6 copy.15
Async XLA Ops:
  1.9 24.0 %all-to-all-start = ((bf16[8,16,2176]{2,1,0:T(8,128)(2,1)}), bf16[8,16,2176]{2,1,0:T(8,128)(2,1)S(1)}, u32[]{:S(2)}, u32[]{:S(2)}) async-start(bf16[8,16,2176]{2,1,0:T(8,128)(2,1)} %shard_map.74), calls=%async_computation | async-start | bytes 1114112 | tf_op jit(solution)/shard_map/all_to_all | solution.py:23
  12.2 13.6 %copy-start.3 = (bf16[1,1,2048,384]{3,2,1,0:T(8,128)(2,1)S(1)}, bf16[1,1,2048,384]{3,2,1,0:T(8,128)(2,1)}, u32[]{:S(2)}) copy-start(bf16[1,1,2048,384]{3,2,1,0:T(8,128)(2,1)} %gate_ref.3) | copy-start | bytes 4718596
  16.6 46.7 %collective-permute-start = (bf16[3200,768]{1,0:T(8,128)(2,1)}, bf16[3200,768]{1,0:T(8,128)(2,1)}, u32[]{:S(2)}, u32[]{:S(2)}) collective-permute-start(bf16[3200,768]{1,0:T(8,128)(2,1)} %get-tuple-element.13), channel_id=1, source_target_pairs={{0,1},{1,0},{2,3},{3,2},{4,5},{5,4},{6,7},{7,6},{8,9},{9,8},{10,11... | collective-permute-start | bytes 14745608 | tf_op jit(solution)/shard_map/ppermute | solution.py:253
  27.0 36.3 %copy-start = (bf16[1,1,2048,384]{3,2,1,0:T(8,128)(2,1)S(1)}, bf16[1,1,2048,384]{3,2,1,0:T(8,128)(2,1)}, u32[]{:S(2)}) copy-start(bf16[1,1,2048,384]{3,2,1,0:T(8,128)(2,1)} %up_ref.3) | copy-start | bytes 4718596
  27.0 36.3 %copy-start.1 = (bf16[1,1,384,2048]{3,2,1,0:T(8,128)(2,1)S(1)}, bf16[1,1,384,2048]{3,2,1,0:T(8,128)(2,1)}, u32[]{:S(2)}) copy-start(bf16[1,1,384,2048]{3,2,1,0:T(8,128)(2,1)} %down_ref.3) | copy-start | bytes 4718596
  100.5 16.4 %copy-start.2 = (bf16[1,2,8,2048]{3,2,1,0:T(8,128)(2,1)S(1)}, bf16[1,2,8,2048]{3,2,1,0:T(8,128)(2,1)}, u32[]{:S(2)}) copy-start(bf16[1,2,8,2048]{3,2,1,0:T(8,128)(2,1)} %param.7) | copy-start | bytes 196612
  117.0 7.4 %collective-permute-start.1 = (bf16[16,2048]{1,0:T(8,128)(2,1)S(1)}, bf16[16,2048]{1,0:T(8,128)(2,1)S(1)}, u32[]{:S(2)}, u32[]{:S(2)}) collective-permute-start(bf16[16,2048]{1,0:T(8,128)(2,1)S(1)} %shard_map.78), channel_id=1, source_target_pairs={{0,128},{128,256},{256,384},{384,0},{1,129},{129,257},{257,385},{3... | collective-permute-start | bytes 196616 | tf_op jit(solution)/shard_map/ppermute | solution.py:294

commit v12 on v10

--- a/solution.py
+++ b/solution.py
@@ -82,7 +82,7 @@
     row = lax.broadcasted_iota(jnp.int32, shape, 0)
     lane = lax.broadcasted_iota(jnp.int32, shape, 1)
     member, other = row >> 6, (row >> 5) & 1
-    chip = jnp.where(core == 0, (z % 4) * RING + member, (member & 3) * RING + y)
+    chip = jnp.where(core == 0, (member & 3) * RING + y, (z % 4) * RING + member)
     expert = chip * 2 + (other ^ core)
     masks[0] = (lane == expert).astype(jnp.bfloat16)
     masks[1] = (lane == expert + 64).astype(jnp.bfloat16)
@@ -193,7 +193,7 @@
     hidden_units = gate_weight.shape[3]
     held = micro * block_tokens
     slots = RING * micro * 2 * CAP
-    spread, deliver = ring_groups("z"), ring_groups("y")
+    spread, deliver = ring_groups("y"), ring_groups("z")
     whole = pl.BlockSpec(memory_space=pltpu.VMEM)
     far = pl.BlockSpec(memory_space=pltpu.HBM)
     bf16 = jnp.bfloat16

time: 125 us -> 125 us (level)
  blocking collectives: 84.6 us -> 87.1 us
  waiting for transfers between devices: 11.3 us -> 9.31 us
    all_to_all x3, blocking collectives: 84.6 us -> 87.1 us  [exchange(): lax.all_to_all(chunks, 'expert', split_axis=0, concat_axis=0, tiled=True,...]
    all_to_all x1, waiting for transfers between devices: 7.37 us -> 5.34 us  [exchange(): lax.all_to_all(chunks, 'expert', split_axis=0, concat_axis=0, tiled=True,...]
where the time goes in v12:
time: 125 us
  blocking collectives  87.1 us (70%)
  starting transfers between devices  15.2 us (12%)
  Pallas kernels  12.6 us (10%)
  waiting for transfers between devices  9.31 us (7%)
    all_to_all x3, blocking collectives, exchange(): lax.all_to_all(chunks, 'expert', split_axis=0, concat_axis=0, tiled=True,...  87.1 us
    pallas_call x6, Pallas kernels, kernel_call(): pl.pallas_call(body, out_shape=out_shape, in_specs=specs or [whole] * len...  12.6 us
    all_to_all x1, starting transfers between devices, exchange(): lax.all_to_all(chunks, 'expert', split_axis=0, concat_axis=0, tiled=True,...  9.27 us
    all_to_all x1, waiting for transfers between devices, exchange(): lax.all_to_all(chunks, 'expert', split_axis=0, concat_axis=0, tiled=True,...  5.34 us
    ppermute x1, waiting for transfers between devices, on_device(): return lax.ppermute(layer_out, 'segment', route).reshape(activations.shape)  3.96 us
    ppermute x1, starting transfers between devices, on_device(): return lax.ppermute(layer_out, 'segment', route).reshape(activations.shape)  3.4 us
    ppermute x1, starting transfers between devices, on_device(): swapped = lax.ppermute(buffer, 'expert', swap)  2.52 us
  transfers between devices with their start and end apart: 3, of which 2 were waited for; matrix products, arithmetic and copies ran while one was open for 0% of the time, Pallas kernels for 4%

profile of v12, /device:TPU:8, one launch (start us, length us, event | category | flops | bytes accessed | tf_op | source)
XLA Modules:
  0.0 124.8 jit_solution(11294338061491655403)
XLA Ops:
  0.0 1.9 %shard_map.74 = bf16[8,16,2176]{2,1,0:T(8,128)(2,1)} custom-call(bf16[16,2048]{1,0:T(8,128)(2,1)} %bitcast.5, f32[1,2048]{1,0:T(1,128)} %refs_1_.1, s32[16,8]{1,0:T(8,128)} %bitcast.8, f32[16,8]{1,0:T(8,128)} %bitcast.9), custom_call_target="tpu_custom_call" | custom-call | tf_op jit(solution)/shard_map/pallas_call | solution.py:178
  1.9 9.3 %all-to-all-start = ((bf16[8,16,2176]{2,1,0:T(8,128)(2,1)}), bf16[8,16,2176]{2,1,0:T(8,128)(2,1)S(1)}, u32[]{:S(2)}, u32[]{:S(2)}) async-start(bf16[8,16,2176]{2,1,0:T(8,128)(2,1)} %shard_map.74), calls=%async_computation | async-start | bytes 1114112 | tf_op jit(solution)/shard_map/all_to_all | solution.py:22
  11.1 0.0 copy-start.3
  11.2 4.3 %shard_map.73 = (bf16[2,512,128]{2,1,0:T(8,128)(2,1)S(1)}, bf16[3200,768]{1,0:T(8,128)(2,1)}) custom-call(s32[1]{0:T(128)} %bitcast.1.place, bf16[1,1,2048,384]{3,2,1,0:T(8,128)(2,1)} %gate_ref.3, bf16[1,1,2048,384]{3,2,1,0:T(8,128)(2,1)} %up_ref.3, bf16[1,1,384,2048]{3,2,1,0:T(8,128)(2,1)} %down_ref.3), custom_call_target="tpu_custom_call" | custom-call | flops 20000000000 | tf_op jit(solution)/shard_map/pallas_call | solution.py:178
  15.5 2.5 %collective-permute-start = (bf16[3200,768]{1,0:T(8,128)(2,1)}, bf16[3200,768]{1,0:T(8,128)(2,1)}, u32[]{:S(2)}, u32[]{:S(2)}) collective-permute-start(bf16[3200,768]{1,0:T(8,128)(2,1)} %get-tuple-element.13), channel_id=1, source_target_pairs={{0,1},{1,0},{2,3},{3,2},{4,5},{5,4},{6,7},{7,6},{8,9},{9,8},{10,11... | collective-permute-start | bytes 14745608 | tf_op jit(solution)/shard_map/ppermute | solution.py:237
  18.0 5.3 %all-to-all-done.gathered = bf16[8,16,2176]{2,1,0:T(8,128)(2,1)S(1)} async-done(((bf16[8,16,2176]{2,1,0:T(8,128)(2,1)}), bf16[8,16,2176]{2,1,0:T(8,128)(2,1)S(1)}, u32[]{:S(2)}, u32[]{:S(2)}) %all-to-all-start) | async-done | bytes 557088 | tf_op jit(solution)/shard_map/all_to_all | solution.py:22
  23.4 0.0 copy-done.3
  23.4 1.1 shard_map.75
  24.5 0.0 copy-start
  24.5 0.0 copy-start.1
  24.5 38.8 %all_to_all.20.rows = bf16[8,64,2048]{2,1,0:T(8,128)(2,1)S(1)} all-to-all(bf16[8,64,2048]{2,1,0:T(8,128)(2,1)S(1)} %get-tuple-element.11), channel_id=1, replica_groups={{0,16,32,48,64,80,96,112},{2,18,34,50,66,82,98,114},{4,20,36,52,68,84,1..., dimensions={0} | all-to-all | bytes 4194304 | tf_op jit(solution)/shard_map/all_to_all | solution.py:22
  63.3 0.0 collective-permute-done.swapped
  63.3 0.0 copy-done
  63.3 0.0 copy-done.1
  63.3 4.4 %shard_map.76 = bf16[8,64,2048]{2,1,0:T(8,128)(2,1)S(1)} custom-call(bf16[8,64,2048]{2,1,0:T(8,128)(2,1)S(1)} %all_to_all.20.rows, bf16[1,1,2048,384]{3,2,1,0:T(8,128)(2,1)S(1)} %get-tuple-element.12.gate_ref, bf16[1,1,2048,384]{3,2,1,0:T(8,128)(2,1)S(1)} %copy-done, bf16[1,1,384,2048]{3,2,1,0:T(8,128)(2,1)S(1)} %copy-done.1, ...), custom_call_target="tpu_custom_call" | custom-call | flops 2415919104 | tf_op jit(solution)/shard_map/pallas_call | solution.py:178
  67.7 32.6 %all_to_all.21.returned = bf16[8,64,2048]{2,1,0:T(8,128)(2,1)S(1)} all-to-all(bf16[8,64,2048]{2,1,0:T(8,128)(2,1)S(1)} %shard_map.76), channel_id=1, replica_groups={{0,16,32,48,64,80,96,112},{2,18,34,50,66,82,98,114},{4,20,36,52,68,84,1..., dimensions={0} | all-to-all | bytes 4194304 | tf_op jit(solution)/shard_map/all_to_all | solution.py:22
  100.3 0.0 copy-start.2
  100.3 0.7 shard_map.77
  101.1 15.7 %all_to_all.22.pieces = bf16[8,16,2048]{2,1,0:T(8,128)(2,1)S(1)} all-to-all(bf16[8,16,2048]{2,1,0:T(8,128)(2,1)S(1)} %shard_map.77), channel_id=1, replica_groups={{0,2,4,6,8,10,12,14},{16,18,20,22,24,26,28,30},{32,34,36,38,40,42,44,46..., dimensions={0} | all-to-all | bytes 1048576 | tf_op jit(solution)/shard_map/all_to_all | solution.py:22
  116.8 0.0 copy-done.2
  116.8 0.1 shard_map.78
  116.8 3.4 %collective-permute-start.1 = (bf16[16,2048]{1,0:T(8,128)(2,1)S(1)}, bf16[16,2048]{1,0:T(8,128)(2,1)S(1)}, u32[]{:S(2)}, u32[]{:S(2)}) collective-permute-start(bf16[16,2048]{1,0:T(8,128)(2,1)S(1)} %shard_map.78), channel_id=1, source_target_pairs={{0,128},{128,256},{256,384},{384,0},{1,129},{129,257},{257,385},{3... | collective-permute-start | bytes 196616 | tf_op jit(solution)/shard_map/ppermute | solution.py:278
  120.3 4.0 %collective-permute-done.1 = bf16[16,2048]{1,0:T(8,128)(2,1)S(1)} collective-permute-done((bf16[16,2048]{1,0:T(8,128)(2,1)S(1)}, bf16[16,2048]{1,0:T(8,128)(2,1)S(1)}, u32[]{:S(2)}, u32[]{:S(2)}) %collective-permute-start.1) | collective-permute-done | bytes 65568 | tf_op jit(solution)/shard_map/ppermute | solution.py:278
  124.2 0.6 copy.15
Async XLA Ops:
  1.9 21.5 %all-to-all-start = ((bf16[8,16,2176]{2,1,0:T(8,128)(2,1)}), bf16[8,16,2176]{2,1,0:T(8,128)(2,1)S(1)}, u32[]{:S(2)}, u32[]{:S(2)}) async-start(bf16[8,16,2176]{2,1,0:T(8,128)(2,1)} %shard_map.74), calls=%async_computation | async-start | bytes 1114112 | tf_op jit(solution)/shard_map/all_to_all | solution.py:22
  11.1 12.2 %copy-start.3 = (bf16[1,1,2048,384]{3,2,1,0:T(8,128)(2,1)S(1)}, bf16[1,1,2048,384]{3,2,1,0:T(8,128)(2,1)}, u32[]{:S(2)}) copy-start(bf16[1,1,2048,384]{3,2,1,0:T(8,128)(2,1)} %gate_ref.3) | copy-start | bytes 4718596
  15.5 47.8 %collective-permute-start = (bf16[3200,768]{1,0:T(8,128)(2,1)}, bf16[3200,768]{1,0:T(8,128)(2,1)}, u32[]{:S(2)}, u32[]{:S(2)}) collective-permute-start(bf16[3200,768]{1,0:T(8,128)(2,1)} %get-tuple-element.13), channel_id=1, source_target_pairs={{0,1},{1,0},{2,3},{3,2},{4,5},{5,4},{6,7},{7,6},{8,9},{9,8},{10,11... | collective-permute-start | bytes 14745608 | tf_op jit(solution)/shard_map/ppermute | solution.py:237
  24.5 38.8 %copy-start = (bf16[1,1,2048,384]{3,2,1,0:T(8,128)(2,1)S(1)}, bf16[1,1,2048,384]{3,2,1,0:T(8,128)(2,1)}, u32[]{:S(2)}) copy-start(bf16[1,1,2048,384]{3,2,1,0:T(8,128)(2,1)} %up_ref.3) | copy-start | bytes 4718596
  24.5 38.8 %copy-start.1 = (bf16[1,1,384,2048]{3,2,1,0:T(8,128)(2,1)S(1)}, bf16[1,1,384,2048]{3,2,1,0:T(8,128)(2,1)}, u32[]{:S(2)}) copy-start(bf16[1,1,384,2048]{3,2,1,0:T(8,128)(2,1)} %down_ref.3) | copy-start | bytes 4718596
  100.3 16.5 %copy-start.2 = (bf16[1,2,8,2048]{3,2,1,0:T(8,128)(2,1)S(1)}, bf16[1,2,8,2048]{3,2,1,0:T(8,128)(2,1)}, u32[]{:S(2)}) copy-start(bf16[1,2,8,2048]{3,2,1,0:T(8,128)(2,1)} %param.7) | copy-start | bytes 196612
  116.8 7.4 %collective-permute-start.1 = (bf16[16,2048]{1,0:T(8,128)(2,1)S(1)}, bf16[16,2048]{1,0:T(8,128)(2,1)S(1)}, u32[]{:S(2)}, u32[]{:S(2)}) collective-permute-start(bf16[16,2048]{1,0:T(8,128)(2,1)S(1)} %shard_map.78), channel_id=1, source_target_pairs={{0,128},{128,256},{256,384},{384,0},{1,129},{129,257},{257,385},{3... | collective-permute-start | bytes 196616 | tf_op jit(solution)/shard_map/ppermute | solution.py:278
